TPU v7x, 32 devices: a whole 2x2x4 slice. The times are simulated.
32 devices in a mesh: fsdp: 8 (over y, x, core), tp: 4 (over z).
Axes of the slice: x: 2, y: 2, z: 4, core: 2. Of those that a mesh axis runs over, the one named last changes fastest.
Arguments:
- tokens: bfloat16 [16, 1024, 2048], P('fsdp', 'tp'), may hold values from -6 to 6
- lengths: int32 [16], P('fsdp'), may hold values from 256 to 1024, as said below
- routes: int32 [16, 1024, 6], P('fsdp'), may hold values from 0 to 7, as said below
- slot_ranks: int32 [16, 1024, 6], P('fsdp'), may hold values from 0 to 1024, as said below
- attn_gain: bfloat16 [2048], P('fsdp'), may hold values from 0.099609375 to 1.8984375
- query_weight: bfloat16 [2048, 3072], P('fsdp', 'tp'), may hold values from -0.125 to 0.125
- latent_key_weight: bfloat16 [2048, 576], P('fsdp'), may hold values from -0.125 to 0.125
- latent_gain: bfloat16 [512], P('fsdp'), may hold values from 0.099609375 to 1.8984375
- kvb_weight: bfloat16 [512, 4096], P('fsdp', 'tp'), may hold values from -0.25 to 0.25
- output_weight: bfloat16 [2048, 2048], P('tp', 'fsdp'), may hold values from -2 to 2
- ffn_gain: bfloat16 [2048], P('fsdp'), may hold values from 0.099609375 to 1.8984375
- router_matrix: bfloat16 [2048, 8], P('fsdp'), may hold values from -0.0625 to 0.0625
- shared_gate_weight: bfloat16 [2048, 2816], P('fsdp', 'tp'), may hold values from -0.125 to 0.125
- shared_up_weight: bfloat16 [2048, 2816], P('fsdp', 'tp'), may hold values from -0.125 to 0.125
- shared_down_weight: bfloat16 [2816, 2048], P('tp', 'fsdp'), may hold values from -0.109375 to 0.109375
- expert_gate: bfloat16 [8, 2048, 1408], P('fsdp', None, 'tp'), may hold values from -0.125 to 0.125
- expert_up: bfloat16 [8, 2048, 1408], P('fsdp', None, 'tp'), may hold values from -0.125 to 0.125
- expert_down: bfloat16 [8, 1408, 2048], P('fsdp', 'tp'), may hold values from -0.15625 to 0.15625
- cotangent: bfloat16 [16, 1024, 2048], P('fsdp', 'tp'), may hold values from -6 to 6
Outputs:
- output: bfloat16 [16, 1024, 2048], P('fsdp', 'tp')
- grad_tokens: bfloat16 [16, 1024, 2048], P('fsdp', 'tp')
- grad_attn_gain: float32 [2048], P('fsdp')
- grad_q_weight: float32 [2048, 3072], P('fsdp', 'tp')
- grad_kva_weight: float32 [2048, 576], P('fsdp')
- grad_latent_gain: float32 [512], P('fsdp')
- grad_kvb_weight: float32 [512, 4096], P('fsdp', 'tp')
- grad_out_weight: float32 [2048, 2048], P('tp', 'fsdp')
- grad_ffn_gain: float32 [2048], P('fsdp')
- grad_router_weight: float32 [2048, 8], P('fsdp')
- grad_shared_gate: float32 [2048, 2816], P('fsdp', 'tp')
- grad_shared_up: float32 [2048, 2816], P('fsdp', 'tp')
- grad_shared_down: float32 [2816, 2048], P('tp', 'fsdp')
- grad_expert_gate: float32 [8, 2048, 1408], P('fsdp', None, 'tp')
- grad_expert_up: float32 [8, 2048, 1408], P('fsdp', None, 'tp')
- grad_expert_down: float32 [8, 1408, 2048], P('fsdp', 'tp')
Inputs may be any that keep to these rules, and one draw needn't show every extreme that they name: `lengths`: of each 2 consecutive sequences one, which one varies, has length 1024; the others have 1024 // 4 or more. `routes`: the 6 experts of a token are different. For a token below its sequence's length, slot_ranks[s, t, k] is the rank of that route among the routes to the same expert from the same 2 consecutive sequences, taken in order of sequence, position and k and counting only tokens below their lengths, where that rank is below 1024; it is 1024 otherwise and for every token at or beyond its length. In every block of 2 sequences some expert gets more than 1024 such routes.
All inputs are finite; a program needn't handle non-finite values.
Results may differ from a plain program's by a relative error of at most 0.034.
Values may be sent and summed in bfloat16 or wider, within the bound.
A program may use at most 576 MiB of HBM per device.

v0:
```python
import jax
import jax.numpy as jnp
from jax import lax
from jax.sharding import PartitionSpec as P

HEAD_COUNT = 16
PLAIN_WIDTH = 128
ROTARY_WIDTH = 64
VALUE_WIDTH = 128
RANK = 512
TOPK = 6


epsilon = 1e-06
narrow = jnp.bfloat16
wide_precision = jnp.float32


def normalize(values, gain_row):
    return (
        values * lax.rsqrt(jnp.mean(values * values, axis=-1, keepdims=True) + epsilon) * gain_row
    )


def rotate(values, positions, direction):
    half_width = values.shape[-1] // 2
    frequency = 10000.0 ** (-jnp.arange(half_width, dtype=jnp.float32) / half_width)
    angles = positions.astype(jnp.float32)[..., None] * frequency
    cosines = jnp.cos(angles)
    sines = jnp.sin(angles) * direction
    first_half = values[..., :half_width]
    second_half = values[..., half_width:]
    return jnp.concatenate(
        [first_half * cosines - second_half * sines, first_half * sines + second_half * cosines],
        axis=-1,
    )


def silu_slope(values):
    sigmoid_part = jax.nn.sigmoid(values)
    return sigmoid_part * (1.0 + values * (1.0 - sigmoid_part))


def total_tp(first_grad, second_grad, third_grad, fourth_grad, fifth_grad):
    return (
        lax.psum(first_grad.astype(jnp.bfloat16), "tp").astype(jnp.float32),
        lax.psum(second_grad.astype(jnp.bfloat16), "tp").astype(jnp.float32),
        lax.psum(third_grad.astype(jnp.bfloat16), "tp").astype(jnp.float32),
        lax.psum(fourth_grad.astype(jnp.bfloat16), "tp").astype(jnp.float32),
        lax.psum(fifth_grad.astype(jnp.bfloat16), "tp").astype(jnp.float32),
    )


def total_fsdp(
    grad_one,
    grad_two,
    grad_three,
    grad_four,
    grad_five,
    grad_six,
    grad_seven,
    grad_eight,
    grad_nine,
    grad_ten,
    grad_eleven,
):
    return (
        lax.psum_scatter(
            grad_one.astype(jnp.bfloat16), "fsdp", scatter_dimension=0, tiled=True
        ).astype(jnp.float32),
        lax.psum_scatter(
            grad_two.astype(jnp.bfloat16), "fsdp", scatter_dimension=0, tiled=True
        ).astype(jnp.float32),
        lax.psum_scatter(
            grad_three.astype(jnp.bfloat16), "fsdp", scatter_dimension=0, tiled=True
        ).astype(jnp.float32),
        lax.psum_scatter(
            grad_four.astype(jnp.bfloat16), "fsdp", scatter_dimension=0, tiled=True
        ).astype(jnp.float32),
        lax.psum_scatter(
            grad_five.astype(jnp.bfloat16), "fsdp", scatter_dimension=0, tiled=True
        ).astype(jnp.float32),
        lax.psum_scatter(
            grad_six.astype(jnp.bfloat16), "fsdp", scatter_dimension=0, tiled=True
        ).astype(jnp.float32),
        lax.psum_scatter(
            grad_seven.astype(jnp.bfloat16), "fsdp", scatter_dimension=0, tiled=True
        ).astype(jnp.float32),
        lax.psum_scatter(
            grad_eight.astype(jnp.bfloat16), "fsdp", scatter_dimension=1, tiled=True
        ).astype(jnp.float32),
        lax.psum_scatter(
            grad_nine.astype(jnp.bfloat16), "fsdp", scatter_dimension=0, tiled=True
        ).astype(jnp.float32),
        lax.psum_scatter(
            grad_ten.astype(jnp.bfloat16), "fsdp", scatter_dimension=0, tiled=True
        ).astype(jnp.float32),
        lax.psum_scatter(
            grad_eleven.astype(jnp.bfloat16), "fsdp", scatter_dimension=1, tiled=True
        ).astype(jnp.float32),
    )


def on_device(
    tokens,
    lengths,
    routes,
    slot_ranks,
    attn_gain,
    query_weight,
    latent_key_weight,
    latent_gain,
    kvb_weight,
    output_weight,
    ffn_gain,
    router_matrix,
    shared_gate_weight,
    shared_up_weight,
    shared_down_weight,
    expert_gate,
    expert_up,
    expert_down,
    cotangent,
):
    tp_count = lax.axis_size("tp")
    tp_rank = lax.axis_index("tp")
    seq_count, local_len, width = tokens.shape
    seq_len = local_len * tp_count
    group_rows = seq_count * seq_len
    own_experts = expert_gate.shape[0]
    expert_count = own_experts * lax.axis_size("fsdp")
    capacity = 4 * group_rows // expert_count
    slot_total = expert_count * capacity
    ffe_local = expert_gate.shape[2]
    head_local = HEAD_COUNT // tp_count
    block_rows = min(512, seq_len)
    seq_blocks = seq_len // block_rows
    block_count = seq_count * seq_blocks
    score_scale = (PLAIN_WIDTH + ROTARY_WIDTH) ** (-0.5)
    own_first = tp_rank * local_len
    own_positions = own_first + jnp.arange(local_len, dtype=jnp.int32)
    all_positions = jnp.arange(seq_len, dtype=jnp.int32)
    (
        attn_gain_all,
        latent_key_whole,
        latent_gain_all,
        ffn_gain_all,
        router_complete,
        query_complete,
        kvb_whole,
        output_whole,
        shared_gate_whole,
        shared_up_whole,
        shared_down_whole,
    ) = (
        lax.all_gather(attn_gain, "fsdp", axis=0, tiled=True),
        lax.all_gather(latent_key_weight, "fsdp", axis=0, tiled=True),
        lax.all_gather(latent_gain, "fsdp", axis=0, tiled=True),
        lax.all_gather(ffn_gain, "fsdp", axis=0, tiled=True),
        lax.all_gather(router_matrix, "fsdp", axis=0, tiled=True),
        lax.all_gather(query_weight, "fsdp", axis=0, tiled=True),
        lax.all_gather(kvb_weight, "fsdp", axis=0, tiled=True),
        lax.all_gather(output_weight, "fsdp", axis=1, tiled=True),
        lax.all_gather(shared_gate_weight, "fsdp", axis=0, tiled=True),
        lax.all_gather(shared_up_weight, "fsdp", axis=0, tiled=True),
        lax.all_gather(shared_down_weight, "fsdp", axis=1, tiled=True),
    )
    attn_scale = attn_gain_all.astype(wide_precision)
    latent_scale = latent_gain_all.astype(wide_precision)
    ffn_scale = ffn_gain_all.astype(wide_precision)
    token_rows = tokens.astype(wide_precision)
    normed_local = normalize(token_rows, attn_scale).astype(narrow)
    latent_local = jnp.einsum(
        "wtk,kx->wtx", normed_local, latent_key_whole, preferred_element_type=wide_precision
    )
    compressed = latent_local[..., :RANK]
    key_raw = latent_local[..., RANK:]
    compressed_n = normalize(compressed, latent_scale).astype(narrow)
    key_rope_own = rotate(key_raw, own_positions, 1.0).astype(narrow)
    normed_complete, compressed_all, key_rope = (
        lax.all_gather(normed_local, "tp", axis=1, tiled=True),
        lax.all_gather(compressed_n, "tp", axis=1, tiled=True),
        lax.all_gather(key_rope_own, "tp", axis=1, tiled=True),
    )
    query_rows = jnp.einsum(
        "nvu,ue->nve", normed_complete, query_complete, preferred_element_type=wide_precision
    ).reshape(seq_count, seq_len, head_local, PLAIN_WIDTH + ROTARY_WIDTH)
    query_nope = query_rows[..., :PLAIN_WIDTH].astype(narrow)
    query_rope = rotate(query_rows[..., PLAIN_WIDTH:], all_positions[:, None], 1.0).astype(narrow)
    keyval = (
        jnp.einsum("slr,rh->slh", compressed_all, kvb_whole, preferred_element_type=wide_precision)
        .astype(narrow)
        .reshape(seq_count, seq_len, head_local, PLAIN_WIDTH + VALUE_WIDTH)
    )
    key_nope = keyval[..., :PLAIN_WIDTH]
    values = keyval[..., PLAIN_WIDTH:]

    def block_scores(block_index):
        sequence = block_index // seq_blocks
        first_row = block_index % seq_blocks * block_rows
        nope_rows = lax.dynamic_slice_in_dim(
            lax.dynamic_index_in_dim(query_nope, sequence, 0, False), first_row, block_rows, 0
        )
        rope_rows = lax.dynamic_slice_in_dim(
            lax.dynamic_index_in_dim(query_rope, sequence, 0, False), first_row, block_rows, 0
        )
        nope_keys = lax.dynamic_index_in_dim(key_nope, sequence, 0, False)
        rope_keys = lax.dynamic_index_in_dim(key_rope, sequence, 0, False)
        value_rows = lax.dynamic_index_in_dim(values, sequence, 0, False)
        length_now = lax.dynamic_index_in_dim(lengths, sequence, 0, False)
        scores = jnp.einsum(
            "qhd,khd->hqk", nope_rows, nope_keys, preferred_element_type=wide_precision
        )
        scores = (
            scores
            + jnp.einsum("qhd,kd->hqk", rope_rows, rope_keys, preferred_element_type=wide_precision)
        ) * score_scale
        row_index = first_row + jnp.arange(block_rows, dtype=jnp.int32)
        live_keys = (all_positions[None, :] <= row_index[:, None]) & (
            all_positions[None, :] < length_now
        )
        scores = jnp.where(live_keys[None], scores, -1e30)
        return (scores, nope_rows, rope_rows, nope_keys, rope_keys, value_rows, sequence, first_row)

    def attend_block(block_index):
        parts = block_scores(block_index)
        row_max = jnp.max(parts[0], axis=-1, keepdims=True)
        exponent = jnp.exp(parts[0] - row_max)
        row_sum = jnp.sum(exponent, axis=-1, keepdims=True)
        chances = (exponent / row_sum).astype(narrow)
        mixed_rows = jnp.einsum(
            "hqk,khd->qhd", chances, parts[5], preferred_element_type=wide_precision
        ).astype(narrow)
        return (mixed_rows, (row_max + jnp.log(row_sum))[..., 0])

    mixed_blocks, log_sums = lax.map(attend_block, jnp.arange(block_count, dtype=jnp.int32))
    mixed_head_values = mixed_blocks.reshape(seq_count, seq_len, head_local * VALUE_WIDTH)
    attention_pieces = jnp.einsum(
        "txc,ci->txi", mixed_head_values, output_whole, preferred_element_type=wide_precision
    )
    attn_own = lax.psum_scatter(
        attention_pieces.astype(jnp.bfloat16), "tp", scatter_dimension=1, tiled=True
    ).astype(jnp.float32)
    hidden = token_rows + attn_own
    hidden_normed = normalize(hidden, ffn_scale).astype(narrow)
    hidden_complete = lax.all_gather(hidden_normed, "tp", axis=1, tiled=True)
    router_logits = jnp.einsum(
        "ntb,bj->ntj", hidden_complete, router_complete, preferred_element_type=wide_precision
    )
    expert_ids = jnp.arange(expert_count, dtype=jnp.int32)
    one_hot = (routes[..., None] == expert_ids).astype(wide_precision)
    picked = jnp.sum(one_hot * router_logits[:, :, None, :], axis=-1)
    exponent = jnp.exp(picked - jnp.max(picked, axis=-1, keepdims=True))
    gate_values = exponent / jnp.sum(exponent, axis=-1, keepdims=True)
    flat_slot = jnp.where(
        slot_ranks < capacity, routes * capacity + slot_ranks, slot_total
    ).reshape(-1)
    token_of = jnp.arange(group_rows * TOPK, dtype=jnp.int32) // TOPK
    slot_token = (
        jnp.full((slot_total + 1,), group_rows, jnp.int32).at[flat_slot].set(token_of)[:slot_total]
    )
    slot_gate = (
        jnp.zeros((slot_total + 1,), wide_precision)
        .at[flat_slot]
        .set(gate_values.reshape(-1))[:slot_total]
    )
    hidden_rows = jnp.concatenate(
        [hidden_complete.reshape(group_rows, width), jnp.zeros((1, width), narrow)], axis=0
    )

    def slot_tables():
        return (slot_token, slot_gate)

    routed_rows = jnp.zeros((group_rows + 1, width), wide_precision)
    gate_w = lax.all_gather(expert_gate, "fsdp", axis=0, tiled=True)
    up_w = lax.all_gather(expert_up, "fsdp", axis=0, tiled=True)
    down_w = lax.all_gather(expert_down, "fsdp", axis=0, tiled=True)
    experts_here = gate_w.shape[0]
    token_piece, gate_piece = slot_tables()
    expert_block = hidden_rows[token_piece].reshape(experts_here, capacity, width)
    gate_part = jnp.einsum(
        "ecd,edf->ecf", expert_block, gate_w, preferred_element_type=wide_precision
    )
    up_part = jnp.einsum("ecd,edf->ecf", expert_block, up_w, preferred_element_type=wide_precision)
    activated = (jax.nn.silu(gate_part) * up_part).astype(narrow)
    expert_out = jnp.einsum(
        "ecf,efd->ecd", activated, down_w, preferred_element_type=wide_precision
    )
    routed_rows = routed_rows.at[token_piece].add(
        expert_out.reshape(experts_here * capacity, width) * gate_piece[:, None]
    )
    forward_saved_parts = jnp.concatenate([gate_part, up_part], axis=-1)
    routed_rows, saved_parts = (routed_rows, forward_saved_parts)
    shared_gate_value = jnp.einsum(
        "hxe,eg->hxg", hidden_complete, shared_gate_whole, preferred_element_type=wide_precision
    )
    shared_up_value = jnp.einsum(
        "hxe,eg->hxg", hidden_complete, shared_up_whole, preferred_element_type=wide_precision
    )
    shared_activation = (jax.nn.silu(shared_gate_value) * shared_up_value).astype(narrow)
    branch_terms = routed_rows[:group_rows].reshape(seq_count, seq_len, width) + jnp.einsum(
        "tkn,na->tka", shared_activation, shared_down_whole, preferred_element_type=wide_precision
    )
    branch_own = lax.psum_scatter(
        branch_terms.astype(jnp.bfloat16), "tp", scatter_dimension=1, tiled=True
    ).astype(jnp.float32)
    live_mask = (own_positions[None, :] < lengths[:, None]).astype(wide_precision)[..., None]
    output = (live_mask * (hidden + branch_own)).astype(narrow)
    grad_out = live_mask * cotangent.astype(wide_precision)
    branch_gradient = lax.all_gather(grad_out.astype(narrow), "tp", axis=1, tiled=True)
    shared_activation_gradient = jnp.einsum(
        "pgn,un->pgu", branch_gradient, shared_down_whole, preferred_element_type=wide_precision
    )
    shared_gate_value_gradient = (
        shared_activation_gradient * shared_up_value * silu_slope(shared_gate_value)
    ).astype(narrow)
    shared_up_value_gradient = (shared_activation_gradient * jax.nn.silu(shared_gate_value)).astype(
        narrow
    )
    shared_down_gradient = jnp.einsum(
        "tcw,tcm->wm", shared_activation, branch_gradient, preferred_element_type=wide_precision
    )
    shared_gate_weight_gradient = jnp.einsum(
        "kjo,kjb->ob",
        hidden_complete,
        shared_gate_value_gradient,
        preferred_element_type=wide_precision,
    )
    shared_up_weight_gradient = jnp.einsum(
        "kjo,kjb->ob",
        hidden_complete,
        shared_up_value_gradient,
        preferred_element_type=wide_precision,
    )
    grad_hidden_all = jnp.einsum(
        "xnj,wj->xnw",
        shared_gate_value_gradient,
        shared_gate_whole,
        preferred_element_type=wide_precision,
    ) + jnp.einsum(
        "xnj,wj->xnw",
        shared_up_value_gradient,
        shared_up_whole,
        preferred_element_type=wide_precision,
    )
    grad_rows = jnp.concatenate(
        [branch_gradient.reshape(group_rows, width), jnp.zeros((1, width), narrow)], axis=0
    )

    def slot_cotangent(token_piece, gate_piece, experts_here):
        incoming = (
            grad_rows[token_piece].astype(wide_precision).reshape(experts_here, capacity, width)
        )
        return (incoming, (incoming * gate_piece.reshape(experts_here, capacity, 1)).astype(narrow))

    grad_rows_acc = jnp.zeros((group_rows + 1, width), wide_precision)
    gate_w = lax.all_gather(expert_gate, "fsdp", axis=0, tiled=True)
    up_w = lax.all_gather(expert_up, "fsdp", axis=0, tiled=True)
    down_w = lax.all_gather(expert_down, "fsdp", axis=0, tiled=True)
    experts_here = gate_w.shape[0]
    token_piece, gate_piece = slot_tables()
    parts_now = saved_parts
    gate_part = parts_now[..., :ffe_local]
    up_part = parts_now[..., ffe_local:]
    activated = (jax.nn.silu(gate_part) * up_part).astype(narrow)
    expert_out = jnp.einsum(
        "ecf,efd->ecd", activated, down_w, preferred_element_type=wide_precision
    )
    incoming, grad_eout = slot_cotangent(token_piece, gate_piece, experts_here)
    grad_gate_piece = jnp.sum(incoming * expert_out, axis=-1).reshape(-1)
    grad_act = jnp.einsum("ecd,efd->ecf", grad_eout, down_w, preferred_element_type=wide_precision)
    grad_eg = (grad_act * up_part * silu_slope(gate_part)).astype(narrow)
    grad_eu = (grad_act * jax.nn.silu(gate_part)).astype(narrow)
    grad_block = jnp.einsum(
        "ecf,edf->ecd", grad_eg, gate_w, preferred_element_type=wide_precision
    ) + jnp.einsum("ecf,edf->ecd", grad_eu, up_w, preferred_element_type=wide_precision)
    grad_rows_acc = grad_rows_acc.at[token_piece].add(
        grad_block.reshape(experts_here * capacity, width)
    )
    grad_gate_slot = grad_gate_piece
    backward_grad_parts = jnp.concatenate([grad_eg, grad_eu], axis=-1)
    grad_rows_acc, grad_gate_slot, grad_parts = (grad_rows_acc, grad_gate_slot, backward_grad_parts)
    token_piece, gate_piece = slot_tables()
    expert_block = hidden_rows[token_piece].reshape(
        own_experts * lax.axis_size("fsdp"), capacity, width
    )
    parts_now = saved_parts
    activated = (jax.nn.silu(parts_now[..., :ffe_local]) * parts_now[..., ffe_local:]).astype(
        narrow
    )
    grad_eout = slot_cotangent(token_piece, gate_piece, own_experts * lax.axis_size("fsdp"))[1]
    grad_gate_w = jnp.einsum(
        "ecd,ecf->edf",
        expert_block,
        grad_parts[..., :ffe_local],
        preferred_element_type=wide_precision,
    )
    grad_up_w = jnp.einsum(
        "ecd,ecf->edf",
        expert_block,
        grad_parts[..., ffe_local:],
        preferred_element_type=wide_precision,
    )
    grad_down_w = jnp.einsum(
        "ecf,ecd->edf", activated, grad_eout, preferred_element_type=wide_precision
    )
    expert_gradients = lax.psum_scatter(
        jnp.stack([grad_gate_w, grad_up_w, grad_down_w], axis=1).astype(jnp.bfloat16),
        "fsdp",
        scatter_dimension=0,
        tiled=True,
    ).astype(jnp.float32)
    grad_egate_w = expert_gradients[:, 0]
    expert_up_weight_gradient = expert_gradients[:, 1]
    grad_edown_w = jnp.swapaxes(expert_gradients[:, 2], 1, 2)
    grad_gate_tok = jnp.concatenate([grad_gate_slot, jnp.zeros((1,), wide_precision)])[
        flat_slot
    ].reshape(seq_count, seq_len, TOPK)
    grad_hidden_all = grad_hidden_all + grad_rows_acc[:group_rows].reshape(
        seq_count, seq_len, width
    )
    grad_hidden_own, grad_gate_own = (
        lax.psum_scatter(
            grad_hidden_all.astype(jnp.bfloat16), "tp", scatter_dimension=1, tiled=True
        ).astype(jnp.float32),
        lax.psum_scatter(
            grad_gate_tok.astype(jnp.bfloat16), "tp", scatter_dimension=1, tiled=True
        ).astype(jnp.float32),
    )
    gates_own = lax.dynamic_slice_in_dim(gate_values, own_first, local_len, 1)
    hot_own = lax.dynamic_slice_in_dim(one_hot, own_first, local_len, 1)
    grad_picked = gates_own * (
        grad_gate_own - jnp.sum(gates_own * grad_gate_own, axis=-1, keepdims=True)
    )
    router_logit_gradient = jnp.sum(hot_own * grad_picked[..., None], axis=2).astype(narrow)
    router_gradient = jnp.einsum(
        "apc,apq->cq", hidden_normed, router_logit_gradient, preferred_element_type=wide_precision
    )
    grad_hidden_own = grad_hidden_own + jnp.einsum(
        "kow,pw->kop", router_logit_gradient, router_complete, preferred_element_type=wide_precision
    )
    hidden_back = jax.vjp(normalize, hidden, ffn_scale)[1]
    grad_hnorm, grad_ffn_gain = hidden_back(grad_hidden_own)
    grad_hidden = grad_out + grad_hnorm
    attention_gradient = lax.all_gather(grad_hidden.astype(narrow), "tp", axis=1, tiled=True)
    grad_mixed = (
        jnp.einsum(
            "yvp,ep->yve", attention_gradient, output_whole, preferred_element_type=wide_precision
        )
        .astype(narrow)
        .reshape(seq_count, seq_len, head_local, VALUE_WIDTH)
    )
    output_weight_gradient = jnp.einsum(
        "nwa,nwp->ap", mixed_head_values, attention_gradient, preferred_element_type=wide_precision
    )

    def attend_back(carried, block_index):
        grad_knope, grad_krope, grad_values = carried
        scores, nope_rows, rope_rows, nope_keys, rope_keys, value_rows, sequence, first_row = (
            block_scores(block_index)
        )
        chances = jnp.exp(scores - log_sums[block_index][..., None])
        grad_rows_now = lax.dynamic_slice_in_dim(
            lax.dynamic_index_in_dim(grad_mixed, sequence, 0, False), first_row, block_rows, 0
        )
        grad_chances = jnp.einsum(
            "qhd,khd->hqk", grad_rows_now, value_rows, preferred_element_type=wide_precision
        )
        grad_scores = (
            chances * (grad_chances - jnp.sum(chances * grad_chances, axis=-1, keepdims=True))
        ).astype(narrow)
        grad_qnope = (
            jnp.einsum(
                "hqk,khd->qhd", grad_scores, nope_keys, preferred_element_type=wide_precision
            )
            * score_scale
        )
        grad_qrope = (
            jnp.einsum("hqk,kd->qhd", grad_scores, rope_keys, preferred_element_type=wide_precision)
            * score_scale
        )
        grad_knope = grad_knope.at[sequence].add(
            jnp.einsum(
                "hqk,qhd->khd", grad_scores, nope_rows, preferred_element_type=wide_precision
            )
            * score_scale
        )
        grad_krope = grad_krope.at[sequence].add(
            jnp.einsum("hqk,qhd->kd", grad_scores, rope_rows, preferred_element_type=wide_precision)
            * score_scale
        )
        grad_values = grad_values.at[sequence].add(
            jnp.einsum(
                "hqk,qhd->khd",
                chances.astype(narrow),
                grad_rows_now,
                preferred_element_type=wide_precision,
            )
        )
        return ((grad_knope, grad_krope, grad_values), (grad_qnope, grad_qrope))

    key_grads, query_grads = lax.scan(
        attend_back,
        (
            jnp.zeros((seq_count, seq_len, head_local, PLAIN_WIDTH), wide_precision),
            jnp.zeros((seq_count, seq_len, ROTARY_WIDTH), wide_precision),
            jnp.zeros((seq_count, seq_len, head_local, VALUE_WIDTH), wide_precision),
        ),
        jnp.arange(block_count, dtype=jnp.int32),
    )
    grad_knope, grad_krope, grad_values = key_grads
    grad_qnope = query_grads[0].reshape(seq_count, seq_len, head_local, PLAIN_WIDTH)
    grad_qrope = rotate(
        query_grads[1].reshape(seq_count, seq_len, head_local, ROTARY_WIDTH),
        all_positions[:, None],
        -1.0,
    )
    query_gradient = (
        jnp.concatenate([grad_qnope, grad_qrope], axis=-1)
        .astype(narrow)
        .reshape(seq_count, seq_len, head_local * (PLAIN_WIDTH + ROTARY_WIDTH))
    )
    grad_keyval = (
        jnp.concatenate([grad_knope, grad_values], axis=-1)
        .astype(narrow)
        .reshape(seq_count, seq_len, head_local * (PLAIN_WIDTH + VALUE_WIDTH))
    )
    query_weight_gradient = jnp.einsum(
        "nvo,nvr->or", normed_complete, query_gradient, preferred_element_type=wide_precision
    )
    grad_kvb_w = jnp.einsum(
        "slr,slh->rh", compressed_all, grad_keyval, preferred_element_type=wide_precision
    )
    grad_normed_all = jnp.einsum(
        "bjq,vq->bjv", query_gradient, query_complete, preferred_element_type=wide_precision
    )
    grad_compressed_all = jnp.einsum(
        "slh,rh->slr", grad_keyval, kvb_whole, preferred_element_type=wide_precision
    )
    grad_normed_own, grad_comp_own, grad_krope_own = (
        lax.psum_scatter(
            grad_normed_all.astype(jnp.bfloat16), "tp", scatter_dimension=1, tiled=True
        ).astype(jnp.float32),
        lax.psum_scatter(
            grad_compressed_all.astype(jnp.bfloat16), "tp", scatter_dimension=1, tiled=True
        ).astype(jnp.float32),
        lax.psum_scatter(
            grad_krope.astype(jnp.bfloat16), "tp", scatter_dimension=1, tiled=True
        ).astype(jnp.float32),
    )
    latent_back = jax.vjp(normalize, compressed, latent_scale)[1]
    grad_compressed, grad_latent_gain = latent_back(grad_comp_own)
    latent_gradient = jnp.concatenate(
        [grad_compressed, rotate(grad_krope_own, own_positions, -1.0)], axis=-1
    ).astype(narrow)
    latent_key_gradient = jnp.einsum(
        "ztk,ztm->km", normed_local, latent_gradient, preferred_element_type=wide_precision
    )
    grad_normed_own = grad_normed_own + jnp.einsum(
        "enw,hw->enh", latent_gradient, latent_key_whole, preferred_element_type=wide_precision
    )
    token_back = jax.vjp(normalize, token_rows, attn_scale)[1]
    grad_tnorm, grad_attn_gain = token_back(grad_normed_own)
    grad_tokens = (grad_hidden + grad_tnorm).astype(narrow)
    summed_tp = total_tp(
        grad_attn_gain, latent_key_gradient, grad_latent_gain, grad_ffn_gain, router_gradient
    )
    reduced = total_fsdp(
        summed_tp[0],
        summed_tp[1],
        summed_tp[2],
        summed_tp[3],
        summed_tp[4],
        query_weight_gradient,
        grad_kvb_w,
        output_weight_gradient,
        shared_gate_weight_gradient,
        shared_up_weight_gradient,
        shared_down_gradient,
    )
    small_sums = reduced[:5]
    return (
        output,
        grad_tokens,
        small_sums[0],
        reduced[5],
        small_sums[1],
        small_sums[2],
        reduced[6],
        reduced[7],
        small_sums[3],
        small_sums[4],
        reduced[8],
        reduced[9],
        reduced[10],
        grad_egate_w,
        expert_up_weight_gradient,
        grad_edown_w,
    )


def solution(mesh):
    in_specs = (
        P("fsdp", "tp", None),
        P("fsdp"),
        P("fsdp", None, None),
        P("fsdp", None, None),
        P("fsdp"),
        P("fsdp", "tp"),
        P("fsdp", None),
        P("fsdp"),
        P("fsdp", "tp"),
        P("tp", "fsdp"),
        P("fsdp"),
        P("fsdp", None),
        P("fsdp", "tp"),
        P("fsdp", "tp"),
        P("tp", "fsdp"),
        P("fsdp", None, "tp"),
        P("fsdp", None, "tp"),
        P("fsdp", "tp", None),
        P("fsdp", "tp", None),
    )
    out_specs = (
        P("fsdp", "tp", None),
        P("fsdp", "tp", None),
        P("fsdp"),
        P("fsdp", "tp"),
        P("fsdp", None),
        P("fsdp"),
        P("fsdp", "tp"),
        P("tp", "fsdp"),
        P("fsdp"),
        P("fsdp", None),
        P("fsdp", "tp"),
        P("fsdp", "tp"),
        P("tp", "fsdp"),
        P("fsdp", None, "tp"),
        P("fsdp", None, "tp"),
        P("fsdp", "tp", None),
    )
    return jax.shard_map(
        on_device, mesh=mesh, in_specs=in_specs, out_specs=out_specs, check_vma=False
    )
```

profile of v0, /device:TPU:0, one launch (start us, length us, event | category | flops | bytes accessed | tf_op | source)
XLA Modules:
  0.0 3261.7 jit_solution(4523189477710105537)
XLA Ops:
  67.4 48.4 %all-gather.20.cloned.1.call-done = bf16[2,1024,512]{1,2,0:T(8,128)(2,1)} async-done(((bf16[2,256,512]{1,2,0:T(8,128)(2,1)}), bf16[2,1024,512]{1,2,0:T(8,128)(2,1)}) %all-gather.20.cloned.1.call-update) | async-done | bytes 2097168 | tf_op jit(solution)/shard_map/all_gather | solution.py:182
  149.2 151.1 %all-gather.24.cloned.1.call-done = bf16[2,1024,2048]{2,1,0:T(8,128)(2,1)} async-done(((bf16[2,256,2048]{2,1,0:T(8,128)(2,1)}), bf16[2,1024,2048]{2,1,0:T(8,128)(2,1)}) %all-gather.24.cloned.1.call-update) | async-done | bytes 8388624 | tf_op jit(solution)/shard_map/all_gather | solution.py:181
  321.7 67.2 %while.43 = (s32[]{:T(128)}, bf16[4,512,4,128]{3,2,1,0:T(4,128)(2,1)}, f32[4,4,512]{2,1,0:T(4,128)}, s32[4]{0:T(128)S(1)}, bf16[2,1024,4,128]{3,1,2,0:T(8,128)(2...) while((s32[]{:T(128)}, ...), condition=%wide.region_5.6_spmd.clone.clone, body=%wide.region_2.5_spmd.clone.clone.sunk | while | flops 1362361856 | bytes 57089560 | solution.py:236
  416.6 129.7 %reduce-scatter.19.cloned.1.call-done = bf16[2,256,2048]{2,1,0:T(8,128)(2,1)} async-done(((bf16[2,1024,2048]{2,1,0:T(8,128)(2,1)}), bf16[2,256,2048]{2,1,0:T(8,128)(2,1)}) %reduce-scatter.19.cloned.1.call-update) | async-done | bytes 2097168 | tf_op jit(solution)/shard_map/reduce_scatter | solution.py:241
  567.3 45.4 %scatter_custom_fusion = s32[8193]{0:T(1024)S(1)} fusion(s32[12288]{0:T(1024)S(1)} %bitcast.381, s32[12288]{0:T(1024)S(1)} %add_select_fusion.2, s32[]{:T(128)} %constant.549.clone.1), kind=kCustom, calls=%fused_computation.250 | custom fusion | bytes 32776 | tf_op jit(solution)/shard_map/scatter | solution.py:260
  613.3 85.6 %all-gather.44.cloned.1.call-done = bf16[2,1024,2048]{2,1,0:T(8,128)(2,1)} async-done(((bf16[2,256,2048]{2,1,0:T(8,128)(2,1)}), bf16[2,1024,2048]{2,1,0:T(8,128)(2,1)}) %all-gather.44.cloned.1.call-update) | async-done | bytes 8388624 | tf_op jit(solution)/shard_map/all_gather | solution.py:310
  707.9 66.9 %gather_fusion.1 = bf16[8192,2048]{1,0:T(8,128)(2,1)} fusion(bf16[2049,2048]{1,0:T(8,128)(2,1)} %concatenate.50, s32[8192]{0:T(1024)S(1)} %get-tuple-element.831), kind=kCustom, calls=%fused_computation.1 | custom fusion | bytes 67141632 | tf_op jit(solution)/shard_map/gather | solution.py:352
  774.9 73.5 %all-gather.30.cloned.1.call-done = bf16[2,1024,2048]{2,1,0:T(8,128)(2,1)} async-done(((bf16[2,256,2048]{2,1,0:T(8,128)(2,1)}), bf16[2,1024,2048]{2,1,0:T(8,128)(2,1)}) %all-gather.30.cloned.1.call-update) | async-done | bytes 8388624 | tf_op jit(solution)/shard_map/all_gather | solution.py:246
  855.8 45.4 %scatter_custom_fusion.1 = f32[8193]{0:T(1024)S(1)} fusion(s32[12288]{0:T(1024)S(1)} %bitcast.382, f32[12288]{0:T(1024)S(1)} %reshape.772, f32[]{:T(128)} %constant.543.clone.1), kind=kCustom, calls=%fused_computation.248 | custom fusion | bytes 32776 | tf_op jit(solution)/shard_map/scatter | solution.py:265
  909.7 66.1 %gather_fusion = bf16[8192,2048]{1,0:T(8,128)(2,1)} fusion(bf16[2049,2048]{1,0:T(8,128)(2,1)} %concatenate.49, s32[8192]{0:T(1024)S(1)} %get-tuple-element.831), kind=kCustom, calls=%fused_computation | custom fusion | bytes 67141632 | tf_op jit(solution)/shard_map/gather | solution.py:280
  1021.9 33.1 %all-gather.36.cloned.1.call-done = bf16[8,352,2048]{2,1,0:T(8,128)(2,1)} async-done(((bf16[1,352,2048]{2,1,0:T(8,128)(2,1)}), bf16[8,352,2048]{2,1,0:T(8,128)(2,1)}) %all-gather.36.cloned.1.call-update) | async-done | bytes 11534352 | tf_op jit(solution)/shard_map/all_gather | solution.py:277
  1055.1 38.5 %multiply_convert_fusion.1 = (bf16[8,1024,352]{1,2,0:T(8,128)(2,1)}, bf16[8,1024,352]{1,2,0:T(8,128)(2,1)}, bf16[8,1024,352]{1,2,0:T(8,128)(2,1)}) fusion(f32[8,1024,352]{1,2,0:T(8,128)} %fusion.166, f32[8,1024,352]{1,2,0:T(8,128)} %fusion.167, bf16[8,352,2048]{2,1,0:T(8,128)(2,1)} %all-gather.36.cloned.1.call-done, bf16[8,1024,2048]{2,1,0:T(8,128)(2,1)} %bitcast.358, ...), kind=kOutput, calls=%fused_computation.116 | convolution fusion | flops 11904745472 | bytes 85491712 | tf_op jit(solution)/shard_map/ecd,efd->ecf/dot_general | solution.py:371
  1093.6 31.9 fusion.168
  1125.5 51.6 %convolution_add_fusion = f32[8,1024,2048]{2,1,0:T(8,128)} fusion(f32[8,1024,2048]{2,1,0:T(8,128)} %fusion.168, bf16[8,1024,352]{1,2,0:T(8,128)(2,1)} %get-tuple-element.808, bf16[8,2048,352]{1,2,0:T(8,128)(2,1)} %all-gather.34.cloned.1.call-done), kind=kOutput, calls=%fused_computation.110 | convolution fusion | flops 11827937280 | bytes 151519232 | tf_op jit(solution)/shard_map/ecf,edf->ecd/dot_general | solution.py:376
  1177.1 109.1 %scatter_custom_fusion.3 = f32[2049,2048]{1,0:T(8,128)} fusion(s32[8192]{0:T(1024)} %get-tuple-element.832, f32[8192,2048]{1,0:T(8,128)} %bitcast.20, f32[]{:T(128)} %constant.543.clone.1), kind=kCustom, calls=%fused_computation.121 | custom fusion | flops 16777216 | bytes 16785920 | tf_op jit(solution)/shard_map/scatter-add | solution.py:377
  1298.0 40.8 %fusion.77 = (bf16[8,1024]{1,0:T(8,128)(2,1)S(1)}, f32[8,1024,2048]{2,1,0:T(8,128)}) fusion(bf16[8,1024,2048]{2,1,0:T(8,128)(2,1)} %bitcast.359, bf16[8,1024,352]{1,2,0:T(8,128)(2,1)S(1)} %bitcast.371, bf16[8,352,2048]{2,1,0:T(8,128)(2,1)} %all-gather.36.cloned.1.call-done), kind=kOutput, calls=%fused_computation.105 | convolution fusion | flops 11861483520 | bytes 117981184 | tf_op jit(solution)/shard_map/ecf,efd->ecd/dot_general | solution.py:286
  1338.9 75.8 %gather_fusion.2 = bf16[12288]{0:T(1024)(128)(2,1)S(1)} fusion(bf16[8193]{0:T(1024)(128)(2,1)S(1)} %pad_maximum_fusion.8, s32[12288]{0:T(1024)S(1)} %copy-done.40), kind=kCustom, calls=%fused_computation.2 | custom fusion | bytes 98304 | tf_op jit(solution)/shard_map/gather | solution.py:416
  1483.6 143.6 %reduce-scatter.23.cloned.1.call-done = bf16[2,256,2048]{2,1,0:T(8,128)(2,1)} async-done(((bf16[2,1024,2048]{2,1,0:T(8,128)(2,1)}), bf16[2,256,2048]{2,1,0:T(8,128)(2,1)}) %reduce-scatter.23.cloned.1.call-update) | async-done | bytes 2097168 | tf_op jit(solution)/shard_map/reduce_scatter | solution.py:423
  1637.1 150.4 %all-gather.46.cloned.1.call-done = bf16[2,1024,2048]{2,1,0:T(8,128)(2,1)} async-done(((bf16[2,256,2048]{2,1,0:T(8,128)(2,1)}), bf16[2,1024,2048]{2,1,0:T(8,128)(2,1)}) %all-gather.46.cloned.1.call-update) | async-done | bytes 8388624 | tf_op jit(solution)/shard_map/all_gather | solution.py:445
  1803.4 262.8 %while.44 = (s32[]{:T(128)}, f32[2,1024,4,128]{1,3,2,0:T(8,128)}, f32[2,1024,64]{1,2,0:T(8,128)}, f32[2,1024,4,128]{1,3,2,0:T(8,128)}, bf16[4,512,4,128]{3,1,0,2...) while((s32[]{:T(128)}, f32[2,1024,4,128]{1,3,2,0:T(8,128)}, ...), condition=%wide.region_26.27_spmd.clone.clone, body=%wide.region_22.26_spmd.clone.clone.sunk | while | flops 3515153920 | bytes 197447536 | solution.py:502
  2092.3 43.4 %reduce-scatter.29.cloned.1.call-done = bf16[2,256,512]{1,2,0:T(8,128)(2,1)} async-done(((bf16[2,1024,512]{1,2,0:T(8,128)(2,1)}), bf16[2,256,512]{1,2,0:T(8,128)(2,1)}) %reduce-scatter.29.cloned.1.call-update) | async-done | bytes 524304 | tf_op jit(solution)/shard_map/reduce_scatter | solution.py:544
  2175.4 27.0 convert_bitcast_fusion.1
  2225.0 27.0 convert_bitcast_fusion.2
  2332.0 46.3 %bitcast_multiply_fusion = f32[8192,2048]{1,0:T(8,128)} fusion(f32[8,1024,2048]{2,1,0:T(8,128)} %get-tuple-element.844, f32[8192]{0:T(1024)S(1)} %copy-done.36), kind=kLoop, calls=%fused_computation.106 | loop fusion | flops 16777216 | bytes 134250496 | tf_op jit(solution)/shard_map/mul | solution.py:290
  2378.3 108.8 %scatter_custom_fusion.2 = f32[2049,2048]{1,0:T(8,128)} fusion(s32[8192]{0:T(1024)} %get-tuple-element.832, f32[8192,2048]{1,0:T(8,128)} %bitcast_multiply_fusion, f32[]{:T(128)} %constant.543.clone.1), kind=kCustom, calls=%fused_computation.123 | custom fusion | flops 16777216 | bytes 16785920 | tf_op jit(solution)/shard_map/scatter-add | solution.py:289
  2524.0 221.1 %all-reduce.14.cloned.1.call-done = bf16[8,3,2048,352]{2,3,0,1:T(8,128)(2,1)} async-done(((bf16[8,3,2048,352]{2,3,0,1:T(8,128)(2,1)}), bf16[8,3,2048,352]{2,3,0,1:T(8,128)(2,1)}) %all-reduce.14.cloned.1.call-update) | async-done | bytes 34603024
  2752.8 31.7 reduce-scatter.35.cloned.1.call-done
  2786.1 43.1 %reduce-scatter.37.cloned.1.call-done = bf16[512,256]{1,0:T(8,128)(2,1)} async-done(((bf16[512,2048]{1,0:T(8,128)(2,1)}), bf16[512,256]{1,0:T(8,128)(2,1)}) %reduce-scatter.37.cloned.1.call-update) | async-done | bytes 262160 | tf_op jit(solution)/shard_map/reduce_scatter | solution.py:89
  2831.0 47.9 %reduce-scatter.33.cloned.1.call-done = bf16[256,768]{1,0:T(8,128)(2,1)} async-done(((bf16[2048,768]{1,0:T(8,128)(2,1)}), bf16[256,768]{1,0:T(8,128)(2,1)}) %reduce-scatter.33.cloned.1.call-update) | async-done | bytes 393232 | tf_op jit(solution)/shard_map/reduce_scatter | solution.py:83
  2880.8 36.4 %all-reduce.12.cloned.1.call-done = bf16[256,576]{0,1:T(8,128)(2,1)} async-done(((bf16[256,576]{0,1:T(8,128)(2,1)}), bf16[256,576]{0,1:T(8,128)(2,1)}) %all-reduce.12.cloned.1.call-update) | async-done | bytes 294928 | tf_op jit(solution)/shard_map/psum | solution.py:47
  2919.0 144.7 %reduce-scatter.27.cloned.1.call-done = bf16[2,256,2048]{2,1,0:T(8,128)(2,1)} async-done(((bf16[2,1024,2048]{2,1,0:T(8,128)(2,1)}), bf16[2,256,2048]{2,1,0:T(8,128)(2,1)}) %reduce-scatter.27.cloned.1.call-update) | async-done | bytes 2097168 | tf_op jit(solution)/shard_map/reduce_scatter | solution.py:541
  3114.0 132.5 %reduce-scatter.21.cloned.1.call-done = bf16[2,256,2048]{2,1,0:T(8,128)(2,1)} async-done(((bf16[2,1024,2048]{2,1,0:T(8,128)(2,1)}), bf16[2,256,2048]{2,1,0:T(8,128)(2,1)}) %reduce-scatter.21.cloned.1.call-update) | async-done | bytes 2097168 | tf_op jit(solution)/shard_map/reduce_scatter | solution.py:304
  (599 shorter events, 919.9 us)
Async XLA Ops:
  7.2 34.9 %all-gather.18.cloned.1.call-start = ((), (), s32[]{:S(2)}) async-start(), calls=%async_computation.15 | async-start | bytes 2654208 | tf_op jit(solution)/shard_map/all_gather | solution.py:157
  7.9 59.5 %all-gather.22.cloned.1.call-start = ((), (), s32[]{:S(2)}) async-start(), calls=%async_computation.17 | async-start | bytes 1179648 | tf_op jit(solution)/shard_map/all_gather | solution.py:162
  8.7 107.2 %all-gather.20.cloned.1.call-start = ((), (), s32[]{:S(2)}) async-start(), calls=%async_computation.16 | async-start | bytes 2621440 | tf_op jit(solution)/shard_map/all_gather | solution.py:182
  47.5 101.7 %all-gather.26.cloned.1.call-start = ((), (), s32[]{:S(2)}) async-start(), calls=%async_computation.19 | async-start | bytes 3538944 | tf_op jit(solution)/shard_map/all_gather | solution.py:161
  49.5 250.8 %all-gather.24.cloned.1.call-start = ((), (), s32[]{:S(2)}) async-start(), calls=%async_computation.18 | async-start | bytes 10485760 | tf_op jit(solution)/shard_map/all_gather | solution.py:181
  50.1 343.5 %all-gather.28.cloned.1.call-start = ((), (), s32[]{:S(2)}) async-start(), calls=%async_computation.20 | async-start | bytes 2359296 | tf_op jit(solution)/shard_map/all_gather | solution.py:163
  50.7 495.7 %reduce-scatter.19.cloned.1.call-start = ((), (), s32[]{:S(2)}) async-start(), calls=%async_computation.21 | async-start | bytes 10485760 | tf_op jit(solution)/shard_map/reduce_scatter | solution.py:241
  403.6 295.3 %all-gather.44.cloned.1.call-start = ((), (), s32[]{:S(2)}) async-start(), calls=%async_computation.30 | async-start | bytes 10485760 | tf_op jit(solution)/shard_map/all_gather | solution.py:310
  407.7 440.6 %all-gather.30.cloned.1.call-start = ((), (), s32[]{:S(2)}) async-start(), calls=%async_computation.22 | async-start | bytes 10485760 | tf_op jit(solution)/shard_map/all_gather | solution.py:246
  552.4 423.4 %all-gather.32.cloned.1.call-start = ((), (), s32[]{:S(2)}) async-start(), calls=%async_computation.23 | async-start | bytes 12976128 | tf_op jit(solution)/shard_map/all_gather | solution.py:275
  553.0 445.9 %all-gather.34.cloned.1.call-start = ((), (), s32[]{:S(2)}) async-start(), calls=%async_computation.24 | async-start | bytes 12976128 | tf_op jit(solution)/shard_map/all_gather | solution.py:276
  553.7 501.4 %all-gather.36.cloned.1.call-start = ((), (), s32[]{:S(2)}) async-start(), calls=%async_computation.25 | async-start | bytes 12976128 | tf_op jit(solution)/shard_map/all_gather | solution.py:277
  554.3 862.4 %all-gather.40.cloned.1.call-start = ((), (), s32[]{:S(2)}) async-start(), calls=%async_computation.27 | async-start | bytes 3244032 | tf_op jit(solution)/shard_map/all_gather | solution.py:165
  555.0 873.0 %all-gather.38.cloned.1.call-start = ((), (), s32[]{:S(2)}) async-start(), calls=%async_computation.26 | async-start | bytes 3244032 | tf_op jit(solution)/shard_map/all_gather | solution.py:164
  555.6 883.5 %all-gather.42.cloned.1.call-start = ((), (), s32[]{:S(2)}) async-start(), calls=%async_computation.28 | async-start | bytes 3244032 | tf_op jit(solution)/shard_map/all_gather | solution.py:166
  556.2 926.5 %reduce-scatter.25.cloned.1.call-start = ((), (), s32[]{:S(2)}) async-start(), calls=%async_computation.32 | async-start | bytes 40960 | tf_op jit(solution)/shard_map/reduce_scatter | solution.py:426
  1416.7 210.6 %reduce-scatter.23.cloned.1.call-start = ((), (), s32[]{:S(2)}) async-start(), calls=%async_computation.31 | async-start | bytes 10485760 | tf_op jit(solution)/shard_map/reduce_scatter | solution.py:423
  1481.9 305.7 %all-gather.46.cloned.1.call-start = ((), (), s32[]{:S(2)}) async-start(), calls=%async_computation.33 | async-start | bytes 10485760 | tf_op jit(solution)/shard_map/all_gather | solution.py:445
  1637.1 454.3 %reduce-scatter.31.cloned.1.call-start = ((), (), s32[]{:S(2)}) async-start(), calls=%async_computation.36 | async-start | bytes 327680 | tf_op jit(solution)/shard_map/reduce_scatter | solution.py:547
  2073.5 62.3 %reduce-scatter.29.cloned.1.call-start = ((), (), s32[]{:S(2)}) async-start(), calls=%async_computation.35 | async-start | bytes 2621440 | tf_op jit(solution)/shard_map/reduce_scatter | solution.py:544
  2081.8 237.8 %reduce-scatter.45.cloned.1.call-start = ((), (), s32[]{:S(2)}) async-start(), calls=%async_computation.43 | async-start | bytes 2654208 | tf_op jit(solution)/shard_map/reduce_scatter | solution.py:71
  2142.8 375.5 %reduce-scatter.39.cloned.1.call-start = ((), (), s32[]{:S(2)}) async-start(), calls=%async_computation.40 | async-start | bytes 3244032 | tf_op jit(solution)/shard_map/reduce_scatter | solution.py:92
  2153.6 366.6 %reduce-scatter.41.cloned.1.call-start = ((), (), s32[]{:S(2)}) async-start(), calls=%async_computation.41 | async-start | bytes 3244032 | tf_op jit(solution)/shard_map/reduce_scatter | solution.py:95
  2164.6 357.5 %reduce-scatter.43.cloned.1.call-start = ((), (), s32[]{:S(2)}) async-start(), calls=%async_computation.42 | async-start | bytes 3244032 | tf_op jit(solution)/shard_map/reduce_scatter | solution.py:98
  2224.5 520.6 %all-reduce.14.cloned.1.call-start = ((), (), s32[]{:S(2)}) async-start(), calls=%async_computation.46 | async-start | bytes 69206016
  2275.6 508.9 %reduce-scatter.35.cloned.1.call-start = ((), (), s32[]{:S(2)}) async-start(), calls=%async_computation.38 | async-start | bytes 1179648 | tf_op jit(solution)/shard_map/reduce_scatter | solution.py:86
  2281.9 547.3 %reduce-scatter.37.cloned.1.call-start = ((), (), s32[]{:S(2)}) async-start(), calls=%async_computation.39 | async-start | bytes 2359296 | tf_op jit(solution)/shard_map/reduce_scatter | solution.py:89
  2291.2 587.7 %reduce-scatter.33.cloned.1.call-start = ((), (), s32[]{:S(2)}) async-start(), calls=%async_computation.37 | async-start | bytes 3538944 | tf_op jit(solution)/shard_map/reduce_scatter | solution.py:83
  2319.6 597.6 %all-reduce.12.cloned.1.call-start = ((), (), s32[]{:S(2)}) async-start(), calls=%async_computation.44 | async-start | bytes 589824 | tf_op jit(solution)/shard_map/psum | solution.py:47
  2320.3 743.4 %reduce-scatter.27.cloned.1.call-start = ((), (), s32[]{:S(2)}) async-start(), calls=%async_computation.34 | async-start | bytes 10485760 | tf_op jit(solution)/shard_map/reduce_scatter | solution.py:541
  2331.3 768.3 %reduce-scatter.47.cloned.1.call-start = ((), (), s32[]{:S(2)}) async-start(), calls=%async_computation.45 | async-start | bytes 36864 | tf_op jit(solution)/shard_map/reduce_scatter | solution.py:80
  2502.9 743.6 %reduce-scatter.21.cloned.1.call-start = ((), (), s32[]{:S(2)}) async-start(), calls=%async_computation.29 | async-start | bytes 10485760 | tf_op jit(solution)/shard_map/reduce_scatter | solution.py:304
  (120 other events, 7366.2 us)
Sparse Core Ops, SparseCore 0:
  9.9 32.1 all-gather.17
  43.9 23.4 all-gather.21
  69.6 46.2 all-gather.19
  118.1 31.0 all-gather.25
  150.6 149.6 all-gather.23
  302.0 26.3 all-gather.27
  403.7 142.5 reduce-scatter.18
  548.5 150.3 all-gather.43
  700.5 147.8 all-gather.29
  850.1 65.8 all-gather.31
  917.9 67.6 all-gather.33
  987.3 67.6 all-gather.35
  1056.9 31.6 all-gather.39
  1090.4 31.6 all-gather.37
  1123.8 31.6 all-gather.41
  1416.8 19.6 reduce-scatter.24
  1482.0 145.2 reduce-scatter.22
  1637.2 150.3 all-gather.45
  2073.6 17.7 reduce-scatter.30
  2093.5 42.1 reduce-scatter.28
  2142.9 41.7 reduce-scatter.44
  2188.1 44.9 reduce-scatter.38
  2237.4 44.9 reduce-scatter.40
  2286.2 44.8 reduce-scatter.42
  2335.3 409.7 all-reduce.13
  2748.4 36.0 reduce-scatter.34
  2788.0 41.2 reduce-scatter.36
  2832.6 46.2 reduce-scatter.32
  2881.4 35.7 all-reduce.11
  2919.5 144.1 reduce-scatter.26
  3067.6 31.9 reduce-scatter.46
  3102.0 144.4 reduce-scatter.20
where the time goes:
time: 3270 us; the launch traced here: 3260 us
  waiting for transfers between devices  1570 us (48%)
  matrix products  691 us (21%)
  local copies, waits for them, and re-layouts  483 us (15%)
  other arithmetic  387 us (12%)
  blocking collectives  81.6 us (2%)
    unnamed x33, waiting for transfers between devices  228 us
    all_gather x1, waiting for transfers between devices, on_device(): lax.all_gather(normed_local, 'tp', axis=1, tiled=True)  151 us
    all_gather x1, waiting for transfers between devices, on_device(): lax.all_gather(grad_hidden.astype(narrow), 'tp', axis=1, tiled=True)  150 us
    reduce_scatter x1, waiting for transfers between devices, on_device(): lax.psum_scatter(grad_normed_all.astype(jnp.bfloat16), 'tp', scatter_dime...  145 us
    reduce_scatter x1, waiting for transfers between devices, on_device(): lax.psum_scatter(grad_hidden_all.astype(jnp.bfloat16), 'tp', scatter_dime...  144 us
    reduce_scatter x1, waiting for transfers between devices, on_device(): lax.psum_scatter(branch_terms.astype(jnp.bfloat16), 'tp', scatter_dimensi...  132 us
    reduce_scatter x1, waiting for transfers between devices, on_device(): lax.psum_scatter(attention_pieces.astype(jnp.bfloat16), 'tp', scatter_dim...  130 us
    scatter-add x1, other arithmetic, on_device(): grad_rows_acc.at[token_piece]  109 us
  transfers between devices with their start and end apart: 32, of which 21 were waited for; matrix products, arithmetic and copies ran while one was open for 38% of the time, Pallas kernels for 0%

commit v1 on v0

v1 whole, which is shorter than its diff:
```python
import functools

import jax
import jax.numpy as jnp
from jax import lax
from jax.experimental import pallas as pl
from jax.experimental.pallas import tpu as pltpu
from jax.sharding import PartitionSpec as P

HEAD_COUNT = 16
PLAIN_WIDTH = 128
ROTARY_WIDTH = 64
VALUE_WIDTH = 128
RANK = 512
TOPK = 6
SCALE = (PLAIN_WIDTH + ROTARY_WIDTH) ** (-0.5)

epsilon = 1e-06
narrow = jnp.bfloat16
wide = jnp.float32
VMEM_LIMIT = 48 * 1024 * 1024


def normalize(values, gain_row):
    return (
        values * lax.rsqrt(jnp.mean(values * values, axis=-1, keepdims=True) + epsilon) * gain_row
    )


def rotate(values, positions, direction):
    half_width = values.shape[-1] // 2
    frequency = 10000.0 ** (-jnp.arange(half_width, dtype=wide) / half_width)
    angles = positions.astype(wide)[..., None] * frequency
    cosines = jnp.cos(angles)
    sines = jnp.sin(angles) * direction
    first_half = values[..., :half_width]
    second_half = values[..., half_width:]
    return jnp.concatenate(
        [first_half * cosines - second_half * sines, first_half * sines + second_half * cosines],
        axis=-1,
    )


def dot(a, b, dims, out=wide):
    return lax.dot_general(a, b, (dims, ((), ())), preferred_element_type=wide).astype(out)


NN = ((1,), (0,))
NT = ((1,), (1,))
TN = ((0,), (0,))


def without(kernel, inputs, waits):
    def body(*refs):
        kernel(*refs[:inputs], *refs[inputs + len(waits) :])

    return body


def waiting(waits):
    return [pl.BlockSpec(memory_space=pl.ANY)] * len(waits)


def swap_halves(values):
    lane = lax.broadcasted_iota(jnp.int32, values.shape, 1)
    count, half = values.shape[1], ROTARY_WIDTH // 2
    return jnp.where(
        lane % ROTARY_WIDTH < half,
        pltpu.roll(values, count - half, 1),
        pltpu.roll(values, half, 1),
    )


def rotary_tables(positions, columns):
    half = ROTARY_WIDTH // 2
    frequency = 10000.0 ** (-jnp.arange(half, dtype=wide) / half)
    angles = positions.astype(wide)[:, None] * frequency
    cosines, sines = jnp.cos(angles), jnp.sin(angles)
    repeats = columns // ROTARY_WIDTH
    return (
        jnp.concatenate([cosines, cosines] * repeats, axis=1),
        jnp.concatenate([-sines, sines] * repeats, axis=1),
    )


def project_kernel(rows, weights, cosines, sines, nope, rope):
    step = pl.program_id(0)
    out = dot(rows[...], weights[...], NN)

    @pl.when(step < HEAD_COUNT * PLAIN_WIDTH // 512)
    def _():
        nope[...] = out.astype(narrow)

    @pl.when(step >= HEAD_COUNT * PLAIN_WIDTH // 512)
    def _():
        turned = out * jnp.concatenate([cosines[...]] * 4, axis=1)
        turned += swap_halves(out) * jnp.concatenate([sines[...]] * 4, axis=1)
        rope[...] = turned.astype(narrow)


def project(rows, weights, cosines, sines):
    count, width = rows.shape
    plain = HEAD_COUNT * PLAIN_WIDTH // 512
    turned = HEAD_COUNT * ROTARY_WIDTH // 512
    return pl.pallas_call(
        project_kernel,
        grid=(plain + turned,),
        in_specs=[
            pl.BlockSpec((count, width), lambda j: (0, 0)),
            pl.BlockSpec((width, 512), lambda j: (0, j)),
            pl.BlockSpec((count, 128), lambda j: (0, 0)),
            pl.BlockSpec((count, 128), lambda j: (0, 0)),
        ],
        out_specs=[
            pl.BlockSpec((count, 512), lambda j: (0, jnp.minimum(j, plain - 1))),
            pl.BlockSpec((count, 512), lambda j: (0, jnp.maximum(j - plain, 0))),
        ],
        out_shape=[
            jax.ShapeDtypeStruct((count, 512 * plain), narrow),
            jax.ShapeDtypeStruct((count, 512 * turned), narrow),
        ],
        compiler_params=pltpu.CompilerParams(vmem_limit_bytes=VMEM_LIMIT),
        cost_estimate=pl.CostEstimate(
            flops=2 * count * width * 512 * (plain + turned),
            bytes_accessed=2 * width * 512 * (plain + turned),
            transcendentals=0,
        ),
    )(rows, weights, cosines, sines)


def pair_half(shape, half):
    lane = lax.broadcasted_iota(jnp.int32, shape, len(shape) - 1)
    return (lane // ROTARY_WIDTH) == half


def attend_kernel(qn, qr, latent, rope, kvb, key_pos, limit, mixed, log_sum, keyval):
    kv = dot(latent[0], kvb_block(kvb), NN, narrow)
    keyval[0] = kv
    live = key_pos[...] <= limit[0]
    rope_keys = rope[0]
    for half in range(2):
        lo = half * 256
        keys = jnp.concatenate([kv[:, lo : lo + 128], rope_keys], axis=1)
        rope_rows = jnp.where(pair_half(qr.shape[1:], half), qr[0], jnp.zeros_like(qr[0]))
        queries = jnp.concatenate([qn[0, :, half * 128 : half * 128 + 128], rope_rows], axis=1)
        scores = jnp.where(live, dot(queries, keys, NT) * SCALE, -1e30)
        row_max = jnp.max(scores, axis=-1, keepdims=True)
        exponent = jnp.exp(scores - row_max)
        row_sum = jnp.sum(exponent, axis=-1, keepdims=True)
        chances = (exponent * (1.0 / row_sum)).astype(narrow)
        rows = dot(chances, kv[:, lo + 128 : lo + 256], NN, narrow)
        mixed[0, :, half * 128 : half * 128 + 128] = rows
        log_sum[0, :, half * 128 : half * 128 + 128] = jnp.broadcast_to(
            row_max + jnp.log(row_sum), rows.shape
        )


def kvb_spec(weights, first, columns):
    count, quarters, rows, _ = weights.shape
    per_piece = quarters * columns // 512
    return pl.BlockSpec(
        (count, 512 // columns, rows, columns),
        lambda p, s: (0, p % per_piece, 0, first // columns + p // per_piece),
    )


def kvb_block(kvb):
    return jnp.concatenate(
        [kvb[:, q].reshape(RANK, kvb.shape[3]) for q in range(kvb.shape[1])], axis=1
    )


def attend(qn, qr, latent, weights, kvb_first, kvb_columns, key_pos, limit):
    seqs, rows, width = qn.shape
    keys = latent.shape[1]
    pairs = HEAD_COUNT // 2
    kv_width = HEAD_COUNT * (PLAIN_WIDTH + VALUE_WIDTH)
    return pl.pallas_call(
        attend_kernel,
        grid=(pairs, seqs),
        in_specs=[
            pl.BlockSpec((1, rows, 256), lambda p, s: (s, 0, p)),
            pl.BlockSpec((1, rows, 128), lambda p, s: (s, 0, p)),
            pl.BlockSpec((1, keys, RANK), lambda p, s: (s, 0, 0)),
            pl.BlockSpec((1, keys, 128), lambda p, s: (s, 0, RANK // 128)),
            kvb_spec(weights, kvb_first, kvb_columns),
            pl.BlockSpec((1, keys), lambda p, s: (0, 0)),
            pl.BlockSpec((1, rows, 1), lambda p, s: (s, 0, 0)),
        ],
        out_specs=[
            pl.BlockSpec((1, rows, 256), lambda p, s: (s, 0, p)),
            pl.BlockSpec((1, rows, 256), lambda p, s: (s, 0, p)),
            pl.BlockSpec((1, keys, 512), lambda p, s: (s, 0, p)),
        ],
        out_shape=[
            jax.ShapeDtypeStruct((seqs, rows, width), narrow),
            jax.ShapeDtypeStruct((seqs, rows, width), wide),
            jax.ShapeDtypeStruct((seqs, keys, kv_width), narrow),
        ],
        compiler_params=pltpu.CompilerParams(vmem_limit_bytes=VMEM_LIMIT),
        cost_estimate=pl.CostEstimate(
            flops=2 * seqs * HEAD_COUNT * keys * (RANK * 256 + rows * 384),
            bytes_accessed=2 * seqs * keys * kv_width,
            transcendentals=seqs * HEAD_COUNT * rows * keys,
        ),
    )(qn, qr, latent, latent, weights, key_pos, limit)


def attend_back_kernel(
    qn, qr, latent, rope, kvb, keyval, grad_mixed, log_sum, key_pos, limit,
    cosines, sines, latents_before, grad_qn, grad_qr, grad_latents, grad_kvb, grad_latent, grad_rope,
):
    pair = pl.program_id(0)
    seq = pl.program_id(1)
    kv = keyval[0]
    live = key_pos[...] <= limit[0]
    rope_keys = rope[0]
    grads = []
    rope_queries = []
    rope_total = None
    for half in range(2):
        lo = half * 256
        values = kv[:, lo + 128 : lo + 256]
        keys = jnp.concatenate([kv[:, lo : lo + 128], rope_keys], axis=1)
        rope_rows = jnp.where(pair_half(qr.shape[1:], half), qr[0], jnp.zeros_like(qr[0]))
        queries = jnp.concatenate([qn[0, :, half * 128 : half * 128 + 128], rope_rows], axis=1)
        sums = log_sum[0, :, half * 128 : half * 128 + 1]
        scores = jnp.where(live, dot(queries, keys, NT) * SCALE, -1e30)
        chances = jnp.exp(scores - sums)
        grad_rows = grad_mixed[0, :, half * 128 : half * 128 + 128]
        grad_chances = dot(grad_rows, values, NT)
        inner = jnp.sum(chances * grad_chances, axis=-1, keepdims=True)
        grad_scores = (chances * (grad_chances - inner)).astype(narrow)
        grad_queries = dot(grad_scores, keys, NN) * SCALE
        grad_qn[0, :, half * 128 : half * 128 + 128] = grad_queries[:, :128].astype(narrow)
        rope_queries.append(grad_queries[:, 128:])
        grad_keys = dot(grad_scores, queries, TN) * SCALE
        grad_values = dot(chances.astype(narrow), grad_rows, TN)
        grads += [grad_keys[:, :128].astype(narrow), grad_values.astype(narrow)]
        rope_part = grad_keys[:, 128:]
        rope_total = rope_part if rope_total is None else rope_total + rope_part
    rope_rows = jnp.where(pair_half(qr.shape[1:], 0), rope_queries[0], rope_queries[1])
    rope_rows = rope_rows * cosines[...] - swap_halves(rope_rows) * sines[...]
    grad_qr[0] = rope_rows.astype(narrow)
    grad_keyval = jnp.concatenate(grads, axis=1)
    latent_part = dot(grad_keyval, kvb_block(kvb), NT)
    kvb_part = dot(latent[0], grad_keyval, TN)

    @pl.when(pair == 0)
    def _():
        grad_latent[seq] = latent_part + latents_before[seq, :, :RANK].astype(wide)
        grad_rope[seq] = rope_total + latents_before[seq, :, RANK:].astype(wide)

    @pl.when(pair > 0)
    def _():
        grad_latent[seq] += latent_part
        grad_rope[seq] += rope_total

    @pl.when(pair == pl.num_programs(0) - 1)
    def _():
        grad_latents[seq, :, :RANK] = grad_latent[seq].astype(narrow)
        rope_sum = grad_rope[seq]
        rope_sum = rope_sum + pltpu.roll(rope_sum, ROTARY_WIDTH, 1)
        grad_latents[seq, :, RANK:] = jnp.where(
            pair_half(rope_sum.shape, 0), rope_sum, 0.0
        ).astype(narrow)

    columns = grad_kvb.shape[3]
    for q in range(grad_kvb.shape[1]):
        part = kvb_part[:, q * columns : (q + 1) * columns].reshape(
            grad_kvb.shape[0], grad_kvb.shape[2], columns
        )

        @pl.when(seq == 0)
        def _(q=q, part=part):
            grad_kvb[:, q] = part

        @pl.when(seq > 0)
        def _(q=q, part=part):
            grad_kvb[:, q] += part


def attend_back(
    qn, qr, latent, weights, kvb_first, kvb_columns, keyval, grad_mixed, log_sum, key_pos, limit,
    cosines, sines, latents_before, first, pairs, waits=(),
):
    seqs, rows, _ = qn.shape
    keys = latent.shape[1]
    width = pairs * 256
    kv = kvb_spec(weights, kvb_first, kvb_columns)
    return pl.pallas_call(
        without(attend_back_kernel, 13, waits),
        grid=(pairs, seqs),
        in_specs=[
            pl.BlockSpec((1, rows, 256), lambda p, s: (s, 0, p + first)),
            pl.BlockSpec((1, rows, 128), lambda p, s: (s, 0, p + first)),
            pl.BlockSpec((1, keys, RANK), lambda p, s: (s, 0, 0)),
            pl.BlockSpec((1, keys, 128), lambda p, s: (s, 0, RANK // 128)),
            pl.BlockSpec(kv.block_shape, lambda p, s: kv.index_map(p + first, s)),
            pl.BlockSpec((1, keys, 512), lambda p, s: (s, 0, p + first)),
            pl.BlockSpec((1, rows, 256), lambda p, s: (s, 0, p + first)),
            pl.BlockSpec((1, rows, 256), lambda p, s: (s, 0, p + first)),
            pl.BlockSpec((1, keys), lambda p, s: (0, 0)),
            pl.BlockSpec((1, rows, 1), lambda p, s: (s, 0, 0)),
            pl.BlockSpec((rows, 128), lambda p, s: (0, 0)),
            pl.BlockSpec((rows, 128), lambda p, s: (0, 0)),
            pl.BlockSpec((seqs, keys, RANK + 128), lambda p, s: (0, 0, 0)),
        ]
        + waiting(waits),
        out_specs=[
            pl.BlockSpec((1, rows, 256), lambda p, s: (s, 0, p)),
            pl.BlockSpec((1, rows, 128), lambda p, s: (s, 0, p)),
            pl.BlockSpec((seqs, keys, RANK + 128), lambda p, s: (0, 0, 0)),
            kvb_spec(weights, 0, kvb_columns),
        ],
        out_shape=[
            jax.ShapeDtypeStruct((seqs, rows, width), narrow),
            jax.ShapeDtypeStruct((seqs, rows, width // 2), narrow),
            jax.ShapeDtypeStruct((seqs, keys, RANK + 128), narrow),
            jax.ShapeDtypeStruct(weights.shape[:3] + (pairs * 512 // weights.shape[1],), wide),
        ],
        scratch_shapes=[
            pltpu.VMEM((seqs, keys, RANK), wide),
            pltpu.VMEM((seqs, keys, 128), wide),
        ],
        compiler_params=pltpu.CompilerParams(vmem_limit_bytes=VMEM_LIMIT),
        cost_estimate=pl.CostEstimate(
            flops=4 * seqs * pairs * keys * (2 * RANK * 256 + rows * 1024),
            bytes_accessed=2 * seqs * keys * pairs * 512,
            transcendentals=2 * seqs * pairs * rows * keys,
        ),
    )(qn, qr, latent, latent, weights, keyval, grad_mixed, log_sum, key_pos, limit, cosines, sines, latents_before, *waits)


def ffn_kernel(pieces, *refs):
    rows_h, rows_g, weight = refs[:pieces], refs[pieces : 2 * pieces], refs[2 * pieces]
    unit_gu, unit_d = refs[2 * pieces + 1], refs[2 * pieces + 2]
    branch, grad_rows = refs[2 * pieces + 3 : 3 * pieces + 3], refs[3 * pieces + 3 : 4 * pieces + 3]
    acts, grad_gate_up, grad_gates, total, grad_total = refs[4 * pieces + 3 :]
    piece = pl.program_id(0)
    step = pl.program_id(1)
    steps = pl.num_programs(1)
    units, hidden, width = unit_d.shape

    def work(source_h, source_g):
        w_gu = unit_gu[...].reshape(2 * units * hidden, width)
        w_d = unit_d[...].reshape(units * hidden, width)
        gate_up = dot(w_gu, source_h[...], NT)
        grad_act = dot(w_d, source_g[...], NT)
        act_parts, grad_parts = [], []
        for k in range(units):
            gate = gate_up[2 * k * hidden : (2 * k + 1) * hidden]
            up = gate_up[(2 * k + 1) * hidden : (2 * k + 2) * hidden]
            part = grad_act[k * hidden : (k + 1) * hidden]
            scale = weight[0, k]
            sigmoid = 1.0 / (1.0 + jnp.exp(-gate))
            silu = gate * sigmoid
            act = silu * up
            grad_gates[0, k] = jnp.sum(act * part, axis=0, keepdims=True)
            act_parts.append((act * scale).astype(narrow))
            part = part * scale
            grad_parts.append((part * up * (sigmoid + silu * (1.0 - sigmoid))).astype(narrow))
            grad_parts.append((part * silu).astype(narrow))
        act_rows = jnp.concatenate(act_parts, axis=0)
        grad_gu = jnp.concatenate(grad_parts, axis=0)
        acts[0] = act_rows.reshape(acts.shape[1:])
        grad_gate_up[0] = grad_gu.reshape(grad_gate_up.shape[1:])
        for first in range(0, width, 1024):
            part = slice(first, first + 1024)
            out = dot(act_rows, w_d[:, part], TN)
            grad = dot(grad_gu, w_gu[:, part], TN)

            @pl.when(step == 0)
            def _(part=part, out=out, grad=grad):
                total[:, part] = out
                grad_total[:, part] = grad

            @pl.when(step > 0)
            def _(part=part, out=out, grad=grad):
                total[:, part] += out
                grad_total[:, part] += grad

    for s in range(pieces):

        @pl.when(piece == s)
        def _(s=s):
            work(rows_h[s], rows_g[s])

            @pl.when(step == steps - 1)
            def _():
                branch[s][...] = total[...].astype(narrow)
                grad_rows[s][...] = grad_total[...].astype(narrow)


def feed_forward(rows_h, rows_g, weights, unit_rows, waits=()):
    pieces = len(rows_h)
    count, width = rows_h[0].shape
    units, hidden, _ = unit_rows.shape
    hidden = hidden // 3
    block = min(units, 4)
    whole = pl.BlockSpec((count, width), lambda s, j: (0, 0), pipeline_mode=pl.Buffered(1))

    def units_of(rows, columns):
        return pl.BlockSpec((1, block, rows, columns), lambda s, j: (s, j, 0, 0))

    outs = pl.pallas_call(
        without(functools.partial(ffn_kernel, pieces), 2 * pieces + 3, waits),
        grid=(pieces, units // block),
        in_specs=[whole] * (2 * pieces)
        + [
            units_of(1, count),
            pl.BlockSpec((block, 2 * hidden, width), lambda s, j: (j, 0, 0)),
            pl.BlockSpec((block, hidden, width), lambda s, j: (j, 2, 0)),
        ]
        + waiting(waits),
        out_specs=[whole] * (2 * pieces)
        + [units_of(hidden, count), units_of(2 * hidden, count), units_of(1, count)],
        out_shape=[jax.ShapeDtypeStruct((count, width), narrow)] * (2 * pieces)
        + [
            jax.ShapeDtypeStruct((pieces, units, hidden, count), narrow),
            jax.ShapeDtypeStruct((pieces, units, 2 * hidden, count), narrow),
            jax.ShapeDtypeStruct((pieces, units, 1, count), wide),
        ],
        scratch_shapes=[pltpu.VMEM((count, width), wide), pltpu.VMEM((count, width), wide)],
        compiler_params=pltpu.CompilerParams(vmem_limit_bytes=60 * 1024 * 1024),
        cost_estimate=pl.CostEstimate(
            flops=12 * pieces * units * hidden * count * width,
            bytes_accessed=pieces * (6 * units * hidden * width + 8 * count * width),
            transcendentals=pieces * units * hidden * count,
        ),
    )(*rows_h, *rows_g, jnp.stack(weights), unit_rows, unit_rows, *waits)
    return [
        (outs[s], outs[pieces + s], outs[2 * pieces], outs[2 * pieces + 1], outs[2 * pieces + 2][s], s)
        for s in range(pieces)
    ]


def weight_grad_kernel(pieces, joined, order, *refs):
    rows_h, rows_g = refs[:pieces], refs[pieces : 2 * pieces]
    acts, grads = refs[2 * pieces : 4 * pieces], refs[4 * pieces : 6 * pieces]
    out = refs[6 * pieces + joined]
    hidden = acts[0].shape[2]
    for k in range(2):
        gate_up = sum(
            dot(grads[2 * s + k][0, 0], rows_h[s][...], NN) for s in range(pieces)
        )
        down = sum(dot(acts[2 * s + k][0, 0], rows_g[s][...], NN) for s in range(pieces))
        if joined:
            before = refs[6 * pieces]
            gate_up += before[k, : 2 * hidden].astype(wide)
            down += before[k, 2 * hidden :].astype(wide)
        out[k, : 2 * hidden] = gate_up.astype(narrow)
        out[k, 2 * hidden :] = down.astype(narrow)


def weight_grads(found, rows_h, rows_g, order, before=None, waits=()):
    pieces, units = len(found), order.shape[0]
    _, _, hidden, count = found[0][2].shape
    width = rows_h[0].shape[1]
    joined = 0 if before is None else 1
    whole = pl.BlockSpec(
        (count, width), lambda j, order: (0, 0), pipeline_mode=pl.Buffered(1)
    )
    pair = pl.BlockSpec((2, 3 * hidden, width), lambda j, order: (j, 0, 0))

    def units_of(rows, at):
        return [
            pl.BlockSpec((1, 1, rows, count), lambda j, order, k=k: (at, order[2 * j + k], 0, 0))
            for k in range(2)
        ]

    return pl.pallas_call(
        without(
            functools.partial(weight_grad_kernel, pieces, joined), 6 * pieces + joined + 1, waits
        ),
        grid_spec=pltpu.PrefetchScalarGridSpec(
            num_scalar_prefetch=1,
            grid=(units // 2,),
            in_specs=[whole] * (2 * pieces)
            + [spec for item in found for spec in units_of(hidden, item[5])]
            + [spec for item in found for spec in units_of(2 * hidden, item[5])]
            + [pair] * joined
            + waiting(waits),
            out_specs=pair,
        ),
        out_shape=jax.ShapeDtypeStruct((units, 3 * hidden, width), narrow),
        compiler_params=pltpu.CompilerParams(vmem_limit_bytes=60 * 1024 * 1024),
        cost_estimate=pl.CostEstimate(
            flops=6 * pieces * units * hidden * count * width,
            bytes_accessed=6 * units * hidden * (width + pieces * count)
            + 4 * pieces * count * width,
            transcendentals=0,
        ),
    )(
        order,
        *rows_h,
        *rows_g,
        *[item[2] for item in found for _ in range(2)],
        *[item[3] for item in found for _ in range(2)],
        *([] if before is None else [before]),
        *waits,
    )


def zero_of(*others):
    firsts = [lax.slice(o, [0] * o.ndim, [1] * o.ndim).reshape(()) for o in others]
    return sum(jnp.where(first != first, 1.0, 0.0) for first in firsts)


def after(values, *others):
    if not others:
        return values
    return (values.astype(wide) + zero_of(*others)).astype(values.dtype)


def hop(values):
    count = lax.axis_size("tp")
    return lax.ppermute(values, "tp", [(i, (i + 1) % count) for i in range(count)])


def ring_gather(values):
    pieces = [values]
    for _ in range(lax.axis_size("tp") - 1):
        pieces.append(hop(pieces[-1]))
    return pieces


def ring_scatter(pieces):
    total = pieces[1].astype(narrow)
    for piece in pieces[2:]:
        total = (hop(total).astype(wide) + piece).astype(narrow)
    return hop(total).astype(wide) + pieces[0]


def cross_scatter(pieces):
    return sum((item.astype(wide) for item in cross_moves(pieces)), pieces[0].astype(wide))


def scatter_tp(values, axis, rows):
    count, rank = lax.axis_size("tp"), lax.axis_index("tp")
    size = values.shape[axis] // count
    placed = jnp.concatenate(
        [
            lax.dynamic_slice_in_dim(
                values, (rank + count - d) % count * size, size, axis
            ).reshape(rows, -1)
            for d in range(count)
        ],
        axis=0,
    )
    return lax.psum_scatter(placed, "tp", scatter_dimension=0, tiled=True).astype(wide)


def cross_moves(pieces):
    count = lax.axis_size("tp")
    return [
        lax.ppermute(pieces[s].astype(narrow), "tp", [(i, (i - s) % count) for i in range(count)])
        for s in range(1, count)
    ]


def cross_sum(values):
    count, rank = lax.axis_size("tp"), lax.axis_index("tp")
    values = values.astype(narrow)
    pieces = [values] + [
        lax.ppermute(values, "tp", [(i, (i + s) % count) for i in range(count)])
        for s in range(1, count)
    ]
    stacked = jnp.stack(pieces)
    return sum(
        lax.dynamic_index_in_dim(stacked, (rank + count - r) % count, 0, False).astype(wide)
        for r in range(count)
    )


def swap(values, mask):
    return lax.ppermute(values, "fsdp", [(i, i ^ mask) for i in range(lax.axis_size("fsdp"))])


def gather_fsdp(values, axis=0):
    return lax.all_gather(values, "fsdp", axis=axis, tiled=True)


def scatter_fsdp(values, axis=0):
    return lax.psum_scatter(values.astype(narrow), "fsdp", scatter_dimension=axis, tiled=True)


def relative_masks(count):
    return [0, 2, 6, 4] if count == 8 else list(range(0, count, 2))


def relative_blocks(values, other, axis):
    count, rank = lax.axis_size("fsdp"), lax.axis_index("fsdp")
    size = values.shape[axis] // count
    return [
        lax.dynamic_slice_in_dim(values, (rank ^ (mask + other)) * size, size, axis)
        for mask in relative_masks(count)
    ]


class Scatter:
    def __init__(self, sent):
        self.sent = sent.astype(narrow)
        self.received = swap(self.sent, 1)

    def join(self, make, *others):
        part = make(self.received, zero_of(*others) if others else None)
        half = part.shape[1] // 2
        self.part = part
        self.from_x, self.from_y = swap(part[1:3, :half], 2), swap(part[2:4, half:], 4)

    def turn(self, *others):
        half = self.part.shape[1] // 2
        zero = zero_of(*others) if others else 0.0
        self.own_top = self.part[0, :half].astype(wide) + self.from_x[0]
        self.own_low = self.part[0, half:].astype(wide) + self.from_y[1]
        top = (self.part[3, :half].astype(wide) + self.from_x[1] + zero).astype(narrow)
        low = (self.part[1, half:].astype(wide) + self.from_y[0] + zero).astype(narrow)
        self.turned = top
        self.last_top, self.last_low = swap(top, 4), swap(low, 2)

    def end(self, *others):
        zero = zero_of(*others) if others else 0.0
        return jnp.concatenate(
            [self.own_top + self.last_top + zero, self.own_low + self.last_low + zero], axis=0
        )


class WholeScatter:
    def __init__(self, values, axis):
        self.sent = self.part = self.turned = values.astype(narrow)
        self.axis = axis

    def join(self, make, *others):
        pass

    def turn(self, *others):
        pass

    def end(self, *others):
        total = scatter_fsdp(self.sent, self.axis).astype(wide)
        return total + zero_of(*others) if others else total


def joiner(make):
    def join(received, zero):
        total = make(0) + received.astype(wide)
        return (total if zero is None else total + zero).astype(narrow)

    return join


def scatter_product(rows, columns, joined=None):
    count = lax.axis_size("fsdp")
    if count != 8:
        out = dot(rows, columns, TN, narrow)
        if joined is not None:
            out = jnp.concatenate([out, joined.astype(narrow)], axis=1)
        return WholeScatter(out, 0), None

    def make(other):
        chosen = jnp.concatenate(relative_blocks(rows, other, 1), axis=1)
        return dot(chosen, columns, TN).reshape(count // 2, -1, columns.shape[1])

    def more(other):
        return jnp.stack(relative_blocks(joined, other, 0))

    if joined is None:
        return Scatter(make(1)), joiner(make)

    def join(received, zero):
        cut = columns.shape[1]
        zero = 0.0 if zero is None else zero
        return jnp.concatenate(
            [
                (make(0) + received[..., :cut].astype(wide) + zero).astype(narrow),
                (more(0) + received[..., cut:].astype(wide)).astype(narrow),
            ],
            axis=2,
        )

    return Scatter(jnp.concatenate([make(1).astype(narrow), more(1).astype(narrow)], axis=2)), join


def scatter_values(values, axis):
    if lax.axis_size("fsdp") != 8:
        return WholeScatter(values, axis), None

    def make(other):
        return jnp.stack(relative_blocks(values, other, axis))

    return Scatter(make(1)), joiner(make)


def on_device(
    tokens,
    lengths,
    routes,
    slot_ranks,
    attn_gain,
    query_weight,
    latent_key_weight,
    latent_gain,
    kvb_weight,
    output_weight,
    ffn_gain,
    router_matrix,
    shared_gate_weight,
    shared_up_weight,
    shared_down_weight,
    expert_gate,
    expert_up,
    expert_down,
    cotangent,
):
    tp_count = lax.axis_size("tp")
    tp_rank = lax.axis_index("tp")
    fsdp_count = lax.axis_size("fsdp")
    seq_count, local_len, width = tokens.shape
    seq_len = local_len * tp_count
    group_rows = seq_count * seq_len
    own_rows = seq_count * local_len
    own_experts = expert_gate.shape[0]
    expert_count = own_experts * fsdp_count
    capacity = 4 * group_rows // expert_count
    ffe = expert_gate.shape[2]
    sff = shared_gate_weight.shape[1]
    head_local = HEAD_COUNT // tp_count
    own_first = tp_rank * local_len
    own_positions = own_first + jnp.arange(local_len, dtype=jnp.int32)
    rel_rank = [(tp_rank + tp_count - s) % tp_count for s in range(tp_count)]
    key_pos = jnp.concatenate(
        [r * local_len + jnp.arange(local_len, dtype=jnp.int32) for r in rel_rank]
    )
    limit = jnp.minimum(own_positions[None, :], lengths[:, None] - 1)[..., None]

    shard = attn_gain.shape[0]
    latent_shard = latent_gain.shape[0]
    latent_width = latent_key_weight.shape[1]
    gain_rows = [latent_width, latent_width + 8, latent_width + 16]
    router_first = latent_width + 24
    small_rows = -(-(router_first + expert_count) // 32) * 32

    def small_stack(latent_key, attn, ffn, latent, router):
        rows = [latent_key]
        for gain in (attn, ffn, latent):
            rows.append(jnp.pad(gain[None], ((0, 7), (0, 0))))
        rows += [router]
        if small_rows > router_first + expert_count:
            rows.append(
                jnp.zeros((small_rows - router_first - expert_count, router.shape[1]), router.dtype)
            )
        return jnp.concatenate(rows, axis=0)

    small_shard = small_stack(
        latent_key_weight.T,
        attn_gain,
        ffn_gain,
        jnp.pad(latent_gain, (0, shard - latent_shard)),
        router_matrix.T,
    )
    small_all = gather_fsdp(small_shard, axis=1)
    latent_key_whole = small_all[:latent_width]
    attn_scale = small_all[gain_rows[0]].astype(wide)
    ffn_scale = small_all[gain_rows[1]].astype(wide)
    latent_scale = (
        small_all[gain_rows[2]]
        .reshape(fsdp_count, shard)[:, :latent_shard]
        .reshape(-1)
        .astype(wide)
    )
    router_t = small_all[router_first : router_first + expert_count]

    query_heads = query_weight.reshape(shard, head_local, PLAIN_WIDTH + ROTARY_WIDTH)
    nope_cols, rope_cols = head_local * PLAIN_WIDTH, head_local * ROTARY_WIDTH
    query_cols, output_cols = query_weight.shape[1], output_weight.shape[0]
    kv_rows, kv_cols = kvb_weight.shape
    quarters = shard // kv_rows
    kvb_columns = kv_cols // quarters
    attention_shard = jnp.concatenate(
        [
            query_heads[..., :PLAIN_WIDTH].reshape(shard, -1),
            query_heads[..., PLAIN_WIDTH:].reshape(shard, -1),
            output_weight.T,
            jnp.concatenate(jnp.split(kvb_weight, quarters, axis=1), axis=0),
        ],
        axis=1,
    )
    attention_pieces = ring_gather(after(attention_shard, small_shard))
    cuts = [0, nope_cols, query_cols, query_cols + output_cols, query_cols + output_cols + kvb_columns]
    attention_joined = jnp.concatenate(
        [
            piece[:, first:last]
            for first, last in zip(cuts[:-1], cuts[1:])
            for piece in attention_pieces
        ],
        axis=1,
    )
    attention_all = gather_fsdp(attention_joined)
    query_end = tp_count * query_cols
    kvb_first = query_end + tp_count * output_cols
    query_whole = attention_all[:, :query_end]
    output_whole = attention_all[:, query_end:kvb_first]
    kvb_whole = attention_all.reshape(fsdp_count, quarters, kv_rows, -1)

    token_rows = tokens.reshape(own_rows, width).astype(wide)
    normed = normalize(token_rows, attn_scale).astype(narrow)
    latent_rows = dot(normed, latent_key_whole, NT)
    compressed = latent_rows[:, :RANK]
    compressed_n = normalize(compressed, latent_scale).astype(narrow)
    row_positions = jnp.concatenate([own_positions] * seq_count)
    key_rope_own = rotate(latent_rows[:, RANK:], row_positions, 1.0).astype(narrow)
    latent_pieces = ring_gather(
        after(
            jnp.concatenate([compressed_n, key_rope_own, key_rope_own], axis=1),
            attention_joined,
        )
    )
    latent_all = jnp.concatenate(
        [piece.reshape(seq_count, local_len, -1) for piece in latent_pieces], axis=1
    )

    split = 2 if ffe % 32 == 0 else 1
    unit = ffe // split
    shared_units = sff // unit
    shared_shard = jnp.concatenate(
        [
            shared_gate_weight.T.reshape(shared_units, unit, shard),
            shared_up_weight.T.reshape(shared_units, unit, shard),
            shared_down_weight.reshape(shared_units, unit, shard),
        ],
        axis=1,
    )
    weights = [
        gather_fsdp(after(shared_shard.reshape(3 * sff, shard), latent_pieces[2]), axis=1).reshape(
            shared_units, 3 * unit, width
        )
    ]
    gate_rows, up_rows = expert_gate[0].T, expert_up[0].T
    for g in range(split):
        part = slice(g * unit, (g + 1) * unit)
        shard_rows = jnp.concatenate([gate_rows[part], up_rows[part], expert_down[0, part]], axis=0)
        weights.append(
            gather_fsdp(after(shard_rows, latent_pieces[1 + 2 * g])).reshape(
                expert_count, 3 * unit, width
            )
        )

    live_mask = (own_positions[None, :] < lengths[:, None]).astype(wide).reshape(own_rows, 1)
    grad_out = live_mask * cotangent.reshape(own_rows, width).astype(wide)
    grad_pieces = ring_gather(after(grad_out.astype(narrow), latent_all))

    cosines, sines = rotary_tables(own_positions, 128)
    query_nope, query_rope = project(
        normed,
        attention_all,
        jnp.concatenate([cosines] * seq_count),
        jnp.concatenate([sines] * seq_count),
    )
    query_nope = query_nope.reshape(seq_count, local_len, -1)
    query_rope = query_rope.reshape(seq_count, local_len, -1)
    key_row = key_pos[None, :]
    mixed, log_sums, keyval = attend(
        query_nope, query_rope, latent_all, kvb_whole, kvb_first, kvb_columns,
        key_row, limit
    )
    mixed = mixed.reshape(own_rows, -1)
    hidden = token_rows + dot(mixed, output_whole, NT)
    hidden_normed = normalize(hidden, ffn_scale).astype(narrow)
    hidden_pieces = ring_gather(hidden_normed)

    expert_ids = jnp.arange(expert_count, dtype=jnp.int32)[:, None, None]
    ones = jnp.ones((shared_units, 1, own_rows), wide)
    gate_tables = []
    for s in range(tp_count):
        first = rel_rank[s] * local_len
        route_t = lax.dynamic_slice_in_dim(routes, first, local_len, 1).reshape(own_rows, TOPK).T
        rank_t = lax.dynamic_slice_in_dim(slot_ranks, first, local_len, 1).reshape(own_rows, TOPK).T
        hits = route_t[None] == expert_ids
        chosen = jnp.any(hits, axis=1)
        kept = jnp.any(hits & (rank_t < capacity)[None], axis=1).astype(wide)
        logits = dot(router_t, hidden_pieces[s], NT)
        picked = jnp.where(chosen, logits, -1e30)
        exponent = jnp.where(chosen, jnp.exp(picked - jnp.max(picked, axis=0, keepdims=True)), 0.0)
        gates = exponent / jnp.sum(exponent, axis=0, keepdims=True)
        gate_tables.append((gates, kept))

    chunks = range(tp_count)
    results = {}
    previous = []

    def run(group, which, *waits):
        tables = [
            ones if group == 0 else (gate_tables[s][0] * gate_tables[s][1])[:, None, :]
            for s in which
        ]
        found = feed_forward(
            [hidden_pieces[s] for s in which],
            [grad_pieces[s] for s in which],
            tables,
            weights[group],
            [*previous, *waits],
        )
        for s, item in zip(which, found):
            results[group, s] = item
        previous[:] = [found[0][4]]

    def grads_of(group, units, *others, before=None):
        out = weight_grads(
            [results[group, s] for s in chunks],
            hidden_pieces,
            grad_pieces,
            units,
            before,
            [*previous, *others],
        )
        previous[:] = [out]
        return out

    def finish_piece(s, *others):
        found = [results[g, s] for g in range(split + 1)]
        branch = sum(item[0].astype(wide) for item in found).astype(narrow)
        gates, kept = gate_tables[s]
        grad_gates = sum(item[4][:, 0] for item in found[1:]) * kept
        logits = (
            gates * (grad_gates - jnp.sum(gates * grad_gates, axis=0, keepdims=True))
        ).astype(narrow)
        grad_hidden = sum(item[1].astype(wide) for item in found)
        if others:
            grad_hidden += zero_of(*others)
        return branch, grad_hidden + dot(logits, router_t, TN), logits

    last_order = list(chunks[1:]) + [0]
    pairs = [chunks[s : s + 2] for s in range(0, tp_count, 2)]
    if split == 2:
        run(1, [0])
        run(1, [1])
    run(0, [0])
    run(0, [1], hidden_pieces[2])
    for which in pairs[1:]:
        if split == 2:
            for s in which:
                run(1, [s])
        run(0, which)
    all_units = jnp.arange(expert_count, dtype=jnp.int32)
    shared_sum = scatter_fsdp(
        grads_of(0, jnp.arange(shared_units, dtype=jnp.int32)).reshape(3 * sff, width), 1
    )
    first_sum = None
    if split == 2:
        first_sum = scatter_fsdp(grads_of(1, all_units).reshape(-1, width))

    pieces, total = {}, None
    for k, s in enumerate(last_order):
        if k == 2:
            previous.append(shared_sum)
        if k == tp_count - 1:
            pieces[last_order[1]] = finish_piece(last_order[1], *previous)
            total = (hop(total).astype(wide) + pieces[last_order[1]][1]).astype(narrow)
            previous.append(total)
        run(split, [s])
        if k == 0:
            pieces[s] = finish_piece(s)
            total = pieces[s][1].astype(narrow)
            previous.append(total)
    for s in last_order[2:-1]:
        pieces[s] = finish_piece(s, *previous)
        total = (hop(total).astype(wide) + pieces[s][1]).astype(narrow)
    previous.append(total)
    if first_sum is not None:
        previous.append(first_sum)
    last_sum = scatter_fsdp(grads_of(split, all_units).reshape(-1, width))
    pieces[0] = finish_piece(0, *previous)
    grad_hidden_own = hop(total).astype(wide) + pieces[0][1]

    hidden_back = jax.vjp(normalize, hidden, ffn_scale)[1]
    grad_hnorm, grad_ffn_gain = hidden_back(grad_hidden_own)
    grad_hidden = grad_out + grad_hnorm
    grad_attn = grad_hidden.astype(narrow)
    branch_total = after(pieces[last_order[0]][0], grad_attn)
    out_scatter, make_out = scatter_product(grad_attn, mixed)
    grad_mixed = dot(after(grad_attn, out_scatter.sent), output_whole, NN, narrow)
    out_scatter.join(make_out, grad_mixed)

    def back(first, pairs, rows, latents_before, waits):
        return attend_back(
            query_nope, query_rope, latent_all, kvb_whole, kvb_first, kvb_columns, keyval,
            rows.reshape(seq_count, local_len, -1), log_sums, key_row, limit,
            cosines, sines, latents_before, first, pairs, waits,
        )

    pairs_half = HEAD_COUNT // 4
    first_qn, first_qr, first_latents, first_kvb = back(
        0, pairs_half, grad_mixed, jnp.zeros_like(latent_all), [out_scatter.part]
    )
    first_query = jnp.concatenate([first_qn, first_qr], axis=-1).reshape(own_rows, -1)
    first_scatter, make_first_query = scatter_product(
        normed, first_query, first_kvb.reshape(width, -1)
    )
    out_scatter.turn(first_scatter.sent)
    branch_total = (
        hop(branch_total).astype(wide) + after(pieces[2][0], out_scatter.turned)
    ).astype(narrow)
    second_qn, second_qr, grad_latent_all, second_kvb = back(
        pairs_half, pairs_half, grad_mixed, first_latents,
        [branch_total, out_scatter.turned, last_sum],
    )

    grad_latent_sum = scatter_tp(grad_latent_all, 1, own_rows)
    second_query = jnp.concatenate([second_qn, second_qr], axis=-1).reshape(own_rows, -1)
    second_scatter, make_second_query = scatter_product(
        normed, second_query, second_kvb.reshape(width, -1)
    )
    out_sum = out_scatter.end(second_scatter.sent)
    first_scatter.join(make_first_query, out_sum)
    second_scatter.join(make_second_query, first_scatter.part)
    half_plain, half_turned = first_qn.shape[2], first_qr.shape[2]
    query_gradient = jnp.concatenate(
        [
            first_query[:, :half_plain],
            second_query[:, :half_plain],
            first_query[:, half_plain:],
            second_query[:, half_plain:],
        ],
        axis=1,
    )
    grad_normed = dot(after(query_gradient, second_scatter.part), query_whole, NT)
    first_scatter.turn(grad_normed)

    latent_back = jax.vjp(normalize, compressed, latent_scale)[1]
    grad_compressed, grad_latent_gain = latent_back(grad_latent_sum[:, :RANK])
    latent_gradient = jnp.concatenate(
        [
            grad_compressed,
            rotate(grad_latent_sum[:, RANK : RANK + ROTARY_WIDTH], row_positions, -1.0),
        ],
        axis=-1,
    ).astype(narrow)
    latent_key_gradient = dot(latent_gradient, normed, TN)
    grad_normed = grad_normed + dot(latent_gradient, latent_key_whole, NN)
    token_back = jax.vjp(normalize, token_rows, attn_scale)[1]
    grad_tnorm, grad_attn_gain = token_back(grad_normed)
    grad_tokens = (grad_hidden + grad_tnorm).astype(narrow).reshape(tokens.shape)

    router_gradient = sum(dot(pieces[s][2], hidden_pieces[s], NN) for s in chunks)

    small_grads = small_stack(
        latent_key_gradient,
        grad_attn_gain,
        grad_ffn_gain,
        jnp.pad(
            grad_latent_gain.reshape(fsdp_count, latent_shard),
            ((0, 0), (0, shard - latent_shard)),
        ).reshape(-1),
        router_gradient,
    )
    small_sum = cross_sum(scatter_fsdp(small_grads, 1))
    second_scatter.turn(small_grads)
    for s in chunks[3:]:
        branch_total = (
            hop(branch_total).astype(wide) + after(pieces[s][0], second_scatter.turned)
        ).astype(narrow)

    first_own = first_scatter.end()
    second_own = second_scatter.end()
    half_query = half_plain + half_turned

    def query_piece(s):
        half = tp_count // 2
        values, at = (first_own, s) if s < half else (second_own, s - half)
        return jnp.concatenate(
            [
                values[:, at * nope_cols : (at + 1) * nope_cols],
                values[:, half_plain + at * rope_cols : half_plain + (at + 1) * rope_cols],
                values[:, half_query + at * kvb_columns : half_query + (at + 1) * kvb_columns],
            ],
            axis=1,
        )

    out_own = cross_scatter(jnp.split(out_sum, tp_count, axis=1)).T
    query_own = cross_scatter([query_piece(s) for s in chunks])
    branch_own = hop(branch_total).astype(wide) + pieces[0][0]
    output = (live_mask * (hidden + branch_own)).astype(narrow).reshape(tokens.shape)
    kvb_own = jnp.concatenate(jnp.split(query_own[:, query_cols:], quarters, axis=0), axis=1)
    query_own = jnp.concatenate(
        [
            query_own[:, :nope_cols].reshape(shard, head_local, PLAIN_WIDTH),
            query_own[:, nope_cols:query_cols].reshape(shard, head_local, ROTARY_WIDTH),
        ],
        axis=-1,
    ).reshape(shard, -1)
    shared_sum = shared_sum.astype(wide).reshape(shared_units, 3, unit, shard)
    expert_sum = [last_sum] if first_sum is None else [first_sum, last_sum]
    expert_sum = jnp.concatenate(
        [item.astype(wide).reshape(3, unit, width) for item in expert_sum], axis=1
    )
    return (
        output,
        grad_tokens,
        small_sum[gain_rows[0]],
        query_own,
        small_sum[:latent_width].T,
        small_sum[gain_rows[2], :latent_shard],
        kvb_own,
        out_own,
        small_sum[gain_rows[1]],
        small_sum[router_first : router_first + expert_count].T,
        shared_sum[:, 0].reshape(sff, shard).T,
        shared_sum[:, 1].reshape(sff, shard).T,
        shared_sum[:, 2].reshape(sff, shard),
        expert_sum[0].T[None],
        expert_sum[1].T[None],
        expert_sum[2][None],
    )


def solution(mesh):
    in_specs = (
        P("fsdp", "tp", None),
        P("fsdp"),
        P("fsdp", None, None),
        P("fsdp", None, None),
        P("fsdp"),
        P("fsdp", "tp"),
        P("fsdp", None),
        P("fsdp"),
        P("fsdp", "tp"),
        P("tp", "fsdp"),
        P("fsdp"),
        P("fsdp", None),
        P("fsdp", "tp"),
        P("fsdp", "tp"),
        P("tp", "fsdp"),
        P("fsdp", None, "tp"),
        P("fsdp", None, "tp"),
        P("fsdp", "tp", None),
        P("fsdp", "tp", None),
    )
    out_specs = (
        P("fsdp", "tp", None),
        P("fsdp", "tp", None),
        P("fsdp"),
        P("fsdp", "tp"),
        P("fsdp", None),
        P("fsdp"),
        P("fsdp", "tp"),
        P("tp", "fsdp"),
        P("fsdp"),
        P("fsdp", None),
        P("fsdp", "tp"),
        P("fsdp", "tp"),
        P("tp", "fsdp"),
        P("fsdp", None, "tp"),
        P("fsdp", None, "tp"),
        P("fsdp", "tp", None),
    )
    return jax.shard_map(
        on_device, mesh=mesh, in_specs=in_specs, out_specs=out_specs, check_vma=False
    )
```

time: 3270 us -> 1300 us (0.40)
  waiting for transfers between devices: 1570 us -> 314 us
  matrix products: 691 us -> 100 us
  Pallas kernels: 0 us -> 559 us
  local copies, waits for them, and re-layouts: 483 us -> 98.6 us
  other arithmetic: 387 us -> 123 us
  blocking collectives: 81.6 us -> 0 us
  starting transfers between devices: 2.72 us -> 47.9 us
    reduce_scatter x15 -> x5, waiting for transfers between devices: 741 us -> 0.02 us  [the longest x1 0.01 us: scatter_tp(): lax.psum_scatter(placed, 'tp', scatter_dimension=0, tiled=True).astype(wide)]
    dot_general x77 -> x24, matrix products: 691 us -> 100 us  [dot(): lax.dot_general(a, b, (dims, ((), ())), preferred_element_type=wide)]
    all_gather x15 -> x5, waiting for transfers between devices: 566 us -> 0.08 us  [gather_fsdp(): return lax.all_gather(values, 'fsdp', axis=axis, tiled=True)]
    pallas_call x0 -> x18, Pallas kernels: none -> 559 us  [the longest x11 307 us: feed_forward(): pl.pallas_call(without(functools.partial(ffn_kernel, pieces), 2 * pieces...]
    ppermute x0 -> x42, waiting for transfers between devices: none -> 314 us  [the longest x18 216 us: hop(): lax.ppermute(values, 'tp', [(i, (i + 1) % count) for i in range(count)])]
    unnamed x33 -> x10, waiting for transfers between devices: 228 us -> 0.16 us
    scatter-add x2 -> x0, other arithmetic: 218 us -> none  [the longest x1 109 us: on_device(): grad_rows_acc.at[token_piece]]
    gather x3 -> x0, local copies, waits for them, and re-layouts: 209 us -> none  [the longest x1 75.8 us: on_device(): jnp.concatenate([grad_gate_slot, jnp.zeros((1,), wide_precision)])]
  transfers between devices with their start and end apart: 32 -> 52, of which waited for: 21 -> 16; matrix products, arithmetic and copies ran while one was open for 38% -> 23% of each run, Pallas kernels for 0% -> 40%
where the time goes in v1:
time: 1300 us; the launch traced here: 1290 us
  Pallas kernels  559 us (43%)
  waiting for transfers between devices  314 us (24%)
  other arithmetic  123 us (9%)
  matrix products  100 us (8%)
  local copies, waits for them, and re-layouts  98.6 us (8%)
  starting transfers between devices  47.9 us (4%)
  between operations  45.2 us (3%)
    pallas_call x11, Pallas kernels, feed_forward(): pl.pallas_call(without(functools.partial(ffn_kernel, pieces), 2 * pieces...  307 us
    ppermute x18, waiting for transfers between devices, hop(): lax.ppermute(values, 'tp', [(i, (i + 1) % count) for i in range(count)])  216 us
    pallas_call x3, Pallas kernels, weight_grads(): pl.pallas_call(without(functools.partial(weight_grad_kernel, pieces, join...  125 us
    dot_general x24, matrix products, dot(): lax.dot_general(a, b, (dims, ((), ())), preferred_element_type=wide)  100 us
    pallas_call x2, Pallas kernels, attend_back(): pl.pallas_call(without(attend_back_kernel, 13, waits), grid=(pairs, seqs)...  75.2 us
    ppermute x6, waiting for transfers between devices, cross_moves(): lax.ppermute(pieces[s].astype(narrow), 'tp', [(i, (i - s) % count) for i...  74.7 us
    pallas_call x1, Pallas kernels, attend(): pl.pallas_call(attend_kernel, grid=(pairs, seqs), in_specs=[pl.BlockSpec(...  38.9 us
    unnamed x403, local copies, waits for them, and re-layouts  37 us
  transfers between devices with their start and end apart: 52, of which 16 were waited for; matrix products, arithmetic and copies ran while one was open for 23% of the time, Pallas kernels for 40%

profile of v1, /device:TPU:0, one launch (start us, length us, event | category | flops | bytes accessed | tf_op | source)
XLA Modules:
  0.0 1288.3 jit_solution(3857499294245538768)
XLA Ops:
  14.9 19.5 %collective-permute-done = bf16[256,1536]{1,0:T(8,128)(2,1)S(1)} collective-permute-done((bf16[256,1536]{1,0:T(8,128)(2,1)S(1)}, bf16[256,1536]{1,0:T(8,128)(2,1)S(1)}, u32[]{:S(2)}, u32[]{:S(2)}) %collective-permute-start) | collective-permute-done | bytes 786464 | tf_op jit(solution)/shard_map/ppermute | solution.py:518
  35.3 19.6 %collective-permute-done.1 = bf16[256,1536]{1,0:T(8,128)(2,1)S(1)} collective-permute-done((bf16[256,1536]{1,0:T(8,128)(2,1)S(1)}, bf16[256,1536]{1,0:T(8,128)(2,1)S(1)}, u32[]{:S(2)}, u32[]{:S(2)}) %collective-permute-start.1) | collective-permute-done | bytes 786464 | tf_op jit(solution)/shard_map/ppermute | solution.py:518
  57.2 17.3 %collective-permute-done.2 = bf16[256,1536]{1,0:T(8,128)(2,1)S(1)} collective-permute-done((bf16[256,1536]{1,0:T(8,128)(2,1)S(1)}, bf16[256,1536]{1,0:T(8,128)(2,1)S(1)}, u32[]{:S(2)}, u32[]{:S(2)}) %collective-permute-start.2) | collective-permute-done | bytes 786464 | tf_op jit(solution)/shard_map/ppermute | solution.py:518
  102.7 11.0 collective-permute-done.3
  117.5 13.9 %collective-permute-done.4 = bf16[512,640]{1,0:T(8,128)(2,1)S(1)} collective-permute-done((bf16[512,640]{1,0:T(8,128)(2,1)S(1)}, bf16[512,640]{1,0:T(8,128)(2,1)S(1)}, u32[]{:S(2)}, u32[]{:S(2)}) %collective-permute-start.4) | collective-permute-done | bytes 655392 | tf_op jit(solution)/shard_map/ppermute | solution.py:518
  136.6 13.0 %collective-permute-done.5 = bf16[512,640]{1,0:T(8,128)(2,1)S(1)} collective-permute-done((bf16[512,640]{1,0:T(8,128)(2,1)S(1)}, bf16[512,640]{1,0:T(8,128)(2,1)S(1)}, u32[]{:S(2)}, u32[]{:S(2)}) %collective-permute-start.5) | collective-permute-done | bytes 655392 | tf_op jit(solution)/shard_map/ppermute | solution.py:518
  163.7 45.8 %collective-permute-done.7.refs_1_.refs_6_ = bf16[512,2048]{1,0:T(8,128)(2,1)} collective-permute-done((bf16[512,2048]{1,0:T(8,128)(2,1)}, bf16[512,2048]{1,0:T(8,128)(2,1)}, u32[]{:S(2)}, u32[]{:S(2)}) %collective-permute-start.7) | collective-permute-done | bytes 2097184 | tf_op jit(solution)/shard_map/ppermute | solution.py:518
  217.8 37.2 %collective-permute-done.10.refs_1_.refs_2_.refs_7_ = bf16[512,2048]{1,0:T(8,128)(2,1)} collective-permute-done((bf16[512,2048]{1,0:T(8,128)(2,1)}, bf16[512,2048]{1,0:T(8,128)(2,1)}, u32[]{:S(2)}, u32[]{:S(2)}) %collective-permute-start.10) | collective-permute-done | bytes 2097184 | tf_op jit(solution)/shard_map/ppermute | solution.py:518
  255.3 12.1 shard_map.306
  267.5 38.9 %shard_map.307 = (bf16[2,256,2048]{2,1,0:T(8,128)(2,1)S(1)}, f32[2,256,2048]{2,1,0:T(8,128)}, bf16[2,1024,4096]{2,1,0:T(8,128)(2,1)}) custom-call(bf16[2,256,2048]{2,1,0:T(8,128)(2,1)S(1)} %bitcast.362, bf16[2,256,1024]{2,1,0:T(8,128)(2,1)S(1)} %bitcast.365, bf16[2,1024,640]{2,1,0:T(8,128)(2,1)} %pad_maximum_fusion.1.latent.rope.refs_2_.refs_3_, ...), custom_call_target="tpu_custom_call" | custom-call | flops 15032385536 | bytes 16777216 | tf_op jit(solution)/shard_map/pallas_call | solution.py:178
  321.1 29.9 %shard_map.308 = (bf16[512,2048]{1,0:T(8,128)(2,1)}, bf16[512,2048]{1,0:T(8,128)(2,1)}, bf16[1,8,176,512]{3,2,1,0:T(8,128)(2,1)}, bf16[1,8,352,512]{3,2,1,0:T(8,128)(2,1)}, f32[1,8,1,512]{3,2,1,0:T(1,128)}) custom-call(bf16[512,2048]{1,0:T(8,128)(2,1)} %multiply_convert_fusion.1.refs_0_.refs_1_, bf16[512,2048]{1,0:T(8,128)(2,1)} %add_convert_fusion.19.refs_1_.refs_5_, ...), custom_call_target="tpu_custom_call" | custom-call | flops 17716740096 | bytes 25690112 | tf_op jit(solution)/shard_map/pallas_call | solution.py:406
  351.0 8.7 collective-permute-done.6.refs_0_.refs_2_
  363.4 30.1 %shard_map.309 = (bf16[512,2048]{1,0:T(8,128)(2,1)}, bf16[512,2048]{1,0:T(8,128)(2,1)}, bf16[1,8,176,512]{3,2,1,0:T(8,128)(2,1)}, bf16[1,8,352,512]{3,2,1,0:T(8,128)(2,1)}, f32[1,8,1,512]{3,2,1,0:T(1,128)}) custom-call(bf16[512,2048]{1,0:T(8,128)(2,1)} %collective-permute-done.6.refs_0_.refs_2_, bf16[512,2048]{1,0:T(8,128)(2,1)} %collective-permute-done.7.refs_1_.refs_6_, ...), custom_call_target="tpu_custom_call" | custom-call | flops 17716740096 | bytes 25690112 | tf_op jit(solution)/shard_map/pallas_call | solution.py:406
  394.1 16.4 %shard_map.310 = (bf16[512,2048]{1,0:T(8,128)(2,1)}, bf16[512,2048]{1,0:T(8,128)(2,1)}, bf16[1,4,176,512]{3,2,1,0:T(8,128)(2,1)}, bf16[1,4,352,512]{3,2,1,0:T(8,128)(2,1)}, f32[1,4,1,512]{3,2,1,0:T(1,128)}) custom-call(bf16[512,2048]{1,0:T(8,128)(2,1)} %multiply_convert_fusion.1.refs_0_.refs_1_, bf16[512,2048]{1,0:T(8,128)(2,1)} %add_convert_fusion.19.refs_1_.refs_5_, ...), custom_call_target="tpu_custom_call" | custom-call | flops 8858370048 | bytes 17039360 | tf_op jit(solution)/shard_map/pallas_call | solution.py:406
  416.6 16.4 %shard_map.311 = (bf16[512,2048]{1,0:T(8,128)(2,1)}, bf16[512,2048]{1,0:T(8,128)(2,1)}, bf16[1,4,176,512]{3,2,1,0:T(8,128)(2,1)}, bf16[1,4,352,512]{3,2,1,0:T(8,128)(2,1)}, f32[1,4,1,512]{3,2,1,0:T(1,128)}) custom-call(bf16[512,2048]{1,0:T(8,128)(2,1)} %collective-permute-done.6.refs_0_.refs_2_, bf16[512,2048]{1,0:T(8,128)(2,1)} %collective-permute-done.7.refs_1_.refs_6_, ...), custom_call_target="tpu_custom_call" | custom-call | flops 8858370048 | bytes 17039360 | tf_op jit(solution)/shard_map/pallas_call | solution.py:406
  433.1 30.0 %shard_map.312 = (bf16[512,2048]{1,0:T(8,128)(2,1)}, bf16[512,2048]{1,0:T(8,128)(2,1)}, bf16[1,8,176,512]{3,2,1,0:T(8,128)(2,1)}, bf16[1,8,352,512]{3,2,1,0:T(8,128)(2,1)}, f32[1,8,1,512]{3,2,1,0:T(1,128)}) custom-call(bf16[512,2048]{1,0:T(8,128)(2,1)} %collective-permute-done.8.refs_6_.refs_0_.refs_3_, ...), custom_call_target="tpu_custom_call" | custom-call | flops 17716740096 | bytes 25690112 | tf_op jit(solution)/shard_map/pallas_call | solution.py:406
  466.7 30.0 %shard_map.313 = (bf16[512,2048]{1,0:T(8,128)(2,1)}, bf16[512,2048]{1,0:T(8,128)(2,1)}, bf16[1,8,176,512]{3,2,1,0:T(8,128)(2,1)}, bf16[1,8,352,512]{3,2,1,0:T(8,128)(2,1)}, f32[1,8,1,512]{3,2,1,0:T(1,128)}) custom-call(bf16[512,2048]{1,0:T(8,128)(2,1)} %collective-permute-done.9.refs_0_.refs_1_.refs_4_, ...), custom_call_target="tpu_custom_call" | custom-call | flops 17716740096 | bytes 25690112 | tf_op jit(solution)/shard_map/pallas_call | solution.py:406
  497.3 31.0 %shard_map.314 = (bf16[512,2048]{1,0:T(8,128)(2,1)}, bf16[512,2048]{1,0:T(8,128)(2,1)}, bf16[512,2048]{1,0:T(8,128)(2,1)}, bf16[512,2048]{1,0:T(8,128)(2,1)}, bf...) custom-call(bf16[512,2048]{1,0:T(8,128)(2,1)} %collective-permute-done.8.refs_6_.refs_0_.r, ...), custom_call_target="tpu_custom_call" | custom-call | flops 17716740096 | bytes 34078720 | tf_op jit(solution)/shard_map/pallas_call | solution.py:406
  530.1 28.6 %shard_map.315.refs_25_ = bf16[4,528,2048]{2,1,0:T(8,128)(2,1)} custom-call(s32[4]{0:T(128)} %iota.47.refs_0_, bf16[512,2048]{1,0:T(8,128)(2,1)} %multiply_convert_fusion.1.refs_0_.refs_1_, bf16[512,2048]{1,0:T(8,128)(2,1)} %collective-permute-done.6.refs_0_.refs_2_, bf16[512,2048]{1,0:T(8,128)(2,1)} %collective-permute-done.8.refs_6_.refs_0_.refs_3_, ...), custom_call_target="tpu_custom_call" | custom-call | flops 17716740096 | bytes 34078720 | tf_op jit(solution)/shard_map/pallas_call | solution.py:472
  559.3 49.1 %shard_map.316.refs_5_ = bf16[8,528,2048]{2,1,0:T(8,128)(2,1)} custom-call(s32[8]{0:T(128)} %iota.46.refs_0_, bf16[512,2048]{1,0:T(8,128)(2,1)} %multiply_convert_fusion.1.refs_0_.refs_1_, bf16[512,2048]{1,0:T(8,128)(2,1)} %collective-permute-done.6.refs_0_.refs_2_, bf16[512,2048]{1,0:T(8,128)(2,1)} %collective-permute-done.8.refs_6_.refs_0_.refs_3_, ...), custom_call_target="tpu_custom_call" | custom-call | flops 35433480192 | bytes 51380224 | tf_op jit(solution)/shard_map/pallas_call | solution.py:472
  608.5 30.4 %shard_map.317 = (bf16[512,2048]{1,0:T(8,128)(2,1)}, bf16[512,2048]{1,0:T(8,128)(2,1)}, bf16[1,8,176,512]{3,2,1,0:T(8,128)(2,1)}, bf16[1,8,352,512]{3,2,1,0:T(8,128)(2,1)}, f32[1,8,1,512]{3,2,1,0:T(1,128)}) custom-call(bf16[512,2048]{1,0:T(8,128)(2,1)} %collective-permute-done.6.refs_0_.refs_2_, bf16[512,2048]{1,0:T(8,128)(2,1)} %collective-permute-done.7.refs_1_.refs_6_, ...), custom_call_target="tpu_custom_call" | custom-call | flops 17716740096 | bytes 25690112 | tf_op jit(solution)/shard_map/pallas_call | solution.py:406
  651.6 32.3 %shard_map.318 = (bf16[512,2048]{1,0:T(8,128)(2,1)}, bf16[512,2048]{1,0:T(8,128)(2,1)}, bf16[1,8,176,512]{3,2,1,0:T(8,128)(2,1)}, bf16[1,8,352,512]{3,2,1,0:T(8,128)(2,1)}, f32[1,8,1,512]{3,2,1,0:T(1,128)}) custom-call(bf16[512,2048]{1,0:T(8,128)(2,1)} %collective-permute-done.8.refs_6_.refs_0_.refs_3_, ...), custom_call_target="tpu_custom_call" | custom-call | flops 17716740096 | bytes 25690112 | tf_op jit(solution)/shard_map/pallas_call | solution.py:406
  689.5 30.6 %shard_map.319 = (bf16[512,2048]{1,0:T(8,128)(2,1)}, bf16[512,2048]{1,0:T(8,128)(2,1)}, bf16[1,8,176,512]{3,2,1,0:T(8,128)(2,1)}, bf16[1,8,352,512]{3,2,1,0:T(8,128)(2,1)}, f32[1,8,1,512]{3,2,1,0:T(1,128)}) custom-call(bf16[512,2048]{1,0:T(8,128)(2,1)} %collective-permute-done.9.refs_0_.refs_1_.refs_4_, ...), custom_call_target="tpu_custom_call" | custom-call | flops 17716740096 | bytes 25690112 | tf_op jit(solution)/shard_map/pallas_call | solution.py:406
  731.2 30.2 %shard_map.320 = (bf16[512,2048]{1,0:T(8,128)(2,1)}, bf16[512,2048]{1,0:T(8,128)(2,1)}, bf16[1,8,176,512]{3,2,1,0:T(8,128)(2,1)}, bf16[1,8,352,512]{3,2,1,0:T(8,128)(2,1)}, f32[1,8,1,512]{3,2,1,0:T(1,128)}) custom-call(bf16[512,2048]{1,0:T(8,128)(2,1)} %multiply_convert_fusion.1.refs_0_.refs_1_, bf16[512,2048]{1,0:T(8,128)(2,1)} %add_convert_fusion.19.refs_1_.refs_5_, ...), custom_call_target="tpu_custom_call" | custom-call | flops 17716740096 | bytes 25690112 | tf_op jit(solution)/shard_map/pallas_call | solution.py:406
  771.5 47.7 %shard_map.321 = bf16[8,528,2048]{2,1,0:T(8,128)(2,1)} custom-call(s32[8]{0:T(128)} %iota.48.refs_0_, bf16[512,2048]{1,0:T(8,128)(2,1)} %multiply_convert_fusion.1.refs_0_.refs_1_, bf16[512,2048]{1,0:T(8,128)(2,1)} %collective-permute-done.6.refs_0_.refs_2_, bf16[512,2048]{1,0:T(8,128)(2,1)} %collective-permute-done.8.refs_6_.refs_0_.refs_3_, ...), custom_call_target="tpu_custom_call" | custom-call | flops 35433480192 | bytes 51380224 | tf_op jit(solution)/shard_map/pallas_call | solution.py:472
  822.4 29.9 %collective-permute-done.14 = bf16[512,2048]{1,0:T(8,128)(2,1)} collective-permute-done((bf16[512,2048]{1,0:T(8,128)(2,1)}, bf16[512,2048]{1,0:T(8,128)(2,1)}, u32[]{:S(2)}, u32[]{:S(2)}) %collective-permute-start.14) | collective-permute-done | bytes 2097184 | tf_op jit(solution)/shard_map/ppermute | solution.py:518
  892.8 8.9 fusion.26
  917.5 37.8 %shard_map.322 = (bf16[2,256,1024]{2,1,0:T(8,128)(2,1)S(1)}, bf16[2,256,512]{2,1,0:T(8,128)(2,1)S(1)}, bf16[2,1024,640]{2,1,0:T(8,128)(2,1)}, f32[8,4,64,512]{3,2,1,0:T(8,128)}) custom-call(bf16[2,256,2048]{2,1,0:T(8,128)(2,1)S(1)} %bitcast.363, bf16[2,256,1024]{2,1,0:T(8,128)(2,1)S(1)} %bitcast.366, ...), custom_call_target="tpu_custom_call" | custom-call | flops 17179869184 | bytes 8388608 | tf_op jit(solution)/shard_map/pallas_call | solution.py:291
  984.9 37.4 %shard_map.323 = (bf16[2,256,1024]{2,1,0:T(8,128)(2,1)S(1)}, bf16[2,256,512]{2,1,0:T(8,128)(2,1)S(1)}, bf16[2,1024,640]{2,1,0:T(8,128)(2,1)}, f32[8,4,64,512]{3,2,1,0:T(8,128)}) custom-call(bf16[2,256,2048]{2,1,0:T(8,128)(2,1)S(1)} %bitcast.364, bf16[2,256,1024]{2,1,0:T(8,128)(2,1)S(1)} %bitcast.367, ...), custom_call_target="tpu_custom_call" | custom-call | flops 17179869184 | bytes 8388608 | tf_op jit(solution)/shard_map/pallas_call | solution.py:291
  1091.1 14.4 %fusion = f32[512,2048]{1,0:T(8,128)} fusion(bf16[2048,6144]{1,0:T(8,128)(2,1)} %all-gather.8.cloned.1.call-done.weights, bf16[512,512]{1,0:T(8,128)(2,1)} %slice.591, bf16[512,512]{1,0:T(8,128)(2,1)} %slice.590, bf16[512,1024]{1,0:T(8,128)(2,1)} %slice.589, bf16[512,1024]{1,0:T(8,128)(2,1)} %slice.588, f32[]{:T(128)} %bitcast.123), kind=kOutput, calls=%fused_computation | convolution fusion | flops 6458179584 | bytes 19923456 | tf_op jit(solution)/shard_map/dot_general | solution.py:45
  1181.9 67.8 %collective-permute-done.35 = bf16[256,1024]{1,0:T(8,128)(2,1)S(1)} collective-permute-done((bf16[256,1024]{1,0:T(8,128)(2,1)S(1)}, bf16[256,1024]{1,0:T(8,128)(2,1)S(1)}, u32[]{:S(2)}, u32[]{:S(2)}) %collective-permute-start.35) | collective-permute-done | bytes 524320 | tf_op jit(solution)/shard_map/ppermute | solution.py:557
  1262.4 8.3 multiply_convert_fusion
  (713 shorter events, 369.2 us)
Async XLA Ops:
  7.2 81.9 %all-gather.6.cloned.1.call-start = ((), (), s32[]{:S(2)}) async-start(), calls=%async_computation.5 | async-start | bytes 2801664 | tf_op jit(solution)/shard_map/all_gather | solution.py:581
  35.3 220.0 %all-gather.8.cloned.1.call-start = ((), (), s32[]{:S(2)}) async-start(), calls=%async_computation.6 | async-start | bytes 28311552 | tf_op jit(solution)/shard_map/all_gather | solution.py:581
  86.6 234.5 %all-gather.12.cloned.1.call-start = ((), (), s32[]{:S(2)}) async-start(), calls=%async_computation.8 | async-start | bytes 19464192 | tf_op jit(solution)/shard_map/all_gather | solution.py:581
  117.3 276.1 %all-gather.10.cloned.1.call-start = ((), (), s32[]{:S(2)}) async-start(), calls=%async_computation.7 | async-start | bytes 9732096 | tf_op jit(solution)/shard_map/all_gather | solution.py:581
  136.5 472.0 %all-gather.14.cloned.1.call-start = ((), (), s32[]{:S(2)}) async-start(), calls=%async_computation.9 | async-start | bytes 19464192 | tf_op jit(solution)/shard_map/all_gather | solution.py:581
  155.7 533.8 %reduce-scatter.6.cloned.1.call-start = ((), (), s32[]{:S(2)}) async-start(), calls=%async_computation.10 | async-start | bytes 9732096 | tf_op jit(solution)/shard_map/reduce_scatter | solution.py:585
  163.7 45.8 %collective-permute-start.7 = (bf16[512,2048]{1,0:T(8,128)(2,1)}, bf16[512,2048]{1,0:T(8,128)(2,1)}, u32[]{:S(2)}, u32[]{:S(2)}) collective-permute-start(bf16[512,2048]{1,0:T(8,128)(2,1)} %add_convert_fusion.19.refs_1_.refs_5_), channel_id=1, source_target_pairs={{0,1},{1,2},{2,3},{3,0},{4,5},{5,6},{6,7},{7,4},{8,9},{9,10},{10,1... | collective-permute-start | bytes 6291464 | tf_op jit(solution)/shard_map/ppermute | solution.py:518
  209.5 45.5 %collective-permute-start.10 = (bf16[512,2048]{1,0:T(8,128)(2,1)}, bf16[512,2048]{1,0:T(8,128)(2,1)}, u32[]{:S(2)}, u32[]{:S(2)}) collective-permute-start(bf16[512,2048]{1,0:T(8,128)(2,1)} %collective-permute-done.7.refs_1_.refs_6_), channel_id=1, source_target_pairs={{0,1},{1,2},{2,3},{3,0},{4,5},{5,6},{6,7},{7,4},{8,9},{9,10},{10,1... | collective-permute-start | bytes 6291464 | tf_op jit(solution)/shard_map/ppermute | solution.py:518
  255.0 211.7 %collective-permute-start.11 = (bf16[512,2048]{1,0:T(8,128)(2,1)}, bf16[512,2048]{1,0:T(8,128)(2,1)}, u32[]{:S(2)}, u32[]{:S(2)}) collective-permute-start(bf16[512,2048]{1,0:T(8,128)(2,1)} %collective-permute-done.10.refs_1_.refs_2_.refs_7_), channel_id=1, source_target_pairs={{0,1},{1,2},{2,3},{3,0},{4,5},{5,6},{6,7},{7,4},{8,9},{9,10},{10,1... | collective-permute-start | bytes 6291464 | tf_op jit(solution)/shard_map/ppermute | solution.py:518
  317.0 42.6 %collective-permute-start.6 = (bf16[512,2048]{1,0:T(8,128)(2,1)}, bf16[512,2048]{1,0:T(8,128)(2,1)}, u32[]{:S(2)}, u32[]{:S(2)}) collective-permute-start(bf16[512,2048]{1,0:T(8,128)(2,1)} %multiply_convert_fusion.1.refs_0_.refs_1_), channel_id=1, source_target_pairs={{0,1},{1,2},{2,3},{3,0},{4,5},{5,6},{6,7},{7,4},{8,9},{9,10},{10,1... | collective-permute-start | bytes 6291464 | tf_op jit(solution)/shard_map/ppermute | solution.py:518
  363.2 47.3 %collective-permute-start.8 = (bf16[512,2048]{1,0:T(8,128)(2,1)}, bf16[512,2048]{1,0:T(8,128)(2,1)}, u32[]{:S(2)}, u32[]{:S(2)}) collective-permute-start(bf16[512,2048]{1,0:T(8,128)(2,1)} %collective-permute-done.6.refs_0_.refs_2_), channel_id=1, source_target_pairs={{0,1},{1,2},{2,3},{3,0},{4,5},{5,6},{6,7},{7,4},{8,9},{9,10},{10,1... | collective-permute-start | bytes 6291464 | tf_op jit(solution)/shard_map/ppermute | solution.py:518
  414.0 49.1 %collective-permute-start.9 = (bf16[512,2048]{1,0:T(8,128)(2,1)}, bf16[512,2048]{1,0:T(8,128)(2,1)}, u32[]{:S(2)}, u32[]{:S(2)}) collective-permute-start(bf16[512,2048]{1,0:T(8,128)(2,1)} %collective-permute-done.8.refs_6_.refs_0_.refs_3_), channel_id=1, source_target_pairs={{0,1},{1,2},{2,3},{3,0},{4,5},{5,6},{6,7},{7,4},{8,9},{9,10},{10,1... | collective-permute-start | bytes 6291464 | tf_op jit(solution)/shard_map/ppermute | solution.py:518
  558.7 212.2 %reduce-scatter.8.cloned.1.call-start = ((), (), s32[]{:S(2)}) async-start(), calls=%async_computation.11 | async-start | bytes 19464192 | tf_op jit(solution)/shard_map/reduce_scatter | solution.py:585
  608.4 374.0 %reduce-scatter.10.cloned.1.call-start = ((), (), s32[]{:S(2)}) async-start(), calls=%async_computation.12 | async-start | bytes 19464192 | tf_op jit(solution)/shard_map/reduce_scatter | solution.py:585
  647.3 75.2 %collective-permute-start.12 = (bf16[512,2048]{1,0:T(8,128)(2,1)}, bf16[512,2048]{1,0:T(8,128)(2,1)}, u32[]{:S(2)}, u32[]{:S(2)}) collective-permute-start(bf16[512,2048]{1,0:T(8,128)(2,1)} %add_convert_fusion.17.refs_6_), channel_id=1, source_target_pairs={{0,1},{1,2},{2,3},{3,0},{4,5},{5,6},{6,7},{7,4},{8,9},{9,10},{10,1... | collective-permute-start | bytes 6291464 | tf_op jit(solution)/shard_map/ppermute | solution.py:518
  819.2 311.2 %reduce-scatter.12.cloned.1.call-start = ((), (), s32[]{:S(2)}) async-start(), calls=%async_computation.13 | async-start | bytes 3276800 | tf_op jit(solution)/shard_map/reduce_scatter | solution.py:551
  907.7 69.0 %collective-permute-start.15 = (bf16[512,2048]{1,0:T(8,128)(2,1)}, bf16[512,2048]{1,0:T(8,128)(2,1)}, u32[]{:S(2)}, u32[]{:S(2)}) collective-permute-start(bf16[512,2048]{1,0:T(8,128)(2,1)} %add_convert_fusion.14), channel_id=1, source_target_pairs={{0,1},{1,2},{2,3},{3,0},{4,5},{5,6},{6,7},{7,4},{8,9},{9,10},{10,1... | collective-permute-start | bytes 6291464 | tf_op jit(solution)/shard_map/ppermute | solution.py:518
  914.0 55.0 %collective-permute-start.17 = (bf16[2,128,2048]{2,1,0:T(8,128)(2,1)}, bf16[2,128,2048]{2,1,0:T(8,128)(2,1)}, u32[]{:S(2)}, u32[]{:S(2)}) collective-permute-start(bf16[2,128,2048]{2,1,0:T(8,128)(2,1)} %get-tuple-element.245), channel_id=1, source_target_pairs={{0,8},{4,12},{8,0},{12,4},{16,24},{20,28},{24,16},{28,20},{1,9},{5... | collective-permute-start | bytes 3145736 | tf_op jit(solution)/shard_map/ppermute | solution.py:577
  915.2 53.8 %collective-permute-start.37 = (bf16[2,128,2048]{2,1,0:T(8,128)(2,1)}, bf16[2,128,2048]{2,1,0:T(8,128)(2,1)}, u32[]{:S(2)}, u32[]{:S(2)}) collective-permute-start(bf16[2,128,2048]{2,1,0:T(8,128)(2,1)} %get-tuple-element.244), channel_id=1, source_target_pairs={{0,16},{4,20},{8,24},{12,28},{16,0},{20,4},{24,8},{28,12},{1,17},{... | collective-permute-start | bytes 3145736 | tf_op jit(solution)/shard_map/ppermute | solution.py:577
  962.0 66.9 %collective-permute-start.20 = (bf16[4,256,2048]{2,1,0:T(8,128)(2,1)}, bf16[4,256,2048]{2,1,0:T(8,128)(2,1)}, u32[]{:S(2)}, u32[]{:S(2)}) collective-permute-start(bf16[4,256,2048]{2,1,0:T(8,128)(2,1)} %maximum_maximum_fusion.1), channel_id=1, source_target_pairs={{0,4},{4,0},{8,12},{12,8},{16,20},{20,16},{24,28},{28,24},{1,5},{5... | collective-permute-start | bytes 12582920 | tf_op jit(solution)/shard_map/ppermute | solution.py:577
  973.1 59.4 %collective-permute-start.21 = (bf16[128,2048]{1,0:T(8,128)(2,1)}, bf16[128,2048]{1,0:T(8,128)(2,1)}, u32[]{:S(2)}, u32[]{:S(2)}) collective-permute-start(bf16[128,2048]{1,0:T(8,128)(2,1)} %get-tuple-element.243.refs_14_), channel_id=1, source_target_pairs={{0,16},{4,20},{8,24},{12,28},{16,0},{20,4},{24,8},{28,12},{1,17},{... | collective-permute-start | bytes 1572872 | tf_op jit(solution)/shard_map/ppermute | solution.py:577
  975.9 56.6 %collective-permute-start.38 = (bf16[128,2048]{1,0:T(8,128)(2,1)}, bf16[128,2048]{1,0:T(8,128)(2,1)}, u32[]{:S(2)}, u32[]{:S(2)}) collective-permute-start(bf16[128,2048]{1,0:T(8,128)(2,1)} %get-tuple-element.242), channel_id=1, source_target_pairs={{0,8},{4,12},{8,0},{12,4},{16,24},{20,28},{24,16},{28,20},{1,9},{5... | collective-permute-start | bytes 1572872 | tf_op jit(solution)/shard_map/ppermute | solution.py:577
  981.6 180.3 %collective-permute-start.18 = (bf16[512,2048]{1,0:T(8,128)(2,1)}, bf16[512,2048]{1,0:T(8,128)(2,1)}, u32[]{:S(2)}, u32[]{:S(2)}) collective-permute-start(bf16[512,2048]{1,0:T(8,128)(2,1)} %add_convert_fusion.10.refs_13_), channel_id=1, source_target_pairs={{0,1},{1,2},{2,3},{3,0},{4,5},{5,6},{6,7},{7,4},{8,9},{9,10},{10,1... | collective-permute-start | bytes 6291464 | tf_op jit(solution)/shard_map/ppermute | solution.py:518
  1028.9 54.3 %collective-permute-start.19 = (bf16[4,256,2048]{2,1,0:T(8,128)(2,1)}, bf16[4,256,2048]{2,1,0:T(8,128)(2,1)}, u32[]{:S(2)}, u32[]{:S(2)}) collective-permute-start(bf16[4,256,2048]{2,1,0:T(8,128)(2,1)} %maximum_maximum_fusion), channel_id=1, source_target_pairs={{0,4},{4,0},{8,12},{12,8},{16,20},{20,16},{24,28},{28,24},{1,5},{5... | collective-permute-start | bytes 12582920 | tf_op jit(solution)/shard_map/ppermute | solution.py:577
  1040.0 37.7 %collective-permute-start.40 = (bf16[256,512]{1,0:T(8,128)(2,1)}, bf16[256,512]{1,0:T(8,128)(2,1)}, u32[]{:S(2)}, u32[]{:S(2)}) collective-permute-start(bf16[256,512]{1,0:T(8,128)(2,1)} %get-tuple-element.314), channel_id=1, source_target_pairs={{0,2},{1,3},{2,0},{3,1},{4,6},{5,7},{6,4},{7,5},{8,10},{9,11},{10,... | collective-permute-start | bytes 786440 | tf_op jit(solution)/shard_map/ppermute | solution.py:557
  1040.4 38.7 %collective-permute-start.41 = (bf16[256,512]{1,0:T(8,128)(2,1)S(1)}, bf16[256,512]{1,0:T(8,128)(2,1)}, u32[]{:S(2)}, u32[]{:S(2)}) collective-permute-start(bf16[256,512]{1,0:T(8,128)(2,1)S(1)} %get-tuple-element.313), channel_id=1, source_target_pairs={{0,1},{1,2},{2,3},{3,0},{4,5},{5,6},{6,7},{7,4},{8,9},{9,10},{10,1... | collective-permute-start | bytes 786440 | tf_op jit(solution)/shard_map/ppermute | solution.py:557
  1051.2 202.3 %reduce-scatter.14.cloned.1.call-start = ((), (), s32[]{:S(2)}) async-start(), calls=%async_computation.14 | async-start | bytes 2801664 | tf_op jit(solution)/shard_map/reduce_scatter | solution.py:585
  1069.6 38.4 %collective-permute-start.27 = (bf16[2,128,2048]{2,1,0:T(8,128)(2,1)}, bf16[2,128,2048]{2,1,0:T(8,128)(2,1)}, u32[]{:S(2)}, u32[]{:S(2)}) collective-permute-start(bf16[2,128,2048]{2,1,0:T(8,128)(2,1)} %get-tuple-element.257), channel_id=1, source_target_pairs={{0,8},{4,12},{8,0},{12,4},{16,24},{20,28},{24,16},{28,20},{1,9},{5... | collective-permute-start | bytes 3145736 | tf_op jit(solution)/shard_map/ppermute | solution.py:577
  1128.7 53.2 %collective-permute-start.31 = (bf16[256,1024]{1,0:T(8,128)(2,1)}, bf16[256,1024]{1,0:T(8,128)(2,1)}, u32[]{:S(2)}, u32[]{:S(2)}) collective-permute-start(bf16[256,1024]{1,0:T(8,128)(2,1)} %pad_maximum_fusion.9), channel_id=1, source_target_pairs={{0,3},{1,0},{2,1},{3,2},{4,7},{5,4},{6,5},{7,6},{8,11},{9,8},{10,9... | collective-permute-start | bytes 1572872 | tf_op jit(solution)/shard_map/ppermute | solution.py:557
  1168.9 93.5 %collective-permute-start.23 = (bf16[512,2048]{1,0:T(8,128)(2,1)}, bf16[512,2048]{1,0:T(8,128)(2,1)}, u32[]{:S(2)}, u32[]{:S(2)}) collective-permute-start(bf16[512,2048]{1,0:T(8,128)(2,1)} %add_convert_fusion.7), channel_id=1, source_target_pairs={{0,1},{1,2},{2,3},{3,0},{4,5},{5,6},{6,7},{7,4},{8,9},{9,10},{10,1... | collective-permute-start | bytes 6291464 | tf_op jit(solution)/shard_map/ppermute | solution.py:518
  1176.6 73.2 %collective-permute-start.35 = (bf16[256,1024]{1,0:T(8,128)(2,1)S(1)}, bf16[256,1024]{1,0:T(8,128)(2,1)S(1)}, u32[]{:S(2)}, u32[]{:S(2)}) collective-permute-start(bf16[256,1024]{1,0:T(8,128)(2,1)S(1)} %pad_maximum_fusion.10), channel_id=1, source_target_pairs={{0,2},{1,3},{2,0},{3,1},{4,6},{5,7},{6,4},{7,5},{8,10},{9,11},{10,... | collective-permute-start | bytes 1572872 | tf_op jit(solution)/shard_map/ppermute | solution.py:557
  1178.7 71.0 %collective-permute-start.36 = (bf16[256,1024]{1,0:T(8,128)(2,1)S(1)}, bf16[256,1024]{1,0:T(8,128)(2,1)S(1)}, u32[]{:S(2)}, u32[]{:S(2)}) collective-permute-start(bf16[256,1024]{1,0:T(8,128)(2,1)S(1)} %pad_maximum_fusion.11), channel_id=1, source_target_pairs={{0,1},{1,2},{2,3},{3,0},{4,5},{5,6},{6,7},{7,4},{8,9},{9,10},{10,1... | collective-permute-start | bytes 1572872 | tf_op jit(solution)/shard_map/ppermute | solution.py:557
  (201 other events, 3363.1 us)
Sparse Core Ops, SparseCore 0:
  35.4 31.2 all-gather.5
  86.8 123.0 all-gather.7
  212.3 92.0 all-gather.11
  306.7 57.1 all-gather.9
  365.6 92.0 all-gather.13
  558.8 72.8 reduce-scatter.5
  635.8 118.5 reduce-scatter.7
  819.4 139.6 reduce-scatter.9
  1051.3 56.3 reduce-scatter.11
  1160.7 46.7 reduce-scatter.13

commit v2 on v1

--- a/solution.py
+++ b/solution.py
@@ -954,10 +954,15 @@
     for k, s in enumerate(last_order):
         if k == 2:
             previous.append(shared_sum)
+            branch_total = after(pieces[last_order[0]][0], *previous)
+            previous.append(branch_total)
         if k == tp_count - 1:
             pieces[last_order[1]] = finish_piece(last_order[1], *previous)
             total = (hop(total).astype(wide) + pieces[last_order[1]][1]).astype(narrow)
-            previous.append(total)
+            branch_total = (
+                hop(branch_total).astype(wide) + after(pieces[last_order[1]][0], total)
+            ).astype(narrow)
+            previous += [total, branch_total]
         run(split, [s])
         if k == 0:
             pieces[s] = finish_piece(s)
@@ -977,10 +982,9 @@
     grad_hnorm, grad_ffn_gain = hidden_back(grad_hidden_own)
     grad_hidden = grad_out + grad_hnorm
     grad_attn = grad_hidden.astype(narrow)
-    branch_total = after(pieces[last_order[0]][0], grad_attn)
+    branch_total = after(branch_total, grad_attn)
     out_scatter, make_out = scatter_product(grad_attn, mixed)
-    grad_mixed = dot(after(grad_attn, out_scatter.sent), output_whole, NN, narrow)
-    out_scatter.join(make_out, grad_mixed)
+    grad_mixed = dot(grad_attn, output_whole, NN, narrow)
 
     def back(first, pairs, rows, latents_before, waits):
         return attend_back(
@@ -991,19 +995,20 @@
 
     pairs_half = HEAD_COUNT // 4
     first_qn, first_qr, first_latents, first_kvb = back(
-        0, pairs_half, grad_mixed, jnp.zeros_like(latent_all), [out_scatter.part]
+        0, pairs_half, grad_mixed, jnp.zeros_like(latent_all), [out_scatter.sent, branch_total]
     )
     first_query = jnp.concatenate([first_qn, first_qr], axis=-1).reshape(own_rows, -1)
     first_scatter, make_first_query = scatter_product(
         normed, first_query, first_kvb.reshape(width, -1)
     )
-    out_scatter.turn(first_scatter.sent)
-    branch_total = (
-        hop(branch_total).astype(wide) + after(pieces[2][0], out_scatter.turned)
-    ).astype(narrow)
+    out_scatter.join(make_out, first_scatter.sent)
+    for s in last_order[2:-1]:
+        branch_total = (
+            hop(branch_total).astype(wide) + after(pieces[s][0], out_scatter.part)
+        ).astype(narrow)
     second_qn, second_qr, grad_latent_all, second_kvb = back(
         pairs_half, pairs_half, grad_mixed, first_latents,
-        [branch_total, out_scatter.turned, last_sum],
+        [branch_total, out_scatter.part, last_sum],
     )
 
     grad_latent_sum = scatter_tp(grad_latent_all, 1, own_rows)
@@ -1011,10 +1016,14 @@
     second_scatter, make_second_query = scatter_product(
         normed, second_query, second_kvb.reshape(width, -1)
     )
-    out_sum = out_scatter.end(second_scatter.sent)
-    first_scatter.join(make_first_query, out_sum)
+    out_scatter.turn(second_scatter.sent)
+    branch_moved = hop(branch_total)
+    first_scatter.join(make_first_query, out_scatter.turned, branch_moved)
     second_scatter.join(make_second_query, first_scatter.part)
     half_plain, half_turned = first_qn.shape[2], first_qr.shape[2]
+    router_gradient = sum(
+        dot(after(pieces[s][2], second_scatter.part), hidden_pieces[s], NN) for s in chunks
+    )
     query_gradient = jnp.concatenate(
         [
             first_query[:, :half_plain],
@@ -1024,7 +1033,7 @@
         ],
         axis=1,
     )
-    grad_normed = dot(after(query_gradient, second_scatter.part), query_whole, NT)
+    grad_normed = dot(after(query_gradient, second_scatter.part, grad_latent_sum), query_whole, NT)
     first_scatter.turn(grad_normed)
 
     latent_back = jax.vjp(normalize, compressed, latent_scale)[1]
@@ -1042,7 +1051,6 @@
     grad_tnorm, grad_attn_gain = token_back(grad_normed)
     grad_tokens = (grad_hidden + grad_tnorm).astype(narrow).reshape(tokens.shape)
 
-    router_gradient = sum(dot(pieces[s][2], hidden_pieces[s], NN) for s in chunks)
 
     small_grads = small_stack(
         latent_key_gradient,
@@ -1056,11 +1064,8 @@
     )
     small_sum = cross_sum(scatter_fsdp(small_grads, 1))
     second_scatter.turn(small_grads)
-    for s in chunks[3:]:
-        branch_total = (
-            hop(branch_total).astype(wide) + after(pieces[s][0], second_scatter.turned)
-        ).astype(narrow)
-
+
+    out_sum = out_scatter.end(small_grads)
     first_own = first_scatter.end()
     second_own = second_scatter.end()
     half_query = half_plain + half_turned
@@ -1079,7 +1084,7 @@
 
     out_own = cross_scatter(jnp.split(out_sum, tp_count, axis=1)).T
     query_own = cross_scatter([query_piece(s) for s in chunks])
-    branch_own = hop(branch_total).astype(wide) + pieces[0][0]
+    branch_own = branch_moved.astype(wide) + after(pieces[0][0], small_grads)
     output = (live_mask * (hidden + branch_own)).astype(narrow).reshape(tokens.shape)
     kvb_own = jnp.concatenate(jnp.split(query_own[:, query_cols:], quarters, axis=0), axis=1)
     query_own = jnp.concatenate(

time: 1300 us -> 1260 us (0.969)
  waiting for transfers between devices: 314 us -> 266 us
    ppermute x6, waiting for transfers between devices: 74.7 us -> 28.8 us  [cross_moves(): lax.ppermute(pieces[s].astype(narrow), 'tp', [(i, (i - s) % count) for i...]
    unnamed x403 -> x407, local copies, waits for them, and re-layouts: 37 us -> 42 us
  transfers between devices with their start and end apart: 52 -> 52, of which waited for: 16 -> 17; matrix products, arithmetic and copies ran while one was open for 23% -> 24% of each run, Pallas kernels for 40% -> 41%
where the time goes in v2:
time: 1260 us; the launch traced here: 1240 us
  Pallas kernels  559 us (44%)
  waiting for transfers between devices  266 us (21%)
  other arithmetic  125 us (10%)
  local copies, waits for them, and re-layouts  107 us (8%)
  matrix products  100 us (8%)
  between operations  47.6 us (4%)
  starting transfers between devices  38.3 us (3%)
    pallas_call x11, Pallas kernels, feed_forward(): pl.pallas_call(without(functools.partial(ffn_kernel, pieces), 2 * pieces...  307 us
    ppermute x18, waiting for transfers between devices, hop(): lax.ppermute(values, 'tp', [(i, (i + 1) % count) for i in range(count)])  204 us
    pallas_call x3, Pallas kernels, weight_grads(): pl.pallas_call(without(functools.partial(weight_grad_kernel, pieces, join...  125 us
    dot_general x24, matrix products, dot(): lax.dot_general(a, b, (dims, ((), ())), preferred_element_type=wide)  100 us
    pallas_call x2, Pallas kernels, attend_back(): pl.pallas_call(without(attend_back_kernel, 13, waits), grid=(pairs, seqs)...  74.6 us
    unnamed x407, local copies, waits for them, and re-layouts  42 us
    pallas_call x1, Pallas kernels, attend(): pl.pallas_call(attend_kernel, grid=(pairs, seqs), in_specs=[pl.BlockSpec(...  39 us
    ppermute x6, waiting for transfers between devices, cross_moves(): lax.ppermute(pieces[s].astype(narrow), 'tp', [(i, (i - s) % count) for i...  28.8 us
  transfers between devices with their start and end apart: 52, of which 17 were waited for; matrix products, arithmetic and copies ran while one was open for 24% of the time, Pallas kernels for 41%

profile of v2, /device:TPU:0, one launch (start us, length us, event | category | flops | bytes accessed | tf_op | source)
XLA Modules:
  0.0 1243.0 jit_solution(11202090859152176558)
XLA Ops:
  14.9 19.5 %collective-permute-done = bf16[256,1536]{1,0:T(8,128)(2,1)S(1)} collective-permute-done((bf16[256,1536]{1,0:T(8,128)(2,1)S(1)}, bf16[256,1536]{1,0:T(8,128)(2,1)S(1)}, u32[]{:S(2)}, u32[]{:S(2)}) %collective-permute-start) | collective-permute-done | bytes 786464 | tf_op jit(solution)/shard_map/ppermute | solution.py:518
  35.3 19.6 %collective-permute-done.1 = bf16[256,1536]{1,0:T(8,128)(2,1)S(1)} collective-permute-done((bf16[256,1536]{1,0:T(8,128)(2,1)S(1)}, bf16[256,1536]{1,0:T(8,128)(2,1)S(1)}, u32[]{:S(2)}, u32[]{:S(2)}) %collective-permute-start.1) | collective-permute-done | bytes 786464 | tf_op jit(solution)/shard_map/ppermute | solution.py:518
  57.2 17.3 %collective-permute-done.2 = bf16[256,1536]{1,0:T(8,128)(2,1)S(1)} collective-permute-done((bf16[256,1536]{1,0:T(8,128)(2,1)S(1)}, bf16[256,1536]{1,0:T(8,128)(2,1)S(1)}, u32[]{:S(2)}, u32[]{:S(2)}) %collective-permute-start.2) | collective-permute-done | bytes 786464 | tf_op jit(solution)/shard_map/ppermute | solution.py:518
  102.7 11.0 collective-permute-done.3
  117.5 13.9 %collective-permute-done.4 = bf16[512,640]{1,0:T(8,128)(2,1)S(1)} collective-permute-done((bf16[512,640]{1,0:T(8,128)(2,1)S(1)}, bf16[512,640]{1,0:T(8,128)(2,1)S(1)}, u32[]{:S(2)}, u32[]{:S(2)}) %collective-permute-start.4) | collective-permute-done | bytes 655392 | tf_op jit(solution)/shard_map/ppermute | solution.py:518
  136.6 13.0 %collective-permute-done.5 = bf16[512,640]{1,0:T(8,128)(2,1)S(1)} collective-permute-done((bf16[512,640]{1,0:T(8,128)(2,1)S(1)}, bf16[512,640]{1,0:T(8,128)(2,1)S(1)}, u32[]{:S(2)}, u32[]{:S(2)}) %collective-permute-start.5) | collective-permute-done | bytes 655392 | tf_op jit(solution)/shard_map/ppermute | solution.py:518
  163.7 45.8 %collective-permute-done.7.refs_1_.refs_6_ = bf16[512,2048]{1,0:T(8,128)(2,1)} collective-permute-done((bf16[512,2048]{1,0:T(8,128)(2,1)}, bf16[512,2048]{1,0:T(8,128)(2,1)}, u32[]{:S(2)}, u32[]{:S(2)}) %collective-permute-start.7) | collective-permute-done | bytes 2097184 | tf_op jit(solution)/shard_map/ppermute | solution.py:518
  217.8 37.2 %collective-permute-done.10.refs_1_.refs_2_.refs_7_ = bf16[512,2048]{1,0:T(8,128)(2,1)} collective-permute-done((bf16[512,2048]{1,0:T(8,128)(2,1)}, bf16[512,2048]{1,0:T(8,128)(2,1)}, u32[]{:S(2)}, u32[]{:S(2)}) %collective-permute-start.10) | collective-permute-done | bytes 2097184 | tf_op jit(solution)/shard_map/ppermute | solution.py:518
  255.3 12.1 shard_map.306
  267.5 39.0 %shard_map.307 = (bf16[2,256,2048]{2,1,0:T(8,128)(2,1)S(1)}, f32[2,256,2048]{2,1,0:T(8,128)}, bf16[2,1024,4096]{2,1,0:T(8,128)(2,1)}) custom-call(bf16[2,256,2048]{2,1,0:T(8,128)(2,1)S(1)} %bitcast.360, bf16[2,256,1024]{2,1,0:T(8,128)(2,1)S(1)} %bitcast.363, bf16[2,1024,640]{2,1,0:T(8,128)(2,1)} %pad_maximum_fusion.1.latent.rope.refs_2_.refs_3_, ...), custom_call_target="tpu_custom_call" | custom-call | flops 15032385536 | bytes 16777216 | tf_op jit(solution)/shard_map/pallas_call | solution.py:178
  321.3 29.9 %shard_map.308 = (bf16[512,2048]{1,0:T(8,128)(2,1)}, bf16[512,2048]{1,0:T(8,128)(2,1)}, bf16[1,8,176,512]{3,2,1,0:T(8,128)(2,1)}, bf16[1,8,352,512]{3,2,1,0:T(8,128)(2,1)}, f32[1,8,1,512]{3,2,1,0:T(1,128)}) custom-call(bf16[512,2048]{1,0:T(8,128)(2,1)} %multiply_convert_fusion.1.refs_0_.refs_1_, bf16[512,2048]{1,0:T(8,128)(2,1)} %add_convert_fusion.20.refs_1_.refs_5_, ...), custom_call_target="tpu_custom_call" | custom-call | flops 17716740096 | bytes 25690112 | tf_op jit(solution)/shard_map/pallas_call | solution.py:406
  363.5 30.1 %shard_map.309 = (bf16[512,2048]{1,0:T(8,128)(2,1)}, bf16[512,2048]{1,0:T(8,128)(2,1)}, bf16[1,8,176,512]{3,2,1,0:T(8,128)(2,1)}, bf16[1,8,352,512]{3,2,1,0:T(8,128)(2,1)}, f32[1,8,1,512]{3,2,1,0:T(1,128)}) custom-call(bf16[512,2048]{1,0:T(8,128)(2,1)} %collective-permute-done.6.refs_0_.refs_2_, bf16[512,2048]{1,0:T(8,128)(2,1)} %collective-permute-done.7.refs_1_.refs_6_, ...), custom_call_target="tpu_custom_call" | custom-call | flops 17716740096 | bytes 25690112 | tf_op jit(solution)/shard_map/pallas_call | solution.py:406
  394.2 16.4 %shard_map.310 = (bf16[512,2048]{1,0:T(8,128)(2,1)}, bf16[512,2048]{1,0:T(8,128)(2,1)}, bf16[1,4,176,512]{3,2,1,0:T(8,128)(2,1)}, bf16[1,4,352,512]{3,2,1,0:T(8,128)(2,1)}, f32[1,4,1,512]{3,2,1,0:T(1,128)}) custom-call(bf16[512,2048]{1,0:T(8,128)(2,1)} %multiply_convert_fusion.1.refs_0_.refs_1_, bf16[512,2048]{1,0:T(8,128)(2,1)} %add_convert_fusion.20.refs_1_.refs_5_, ...), custom_call_target="tpu_custom_call" | custom-call | flops 8858370048 | bytes 17039360 | tf_op jit(solution)/shard_map/pallas_call | solution.py:406
  416.8 16.4 %shard_map.311 = (bf16[512,2048]{1,0:T(8,128)(2,1)}, bf16[512,2048]{1,0:T(8,128)(2,1)}, bf16[1,4,176,512]{3,2,1,0:T(8,128)(2,1)}, bf16[1,4,352,512]{3,2,1,0:T(8,128)(2,1)}, f32[1,4,1,512]{3,2,1,0:T(1,128)}) custom-call(bf16[512,2048]{1,0:T(8,128)(2,1)} %collective-permute-done.6.refs_0_.refs_2_, bf16[512,2048]{1,0:T(8,128)(2,1)} %collective-permute-done.7.refs_1_.refs_6_, ...), custom_call_target="tpu_custom_call" | custom-call | flops 8858370048 | bytes 17039360 | tf_op jit(solution)/shard_map/pallas_call | solution.py:406
  433.2 30.1 %shard_map.312 = (bf16[512,2048]{1,0:T(8,128)(2,1)}, bf16[512,2048]{1,0:T(8,128)(2,1)}, bf16[1,8,176,512]{3,2,1,0:T(8,128)(2,1)}, bf16[1,8,352,512]{3,2,1,0:T(8,128)(2,1)}, f32[1,8,1,512]{3,2,1,0:T(1,128)}) custom-call(bf16[512,2048]{1,0:T(8,128)(2,1)} %collective-permute-done.8.refs_6_.refs_0_.refs_3_, ...), custom_call_target="tpu_custom_call" | custom-call | flops 17716740096 | bytes 25690112 | tf_op jit(solution)/shard_map/pallas_call | solution.py:406
  466.8 30.0 %shard_map.313 = (bf16[512,2048]{1,0:T(8,128)(2,1)}, bf16[512,2048]{1,0:T(8,128)(2,1)}, bf16[1,8,176,512]{3,2,1,0:T(8,128)(2,1)}, bf16[1,8,352,512]{3,2,1,0:T(8,128)(2,1)}, f32[1,8,1,512]{3,2,1,0:T(1,128)}) custom-call(bf16[512,2048]{1,0:T(8,128)(2,1)} %collective-permute-done.9.refs_0_.refs_1_.refs_4_, ...), custom_call_target="tpu_custom_call" | custom-call | flops 17716740096 | bytes 25690112 | tf_op jit(solution)/shard_map/pallas_call | solution.py:406
  497.4 31.0 %shard_map.314 = (bf16[512,2048]{1,0:T(8,128)(2,1)}, bf16[512,2048]{1,0:T(8,128)(2,1)}, bf16[512,2048]{1,0:T(8,128)(2,1)}, bf16[512,2048]{1,0:T(8,128)(2,1)}, bf...) custom-call(bf16[512,2048]{1,0:T(8,128)(2,1)} %collective-permute-done.8.refs_6_.refs_0_.r, ...), custom_call_target="tpu_custom_call" | custom-call | flops 17716740096 | bytes 34078720 | tf_op jit(solution)/shard_map/pallas_call | solution.py:406
  530.2 28.6 %shard_map.315.refs_25_ = bf16[4,528,2048]{2,1,0:T(8,128)(2,1)} custom-call(s32[4]{0:T(128)} %iota.47.refs_0_, bf16[512,2048]{1,0:T(8,128)(2,1)} %multiply_convert_fusion.1.refs_0_.refs_1_, bf16[512,2048]{1,0:T(8,128)(2,1)} %collective-permute-done.6.refs_0_.refs_2_, bf16[512,2048]{1,0:T(8,128)(2,1)} %collective-permute-done.8.refs_6_.refs_0_.refs_3_, ...), custom_call_target="tpu_custom_call" | custom-call | flops 17716740096 | bytes 34078720 | tf_op jit(solution)/shard_map/pallas_call | solution.py:472
  559.5 48.9 %shard_map.316.refs_5_ = bf16[8,528,2048]{2,1,0:T(8,128)(2,1)} custom-call(s32[8]{0:T(128)} %iota.46.refs_0_, bf16[512,2048]{1,0:T(8,128)(2,1)} %multiply_convert_fusion.1.refs_0_.refs_1_, bf16[512,2048]{1,0:T(8,128)(2,1)} %collective-permute-done.6.refs_0_.refs_2_, bf16[512,2048]{1,0:T(8,128)(2,1)} %collective-permute-done.8.refs_6_.refs_0_.refs_3_, ...), custom_call_target="tpu_custom_call" | custom-call | flops 35433480192 | bytes 51380224 | tf_op jit(solution)/shard_map/pallas_call | solution.py:472
  608.5 30.4 %shard_map.317 = (bf16[512,2048]{1,0:T(8,128)(2,1)}, bf16[512,2048]{1,0:T(8,128)(2,1)}, bf16[1,8,176,512]{3,2,1,0:T(8,128)(2,1)}, bf16[1,8,352,512]{3,2,1,0:T(8,128)(2,1)}, f32[1,8,1,512]{3,2,1,0:T(1,128)}) custom-call(bf16[512,2048]{1,0:T(8,128)(2,1)} %collective-permute-done.6.refs_0_.refs_2_, bf16[512,2048]{1,0:T(8,128)(2,1)} %collective-permute-done.7.refs_1_.refs_6_, ...), custom_call_target="tpu_custom_call" | custom-call | flops 17716740096 | bytes 25690112 | tf_op jit(solution)/shard_map/pallas_call | solution.py:406
  651.9 32.3 %shard_map.318 = (bf16[512,2048]{1,0:T(8,128)(2,1)}, bf16[512,2048]{1,0:T(8,128)(2,1)}, bf16[1,8,176,512]{3,2,1,0:T(8,128)(2,1)}, bf16[1,8,352,512]{3,2,1,0:T(8,128)(2,1)}, f32[1,8,1,512]{3,2,1,0:T(1,128)}) custom-call(bf16[512,2048]{1,0:T(8,128)(2,1)} %collective-permute-done.8.refs_6_.refs_0_.refs_3_, ...), custom_call_target="tpu_custom_call" | custom-call | flops 17716740096 | bytes 25690112 | tf_op jit(solution)/shard_map/pallas_call | solution.py:406
  700.9 30.8 %shard_map.319 = (bf16[512,2048]{1,0:T(8,128)(2,1)}, bf16[512,2048]{1,0:T(8,128)(2,1)}, bf16[1,8,176,512]{3,2,1,0:T(8,128)(2,1)}, bf16[1,8,352,512]{3,2,1,0:T(8,128)(2,1)}, f32[1,8,1,512]{3,2,1,0:T(1,128)}) custom-call(bf16[512,2048]{1,0:T(8,128)(2,1)} %collective-permute-done.9.refs_0_.refs_1_.refs_4_, ...), custom_call_target="tpu_custom_call" | custom-call | flops 17716740096 | bytes 25690112 | tf_op jit(solution)/shard_map/pallas_call | solution.py:406
  734.3 8.7 add_convert_fusion.15.refs_6_
  750.6 30.0 %shard_map.320 = (bf16[512,2048]{1,0:T(8,128)(2,1)}, bf16[512,2048]{1,0:T(8,128)(2,1)}, bf16[1,8,176,512]{3,2,1,0:T(8,128)(2,1)}, bf16[1,8,352,512]{3,2,1,0:T(8,128)(2,1)}, f32[1,8,1,512]{3,2,1,0:T(1,128)}) custom-call(bf16[512,2048]{1,0:T(8,128)(2,1)} %multiply_convert_fusion.1.refs_0_.refs_1_, bf16[512,2048]{1,0:T(8,128)(2,1)} %add_convert_fusion.20.refs_1_.refs_5_, ...), custom_call_target="tpu_custom_call" | custom-call | flops 17716740096 | bytes 25690112 | tf_op jit(solution)/shard_map/pallas_call | solution.py:406
  789.9 47.9 %shard_map.321 = bf16[8,528,2048]{2,1,0:T(8,128)(2,1)} custom-call(s32[8]{0:T(128)} %iota.48.refs_0_, bf16[512,2048]{1,0:T(8,128)(2,1)} %multiply_convert_fusion.1.refs_0_.refs_1_, bf16[512,2048]{1,0:T(8,128)(2,1)} %collective-permute-done.6.refs_0_.refs_2_, bf16[512,2048]{1,0:T(8,128)(2,1)} %collective-permute-done.8.refs_6_.refs_0_.refs_3_, ...), custom_call_target="tpu_custom_call" | custom-call | flops 35433480192 | bytes 51380224 | tf_op jit(solution)/shard_map/pallas_call | solution.py:472
  847.6 18.5 %collective-permute-done.15 = bf16[512,2048]{1,0:T(8,128)(2,1)} collective-permute-done((bf16[512,2048]{1,0:T(8,128)(2,1)}, bf16[512,2048]{1,0:T(8,128)(2,1)}, u32[]{:S(2)}, u32[]{:S(2)}) %collective-permute-start.15) | collective-permute-done | bytes 2097184 | tf_op jit(solution)/shard_map/ppermute | solution.py:518
  890.5 9.7 fusion.26
  902.7 37.2 %shard_map.322 = (bf16[2,256,1024]{2,1,0:T(8,128)(2,1)S(1)}, bf16[2,256,512]{2,1,0:T(8,128)(2,1)S(1)}, bf16[2,1024,640]{2,1,0:T(8,128)(2,1)}, f32[8,4,64,512]{3,2,1,0:T(8,128)}) custom-call(bf16[2,256,2048]{2,1,0:T(8,128)(2,1)S(1)} %bitcast.361, bf16[2,256,1024]{2,1,0:T(8,128)(2,1)S(1)} %bitcast.364, ...), custom_call_target="tpu_custom_call" | custom-call | flops 17179869184 | bytes 8388608 | tf_op jit(solution)/shard_map/pallas_call | solution.py:291
  974.8 37.4 %shard_map.323 = (bf16[2,256,1024]{2,1,0:T(8,128)(2,1)S(1)}, bf16[2,256,512]{2,1,0:T(8,128)(2,1)S(1)}, bf16[2,1024,640]{2,1,0:T(8,128)(2,1)}, f32[8,4,64,512]{3,2,1,0:T(8,128)}) custom-call(bf16[2,256,2048]{2,1,0:T(8,128)(2,1)S(1)} %bitcast.362, bf16[2,256,1024]{2,1,0:T(8,128)(2,1)S(1)} %bitcast.365, ...), custom_call_target="tpu_custom_call" | custom-call | flops 17179869184 | bytes 8388608 | tf_op jit(solution)/shard_map/pallas_call | solution.py:291
  1105.3 14.3 %fusion = f32[512,2048]{1,0:T(8,128)} fusion(bf16[2048,6144]{1,0:T(8,128)(2,1)} %all-gather.8.cloned.1.call-done.weights, bf16[512,512]{1,0:T(8,128)(2,1)} %slice.591, bf16[512,512]{1,0:T(8,128)(2,1)} %slice.590, bf16[512,1024]{1,0:T(8,128)(2,1)} %slice.589, bf16[512,1024]{1,0:T(8,128)(2,1)} %slice.588, f32[]{:T(128)S(6)} %add.800), kind=kOutput, calls=%fused_computation | convolution fusion | flops 6458179584 | bytes 19922948 | tf_op jit(solution)/shard_map/dot_general | solution.py:45
  1155.4 9.1 collective-permute-done.31
  1179.2 28.8 %collective-permute-done.34 = bf16[256,1024]{1,0:T(8,128)(2,1)} collective-permute-done((bf16[256,1024]{1,0:T(8,128)(2,1)}, bf16[256,1024]{1,0:T(8,128)(2,1)}, u32[]{:S(2)}, u32[]{:S(2)}) %collective-permute-start.34) | collective-permute-done | bytes 524320 | tf_op jit(solution)/shard_map/ppermute | solution.py:557
  (721 shorter events, 370.6 us)
Async XLA Ops:
  7.2 81.9 %all-gather.6.cloned.1.call-start = ((), (), s32[]{:S(2)}) async-start(), calls=%async_computation.5 | async-start | bytes 2801664 | tf_op jit(solution)/shard_map/all_gather | solution.py:581
  35.2 220.1 %all-gather.8.cloned.1.call-start = ((), (), s32[]{:S(2)}) async-start(), calls=%async_computation.6 | async-start | bytes 28311552 | tf_op jit(solution)/shard_map/all_gather | solution.py:581
  86.7 234.6 %all-gather.12.cloned.1.call-start = ((), (), s32[]{:S(2)}) async-start(), calls=%async_computation.8 | async-start | bytes 19464192 | tf_op jit(solution)/shard_map/all_gather | solution.py:581
  117.4 276.2 %all-gather.10.cloned.1.call-start = ((), (), s32[]{:S(2)}) async-start(), calls=%async_computation.7 | async-start | bytes 9732096 | tf_op jit(solution)/shard_map/all_gather | solution.py:581
  136.5 471.9 %all-gather.14.cloned.1.call-start = ((), (), s32[]{:S(2)}) async-start(), calls=%async_computation.9 | async-start | bytes 19464192 | tf_op jit(solution)/shard_map/all_gather | solution.py:581
  155.7 536.6 %reduce-scatter.6.cloned.1.call-start = ((), (), s32[]{:S(2)}) async-start(), calls=%async_computation.10 | async-start | bytes 9732096 | tf_op jit(solution)/shard_map/reduce_scatter | solution.py:585
  163.7 45.8 %collective-permute-start.7 = (bf16[512,2048]{1,0:T(8,128)(2,1)}, bf16[512,2048]{1,0:T(8,128)(2,1)}, u32[]{:S(2)}, u32[]{:S(2)}) collective-permute-start(bf16[512,2048]{1,0:T(8,128)(2,1)} %add_convert_fusion.20.refs_1_.refs_5_), channel_id=1, source_target_pairs={{0,1},{1,2},{2,3},{3,0},{4,5},{5,6},{6,7},{7,4},{8,9},{9,10},{10,1... | collective-permute-start | bytes 6291464 | tf_op jit(solution)/shard_map/ppermute | solution.py:518
  209.5 45.5 %collective-permute-start.10 = (bf16[512,2048]{1,0:T(8,128)(2,1)}, bf16[512,2048]{1,0:T(8,128)(2,1)}, u32[]{:S(2)}, u32[]{:S(2)}) collective-permute-start(bf16[512,2048]{1,0:T(8,128)(2,1)} %collective-permute-done.7.refs_1_.refs_6_), channel_id=1, source_target_pairs={{0,1},{1,2},{2,3},{3,0},{4,5},{5,6},{6,7},{7,4},{8,9},{9,10},{10,1... | collective-permute-start | bytes 6291464 | tf_op jit(solution)/shard_map/ppermute | solution.py:518
  255.0 211.8 %collective-permute-start.11 = (bf16[512,2048]{1,0:T(8,128)(2,1)}, bf16[512,2048]{1,0:T(8,128)(2,1)}, u32[]{:S(2)}, u32[]{:S(2)}) collective-permute-start(bf16[512,2048]{1,0:T(8,128)(2,1)} %collective-permute-done.10.refs_1_.refs_2_.refs_7_), channel_id=1, source_target_pairs={{0,1},{1,2},{2,3},{3,0},{4,5},{5,6},{6,7},{7,4},{8,9},{9,10},{10,1... | collective-permute-start | bytes 6291464 | tf_op jit(solution)/shard_map/ppermute | solution.py:518
  317.2 42.6 %collective-permute-start.6 = (bf16[512,2048]{1,0:T(8,128)(2,1)}, bf16[512,2048]{1,0:T(8,128)(2,1)}, u32[]{:S(2)}, u32[]{:S(2)}) collective-permute-start(bf16[512,2048]{1,0:T(8,128)(2,1)} %multiply_convert_fusion.1.refs_0_.refs_1_), channel_id=1, source_target_pairs={{0,1},{1,2},{2,3},{3,0},{4,5},{5,6},{6,7},{7,4},{8,9},{9,10},{10,1... | collective-permute-start | bytes 6291464 | tf_op jit(solution)/shard_map/ppermute | solution.py:518
  363.3 47.3 %collective-permute-start.8 = (bf16[512,2048]{1,0:T(8,128)(2,1)}, bf16[512,2048]{1,0:T(8,128)(2,1)}, u32[]{:S(2)}, u32[]{:S(2)}) collective-permute-start(bf16[512,2048]{1,0:T(8,128)(2,1)} %collective-permute-done.6.refs_0_.refs_2_), channel_id=1, source_target_pairs={{0,1},{1,2},{2,3},{3,0},{4,5},{5,6},{6,7},{7,4},{8,9},{9,10},{10,1... | collective-permute-start | bytes 6291464 | tf_op jit(solution)/shard_map/ppermute | solution.py:518
  414.1 49.1 %collective-permute-start.9 = (bf16[512,2048]{1,0:T(8,128)(2,1)}, bf16[512,2048]{1,0:T(8,128)(2,1)}, u32[]{:S(2)}, u32[]{:S(2)}) collective-permute-start(bf16[512,2048]{1,0:T(8,128)(2,1)} %collective-permute-done.8.refs_6_.refs_0_.refs_3_), channel_id=1, source_target_pairs={{0,1},{1,2},{2,3},{3,0},{4,5},{5,6},{6,7},{7,4},{8,9},{9,10},{10,1... | collective-permute-start | bytes 6291464 | tf_op jit(solution)/shard_map/ppermute | solution.py:518
  558.9 230.4 %reduce-scatter.8.cloned.1.call-start = ((), (), s32[]{:S(2)}) async-start(), calls=%async_computation.11 | async-start | bytes 19464192 | tf_op jit(solution)/shard_map/reduce_scatter | solution.py:585
  608.4 364.0 %reduce-scatter.10.cloned.1.call-start = ((), (), s32[]{:S(2)}) async-start(), calls=%async_computation.12 | async-start | bytes 19464192 | tf_op jit(solution)/shard_map/reduce_scatter | solution.py:585
  647.1 87.1 %collective-permute-start.13 = (bf16[512,2048]{1,0:T(8,128)(2,1)}, bf16[512,2048]{1,0:T(8,128)(2,1)}, u32[]{:S(2)}, u32[]{:S(2)}) collective-permute-start(bf16[512,2048]{1,0:T(8,128)(2,1)} %add_convert_fusion.18.refs_6_), channel_id=1, source_target_pairs={{0,1},{1,2},{2,3},{3,0},{4,5},{5,6},{6,7},{7,4},{8,9},{9,10},{10,1... | collective-permute-start | bytes 6291464 | tf_op jit(solution)/shard_map/ppermute | solution.py:518
  700.9 44.9 %collective-permute-start.12 = (bf16[512,2048]{1,0:T(8,128)(2,1)}, bf16[512,2048]{1,0:T(8,128)(2,1)}, u32[]{:S(2)}, u32[]{:S(2)}) collective-permute-start(bf16[512,2048]{1,0:T(8,128)(2,1)} %add_convert_fusion.17.refs_7_), channel_id=1, source_target_pairs={{0,1},{1,2},{2,3},{3,0},{4,5},{5,6},{6,7},{7,4},{8,9},{9,10},{10,1... | collective-permute-start | bytes 6291464 | tf_op jit(solution)/shard_map/ppermute | solution.py:518
  744.1 39.0 %collective-permute-start.14 = (bf16[512,2048]{1,0:T(8,128)(2,1)}, bf16[512,2048]{1,0:T(8,128)(2,1)}, u32[]{:S(2)}, u32[]{:S(2)}) collective-permute-start(bf16[512,2048]{1,0:T(8,128)(2,1)} %add_convert_fusion.15.refs_6_), channel_id=1, source_target_pairs={{0,1},{1,2},{2,3},{3,0},{4,5},{5,6},{6,7},{7,4},{8,9},{9,10},{10,1... | collective-permute-start | bytes 6291464 | tf_op jit(solution)/shard_map/ppermute | solution.py:518
  837.8 250.9 %reduce-scatter.12.cloned.1.call-start = ((), (), s32[]{:S(2)}) async-start(), calls=%async_computation.13 | async-start | bytes 3276800 | tf_op jit(solution)/shard_map/reduce_scatter | solution.py:551
  888.0 67.9 %collective-permute-start.17 = (bf16[4,256,2048]{2,1,0:T(8,128)(2,1)}, bf16[4,256,2048]{2,1,0:T(8,128)(2,1)}, u32[]{:S(2)}, u32[]{:S(2)}) collective-permute-start(bf16[4,256,2048]{2,1,0:T(8,128)(2,1)} %convolution_convert_fusion.2.refs_13_), channel_id=1, source_target_pairs={{0,4},{4,0},{8,12},{12,8},{16,20},{20,16},{24,28},{28,24},{1,5},{5... | collective-permute-start | bytes 12582920 | tf_op jit(solution)/shard_map/ppermute | solution.py:577
  889.8 75.4 %collective-permute-start.16 = (bf16[512,2048]{1,0:T(8,128)(2,1)}, bf16[512,2048]{1,0:T(8,128)(2,1)}, u32[]{:S(2)}, u32[]{:S(2)}) collective-permute-start(bf16[512,2048]{1,0:T(8,128)(2,1)} %add_convert_fusion.11.refs_14_), channel_id=1, source_target_pairs={{0,1},{1,2},{2,3},{3,0},{4,5},{5,6},{6,7},{7,4},{8,9},{9,10},{10,1... | collective-permute-start | bytes 6291464 | tf_op jit(solution)/shard_map/ppermute | solution.py:518
  955.6 82.5 %collective-permute-start.20 = (bf16[4,256,2048]{2,1,0:T(8,128)(2,1)}, bf16[4,256,2048]{2,1,0:T(8,128)(2,1)}, u32[]{:S(2)}, u32[]{:S(2)}) collective-permute-start(bf16[4,256,2048]{2,1,0:T(8,128)(2,1)} %maximum_maximum_fusion.1), channel_id=1, source_target_pairs={{0,4},{4,0},{8,12},{12,8},{16,20},{20,16},{24,28},{28,24},{1,5},{5... | collective-permute-start | bytes 12582920 | tf_op jit(solution)/shard_map/ppermute | solution.py:577
  969.9 69.8 %collective-permute-start.18 = (bf16[512,2048]{1,0:T(8,128)(2,1)}, bf16[512,2048]{1,0:T(8,128)(2,1)}, u32[]{:S(2)}, u32[]{:S(2)}) collective-permute-start(bf16[512,2048]{1,0:T(8,128)(2,1)} %add_convert_fusion.8.refs_13_), channel_id=1, source_target_pairs={{0,1},{1,2},{2,3},{3,0},{4,5},{5,6},{6,7},{7,4},{8,9},{9,10},{10,1... | collective-permute-start | bytes 6291464 | tf_op jit(solution)/shard_map/ppermute | solution.py:518
  1020.2 51.9 %collective-permute-start.19 = (bf16[4,256,2048]{2,1,0:T(8,128)(2,1)}, bf16[4,256,2048]{2,1,0:T(8,128)(2,1)}, u32[]{:S(2)}, u32[]{:S(2)}) collective-permute-start(bf16[4,256,2048]{2,1,0:T(8,128)(2,1)} %maximum_maximum_fusion), channel_id=1, source_target_pairs={{0,4},{4,0},{8,12},{12,8},{16,20},{20,16},{24,28},{28,24},{1,5},{5... | collective-permute-start | bytes 12582920 | tf_op jit(solution)/shard_map/ppermute | solution.py:577
  1035.9 175.3 %reduce-scatter.14.cloned.1.call-start = ((), (), s32[]{:S(2)}) async-start(), calls=%async_computation.14 | async-start | bytes 2801664 | tf_op jit(solution)/shard_map/reduce_scatter | solution.py:585
  1051.0 45.6 %collective-permute-start.36 = (bf16[128,2048]{1,0:T(8,128)(2,1)}, bf16[128,2048]{1,0:T(8,128)(2,1)}, u32[]{:S(2)}, u32[]{:S(2)}) collective-permute-start(bf16[128,2048]{1,0:T(8,128)(2,1)} %get-tuple-element.243), channel_id=1, source_target_pairs={{0,16},{4,20},{8,24},{12,28},{16,0},{20,4},{24,8},{28,12},{1,17},{... | collective-permute-start | bytes 1572872 | tf_op jit(solution)/shard_map/ppermute | solution.py:577
  1055.9 41.3 %collective-permute-start.38 = (bf16[128,2048]{1,0:T(8,128)(2,1)}, bf16[128,2048]{1,0:T(8,128)(2,1)}, u32[]{:S(2)}, u32[]{:S(2)}) collective-permute-start(bf16[128,2048]{1,0:T(8,128)(2,1)} %get-tuple-element.242), channel_id=1, source_target_pairs={{0,8},{4,12},{8,0},{12,4},{16,24},{20,28},{24,16},{28,20},{1,9},{5... | collective-permute-start | bytes 1572872 | tf_op jit(solution)/shard_map/ppermute | solution.py:577
  1063.9 58.2 %collective-permute-start.25 = (bf16[2,128,2048]{2,1,0:T(8,128)(2,1)}, bf16[2,128,2048]{2,1,0:T(8,128)(2,1)}, u32[]{:S(2)}, u32[]{:S(2)}) collective-permute-start(bf16[2,128,2048]{2,1,0:T(8,128)(2,1)} %get-tuple-element.261), channel_id=1, source_target_pairs={{0,8},{4,12},{8,0},{12,4},{16,24},{20,28},{24,16},{28,20},{1,9},{5... | collective-permute-start | bytes 3145736 | tf_op jit(solution)/shard_map/ppermute | solution.py:577
  1065.4 56.7 %collective-permute-start.27 = (bf16[2,128,2048]{2,1,0:T(8,128)(2,1)}, bf16[2,128,2048]{2,1,0:T(8,128)(2,1)}, u32[]{:S(2)}, u32[]{:S(2)}) collective-permute-start(bf16[2,128,2048]{2,1,0:T(8,128)(2,1)} %get-tuple-element.260), channel_id=1, source_target_pairs={{0,16},{4,20},{8,24},{12,28},{16,0},{20,4},{24,8},{28,12},{1,17},{... | collective-permute-start | bytes 3145736 | tf_op jit(solution)/shard_map/ppermute | solution.py:577
  1081.0 65.0 %collective-permute-start.30 = (bf16[2,128,2048]{2,1,0:T(8,128)(2,1)}, bf16[2,128,2048]{2,1,0:T(8,128)(2,1)}, u32[]{:S(2)}, u32[]{:S(2)}) collective-permute-start(bf16[2,128,2048]{2,1,0:T(8,128)(2,1)} %get-tuple-element.250), channel_id=1, source_target_pairs={{0,8},{4,12},{8,0},{12,4},{16,24},{20,28},{24,16},{28,20},{1,9},{5... | collective-permute-start | bytes 3145736 | tf_op jit(solution)/shard_map/ppermute | solution.py:577
  1096.6 49.6 %collective-permute-start.32 = (bf16[2,128,2048]{2,1,0:T(8,128)(2,1)}, bf16[2,128,2048]{2,1,0:T(8,128)(2,1)}, u32[]{:S(2)}, u32[]{:S(2)}) collective-permute-start(bf16[2,128,2048]{2,1,0:T(8,128)(2,1)} %get-tuple-element.251), channel_id=1, source_target_pairs={{0,16},{4,20},{8,24},{12,28},{16,0},{20,4},{24,8},{28,12},{1,17},{... | collective-permute-start | bytes 3145736 | tf_op jit(solution)/shard_map/ppermute | solution.py:577
  1100.8 71.9 %collective-permute-start.39 = (bf16[256,512]{1,0:T(8,128)(2,1)}, bf16[256,512]{1,0:T(8,128)(2,1)}, u32[]{:S(2)}, u32[]{:S(2)}) collective-permute-start(bf16[256,512]{1,0:T(8,128)(2,1)} %get-tuple-element.312), channel_id=1, source_target_pairs={{0,3},{1,0},{2,1},{3,2},{4,7},{5,4},{6,5},{7,6},{8,11},{9,8},{10,9... | collective-permute-start | bytes 786440 | tf_op jit(solution)/shard_map/ppermute | solution.py:557
  1171.8 36.2 %collective-permute-start.34 = (bf16[256,1024]{1,0:T(8,128)(2,1)}, bf16[256,1024]{1,0:T(8,128)(2,1)}, u32[]{:S(2)}, u32[]{:S(2)}) collective-permute-start(bf16[256,1024]{1,0:T(8,128)(2,1)} %pad_maximum_fusion.10), channel_id=1, source_target_pairs={{0,2},{1,3},{2,0},{3,1},{4,6},{5,7},{6,4},{7,5},{8,10},{9,11},{10,... | collective-permute-start | bytes 1572872 | tf_op jit(solution)/shard_map/ppermute | solution.py:557
  (203 other events, 3123.3 us)
Sparse Core Ops, SparseCore 0:
  35.4 31.3 all-gather.5
  86.8 123.0 all-gather.7
  212.3 92.0 all-gather.11
  306.8 57.1 all-gather.9
  365.6 92.0 all-gather.13
  559.0 73.0 reduce-scatter.5
  636.2 118.5 reduce-scatter.7
  838.0 119.9 reduce-scatter.9
  1036.0 49.8 reduce-scatter.11
  1137.4 42.5 reduce-scatter.13

commit v3 on v2

--- a/solution.py
+++ b/solution.py
@@ -976,7 +976,8 @@
         previous.append(first_sum)
     last_sum = scatter_fsdp(grads_of(split, all_units).reshape(-1, width))
     pieces[0] = finish_piece(0, *previous)
-    grad_hidden_own = hop(total).astype(wide) + pieces[0][1]
+    router_gradient = sum(dot(pieces[s][2], hidden_pieces[s], NN) for s in chunks)
+    grad_hidden_own = hop(total).astype(wide) + (pieces[0][1] + zero_of(router_gradient))
 
     hidden_back = jax.vjp(normalize, hidden, ffn_scale)[1]
     grad_hnorm, grad_ffn_gain = hidden_back(grad_hidden_own)
@@ -1021,9 +1022,6 @@
     first_scatter.join(make_first_query, out_scatter.turned, branch_moved)
     second_scatter.join(make_second_query, first_scatter.part)
     half_plain, half_turned = first_qn.shape[2], first_qr.shape[2]
-    router_gradient = sum(
-        dot(after(pieces[s][2], second_scatter.part), hidden_pieces[s], NN) for s in chunks
-    )
     query_gradient = jnp.concatenate(
         [
             first_query[:, :half_plain],
@@ -1033,7 +1031,7 @@
         ],
         axis=1,
     )
-    grad_normed = dot(after(query_gradient, second_scatter.part, grad_latent_sum), query_whole, NT)
+    grad_normed = dot(after(query_gradient, second_scatter.part), query_whole, NT)
     first_scatter.turn(grad_normed)
 
     latent_back = jax.vjp(normalize, compressed, latent_scale)[1]

time: 1260 us -> 1240 us (0.984)
  waiting for transfers between devices: 266 us -> 253 us
    unnamed x407 -> x415, local copies, waits for them, and re-layouts: 42 us -> 33.5 us
  transfers between devices with their start and end apart: 52 -> 52, of which waited for: 17 -> 18; matrix products, arithmetic and copies ran while one was open for 24% -> 25% of each run, Pallas kernels for 41% -> 42%
where the time goes in v3:
time: 1240 us; the launch traced here: 1230 us
  Pallas kernels  559 us (45%)
  waiting for transfers between devices  253 us (20%)
  other arithmetic  130 us (10%)
  matrix products  99 us (8%)
  local copies, waits for them, and re-layouts  98.2 us (8%)
  between operations  49 us (4%)
  starting transfers between devices  39.2 us (3%)
    pallas_call x11, Pallas kernels, feed_forward(): pl.pallas_call(without(functools.partial(ffn_kernel, pieces), 2 * pieces...  308 us
    ppermute x18, waiting for transfers between devices, hop(): lax.ppermute(values, 'tp', [(i, (i + 1) % count) for i in range(count)])  193 us
    pallas_call x3, Pallas kernels, weight_grads(): pl.pallas_call(without(functools.partial(weight_grad_kernel, pieces, join...  126 us
    dot_general x24, matrix products, dot(): lax.dot_general(a, b, (dims, ((), ())), preferred_element_type=wide)  99 us
    pallas_call x2, Pallas kernels, attend_back(): pl.pallas_call(without(attend_back_kernel, 13, waits), grid=(pairs, seqs)...  74.9 us
    pallas_call x1, Pallas kernels, attend(): pl.pallas_call(attend_kernel, grid=(pairs, seqs), in_specs=[pl.BlockSpec(...  39 us
    unnamed x415, local copies, waits for them, and re-layouts  33.5 us
    ppermute x6, waiting for transfers between devices, cross_moves(): lax.ppermute(pieces[s].astype(narrow), 'tp', [(i, (i - s) % count) for i...  28.5 us
  transfers between devices with their start and end apart: 52, of which 18 were waited for; matrix products, arithmetic and copies ran while one was open for 25% of the time, Pallas kernels for 42%

profile of v3, /device:TPU:0, one launch (start us, length us, event | category | flops | bytes accessed | tf_op | source)
XLA Modules:
  0.0 1227.0 jit_solution(2838282274210465611)
XLA Ops:
  14.9 19.5 %collective-permute-done = bf16[256,1536]{1,0:T(8,128)(2,1)S(1)} collective-permute-done((bf16[256,1536]{1,0:T(8,128)(2,1)S(1)}, bf16[256,1536]{1,0:T(8,128)(2,1)S(1)}, u32[]{:S(2)}, u32[]{:S(2)}) %collective-permute-start) | collective-permute-done | bytes 786464 | tf_op jit(solution)/shard_map/ppermute | solution.py:518
  35.3 19.6 %collective-permute-done.1 = bf16[256,1536]{1,0:T(8,128)(2,1)S(1)} collective-permute-done((bf16[256,1536]{1,0:T(8,128)(2,1)S(1)}, bf16[256,1536]{1,0:T(8,128)(2,1)S(1)}, u32[]{:S(2)}, u32[]{:S(2)}) %collective-permute-start.1) | collective-permute-done | bytes 786464 | tf_op jit(solution)/shard_map/ppermute | solution.py:518
  57.2 17.3 %collective-permute-done.2 = bf16[256,1536]{1,0:T(8,128)(2,1)S(1)} collective-permute-done((bf16[256,1536]{1,0:T(8,128)(2,1)S(1)}, bf16[256,1536]{1,0:T(8,128)(2,1)S(1)}, u32[]{:S(2)}, u32[]{:S(2)}) %collective-permute-start.2) | collective-permute-done | bytes 786464 | tf_op jit(solution)/shard_map/ppermute | solution.py:518
  103.2 11.0 collective-permute-done.3
  118.0 13.9 %collective-permute-done.4 = bf16[512,640]{1,0:T(8,128)(2,1)S(1)} collective-permute-done((bf16[512,640]{1,0:T(8,128)(2,1)S(1)}, bf16[512,640]{1,0:T(8,128)(2,1)S(1)}, u32[]{:S(2)}, u32[]{:S(2)}) %collective-permute-start.4) | collective-permute-done | bytes 655392 | tf_op jit(solution)/shard_map/ppermute | solution.py:518
  137.1 13.0 %collective-permute-done.5 = bf16[512,640]{1,0:T(8,128)(2,1)S(1)} collective-permute-done((bf16[512,640]{1,0:T(8,128)(2,1)S(1)}, bf16[512,640]{1,0:T(8,128)(2,1)S(1)}, u32[]{:S(2)}, u32[]{:S(2)}) %collective-permute-start.5) | collective-permute-done | bytes 655392 | tf_op jit(solution)/shard_map/ppermute | solution.py:518
  164.0 45.8 %collective-permute-done.7.refs_1_.refs_6_ = bf16[512,2048]{1,0:T(8,128)(2,1)} collective-permute-done((bf16[512,2048]{1,0:T(8,128)(2,1)}, bf16[512,2048]{1,0:T(8,128)(2,1)}, u32[]{:S(2)}, u32[]{:S(2)}) %collective-permute-start.7) | collective-permute-done | bytes 2097184 | tf_op jit(solution)/shard_map/ppermute | solution.py:518
  218.1 37.4 %collective-permute-done.10.refs_1_.refs_2_.refs_7_ = bf16[512,2048]{1,0:T(8,128)(2,1)} collective-permute-done((bf16[512,2048]{1,0:T(8,128)(2,1)}, bf16[512,2048]{1,0:T(8,128)(2,1)}, u32[]{:S(2)}, u32[]{:S(2)}) %collective-permute-start.10) | collective-permute-done | bytes 2097184 | tf_op jit(solution)/shard_map/ppermute | solution.py:518
  255.6 11.9 shard_map.306
  267.6 39.0 %shard_map.307 = (bf16[2,256,2048]{2,1,0:T(8,128)(2,1)S(1)}, f32[2,256,2048]{2,1,0:T(8,128)}, bf16[2,1024,4096]{2,1,0:T(8,128)(2,1)}) custom-call(bf16[2,256,2048]{2,1,0:T(8,128)(2,1)S(1)} %bitcast.364, bf16[2,256,1024]{2,1,0:T(8,128)(2,1)S(1)} %bitcast.367, bf16[2,1024,640]{2,1,0:T(8,128)(2,1)} %pad_maximum_fusion.1.latent.rope.refs_2_.refs_3_, ...), custom_call_target="tpu_custom_call" | custom-call | flops 15032385536 | bytes 16777216 | tf_op jit(solution)/shard_map/pallas_call | solution.py:178
  321.0 29.9 %shard_map.308 = (bf16[512,2048]{1,0:T(8,128)(2,1)}, bf16[512,2048]{1,0:T(8,128)(2,1)}, bf16[1,8,176,512]{3,2,1,0:T(8,128)(2,1)}, bf16[1,8,352,512]{3,2,1,0:T(8,128)(2,1)}, f32[1,8,1,512]{3,2,1,0:T(1,128)}) custom-call(bf16[512,2048]{1,0:T(8,128)(2,1)} %multiply_convert_fusion.1.refs_0_.refs_1_, bf16[512,2048]{1,0:T(8,128)(2,1)} %add_convert_fusion.20.refs_1_.refs_5_, ...), custom_call_target="tpu_custom_call" | custom-call | flops 17716740096 | bytes 25690112 | tf_op jit(solution)/shard_map/pallas_call | solution.py:406
  350.9 8.6 collective-permute-done.6.refs_0_.refs_2_
  363.3 30.4 %shard_map.309 = (bf16[512,2048]{1,0:T(8,128)(2,1)}, bf16[512,2048]{1,0:T(8,128)(2,1)}, bf16[1,8,176,512]{3,2,1,0:T(8,128)(2,1)}, bf16[1,8,352,512]{3,2,1,0:T(8,128)(2,1)}, f32[1,8,1,512]{3,2,1,0:T(1,128)}) custom-call(bf16[512,2048]{1,0:T(8,128)(2,1)} %collective-permute-done.6.refs_0_.refs_2_, bf16[512,2048]{1,0:T(8,128)(2,1)} %collective-permute-done.7.refs_1_.refs_6_, ...), custom_call_target="tpu_custom_call" | custom-call | flops 17716740096 | bytes 25690112 | tf_op jit(solution)/shard_map/pallas_call | solution.py:406
  394.3 16.4 %shard_map.310 = (bf16[512,2048]{1,0:T(8,128)(2,1)}, bf16[512,2048]{1,0:T(8,128)(2,1)}, bf16[1,4,176,512]{3,2,1,0:T(8,128)(2,1)}, bf16[1,4,352,512]{3,2,1,0:T(8,128)(2,1)}, f32[1,4,1,512]{3,2,1,0:T(1,128)}) custom-call(bf16[512,2048]{1,0:T(8,128)(2,1)} %multiply_convert_fusion.1.refs_0_.refs_1_, bf16[512,2048]{1,0:T(8,128)(2,1)} %add_convert_fusion.20.refs_1_.refs_5_, ...), custom_call_target="tpu_custom_call" | custom-call | flops 8858370048 | bytes 17039360 | tf_op jit(solution)/shard_map/pallas_call | solution.py:406
  416.7 16.4 %shard_map.311 = (bf16[512,2048]{1,0:T(8,128)(2,1)}, bf16[512,2048]{1,0:T(8,128)(2,1)}, bf16[1,4,176,512]{3,2,1,0:T(8,128)(2,1)}, bf16[1,4,352,512]{3,2,1,0:T(8,128)(2,1)}, f32[1,4,1,512]{3,2,1,0:T(1,128)}) custom-call(bf16[512,2048]{1,0:T(8,128)(2,1)} %collective-permute-done.6.refs_0_.refs_2_, bf16[512,2048]{1,0:T(8,128)(2,1)} %collective-permute-done.7.refs_1_.refs_6_, ...), custom_call_target="tpu_custom_call" | custom-call | flops 8858370048 | bytes 17039360 | tf_op jit(solution)/shard_map/pallas_call | solution.py:406
  433.1 30.1 %shard_map.312 = (bf16[512,2048]{1,0:T(8,128)(2,1)}, bf16[512,2048]{1,0:T(8,128)(2,1)}, bf16[1,8,176,512]{3,2,1,0:T(8,128)(2,1)}, bf16[1,8,352,512]{3,2,1,0:T(8,128)(2,1)}, f32[1,8,1,512]{3,2,1,0:T(1,128)}) custom-call(bf16[512,2048]{1,0:T(8,128)(2,1)} %collective-permute-done.8.refs_6_.refs_0_.refs_3_, ...), custom_call_target="tpu_custom_call" | custom-call | flops 17716740096 | bytes 25690112 | tf_op jit(solution)/shard_map/pallas_call | solution.py:406
  466.8 30.3 %shard_map.313 = (bf16[512,2048]{1,0:T(8,128)(2,1)}, bf16[512,2048]{1,0:T(8,128)(2,1)}, bf16[1,8,176,512]{3,2,1,0:T(8,128)(2,1)}, bf16[1,8,352,512]{3,2,1,0:T(8,128)(2,1)}, f32[1,8,1,512]{3,2,1,0:T(1,128)}) custom-call(bf16[512,2048]{1,0:T(8,128)(2,1)} %collective-permute-done.9.refs_0_.refs_1_.refs_4_, ...), custom_call_target="tpu_custom_call" | custom-call | flops 17716740096 | bytes 25690112 | tf_op jit(solution)/shard_map/pallas_call | solution.py:406
  497.7 31.0 %shard_map.314 = (bf16[512,2048]{1,0:T(8,128)(2,1)}, bf16[512,2048]{1,0:T(8,128)(2,1)}, bf16[512,2048]{1,0:T(8,128)(2,1)}, bf16[512,2048]{1,0:T(8,128)(2,1)}, bf...) custom-call(bf16[512,2048]{1,0:T(8,128)(2,1)} %collective-permute-done.8.refs_6_.refs_0_.r, ...), custom_call_target="tpu_custom_call" | custom-call | flops 17716740096 | bytes 34078720 | tf_op jit(solution)/shard_map/pallas_call | solution.py:406
  530.5 28.6 %shard_map.315.refs_25_ = bf16[4,528,2048]{2,1,0:T(8,128)(2,1)} custom-call(s32[4]{0:T(128)} %iota.47.refs_0_, bf16[512,2048]{1,0:T(8,128)(2,1)} %multiply_convert_fusion.1.refs_0_.refs_1_, bf16[512,2048]{1,0:T(8,128)(2,1)} %collective-permute-done.6.refs_0_.refs_2_, bf16[512,2048]{1,0:T(8,128)(2,1)} %collective-permute-done.8.refs_6_.refs_0_.refs_3_, ...), custom_call_target="tpu_custom_call" | custom-call | flops 17716740096 | bytes 34078720 | tf_op jit(solution)/shard_map/pallas_call | solution.py:472
  559.7 49.1 %shard_map.316.refs_5_ = bf16[8,528,2048]{2,1,0:T(8,128)(2,1)} custom-call(s32[8]{0:T(128)} %iota.46.refs_0_, bf16[512,2048]{1,0:T(8,128)(2,1)} %multiply_convert_fusion.1.refs_0_.refs_1_, bf16[512,2048]{1,0:T(8,128)(2,1)} %collective-permute-done.6.refs_0_.refs_2_, bf16[512,2048]{1,0:T(8,128)(2,1)} %collective-permute-done.8.refs_6_.refs_0_.refs_3_, ...), custom_call_target="tpu_custom_call" | custom-call | flops 35433480192 | bytes 51380224 | tf_op jit(solution)/shard_map/pallas_call | solution.py:472
  609.0 30.2 %shard_map.317 = (bf16[512,2048]{1,0:T(8,128)(2,1)}, bf16[512,2048]{1,0:T(8,128)(2,1)}, bf16[1,8,176,512]{3,2,1,0:T(8,128)(2,1)}, bf16[1,8,352,512]{3,2,1,0:T(8,128)(2,1)}, f32[1,8,1,512]{3,2,1,0:T(1,128)}) custom-call(bf16[512,2048]{1,0:T(8,128)(2,1)} %collective-permute-done.6.refs_0_.refs_2_, bf16[512,2048]{1,0:T(8,128)(2,1)} %collective-permute-done.7.refs_1_.refs_6_, ...), custom_call_target="tpu_custom_call" | custom-call | flops 17716740096 | bytes 25690112 | tf_op jit(solution)/shard_map/pallas_call | solution.py:406
  652.2 32.3 %shard_map.318 = (bf16[512,2048]{1,0:T(8,128)(2,1)}, bf16[512,2048]{1,0:T(8,128)(2,1)}, bf16[1,8,176,512]{3,2,1,0:T(8,128)(2,1)}, bf16[1,8,352,512]{3,2,1,0:T(8,128)(2,1)}, f32[1,8,1,512]{3,2,1,0:T(1,128)}) custom-call(bf16[512,2048]{1,0:T(8,128)(2,1)} %collective-permute-done.8.refs_6_.refs_0_.refs_3_, ...), custom_call_target="tpu_custom_call" | custom-call | flops 17716740096 | bytes 25690112 | tf_op jit(solution)/shard_map/pallas_call | solution.py:406
  701.1 30.6 %shard_map.319 = (bf16[512,2048]{1,0:T(8,128)(2,1)}, bf16[512,2048]{1,0:T(8,128)(2,1)}, bf16[1,8,176,512]{3,2,1,0:T(8,128)(2,1)}, bf16[1,8,352,512]{3,2,1,0:T(8,128)(2,1)}, f32[1,8,1,512]{3,2,1,0:T(1,128)}) custom-call(bf16[512,2048]{1,0:T(8,128)(2,1)} %collective-permute-done.9.refs_0_.refs_1_.refs_4_, ...), custom_call_target="tpu_custom_call" | custom-call | flops 17716740096 | bytes 25690112 | tf_op jit(solution)/shard_map/pallas_call | solution.py:406
  734.3 8.7 add_convert_fusion.15.refs_6_
  750.7 30.0 %shard_map.320 = (bf16[512,2048]{1,0:T(8,128)(2,1)}, bf16[512,2048]{1,0:T(8,128)(2,1)}, bf16[1,8,176,512]{3,2,1,0:T(8,128)(2,1)}, bf16[1,8,352,512]{3,2,1,0:T(8,128)(2,1)}, f32[1,8,1,512]{3,2,1,0:T(1,128)}) custom-call(bf16[512,2048]{1,0:T(8,128)(2,1)} %multiply_convert_fusion.1.refs_0_.refs_1_, bf16[512,2048]{1,0:T(8,128)(2,1)} %add_convert_fusion.20.refs_1_.refs_5_, ...), custom_call_target="tpu_custom_call" | custom-call | flops 17716740096 | bytes 25690112 | tf_op jit(solution)/shard_map/pallas_call | solution.py:406
  790.1 47.9 %shard_map.321 = bf16[8,528,2048]{2,1,0:T(8,128)(2,1)} custom-call(s32[8]{0:T(128)} %iota.48.refs_0_, bf16[512,2048]{1,0:T(8,128)(2,1)} %multiply_convert_fusion.1.refs_0_.refs_1_, bf16[512,2048]{1,0:T(8,128)(2,1)} %collective-permute-done.6.refs_0_.refs_2_, bf16[512,2048]{1,0:T(8,128)(2,1)} %collective-permute-done.8.refs_6_.refs_0_.refs_3_, ...), custom_call_target="tpu_custom_call" | custom-call | flops 35433480192 | bytes 51380224 | tf_op jit(solution)/shard_map/pallas_call | solution.py:472
  887.3 9.7 fusion.26
  899.6 37.2 %shard_map.322 = (bf16[2,256,1024]{2,1,0:T(8,128)(2,1)S(1)}, bf16[2,256,512]{2,1,0:T(8,128)(2,1)S(1)}, bf16[2,1024,640]{2,1,0:T(8,128)(2,1)}, f32[8,4,64,512]{3,2,1,0:T(8,128)}) custom-call(bf16[2,256,2048]{2,1,0:T(8,128)(2,1)S(1)} %bitcast.365, bf16[2,256,1024]{2,1,0:T(8,128)(2,1)S(1)} %bitcast.368, ...), custom_call_target="tpu_custom_call" | custom-call | flops 17179869184 | bytes 8388608 | tf_op jit(solution)/shard_map/pallas_call | solution.py:291
  974.1 37.7 %shard_map.323 = (bf16[2,256,1024]{2,1,0:T(8,128)(2,1)S(1)}, bf16[2,256,512]{2,1,0:T(8,128)(2,1)S(1)}, bf16[2,1024,640]{2,1,0:T(8,128)(2,1)}, f32[8,4,64,512]{3,2,1,0:T(8,128)}) custom-call(bf16[2,256,2048]{2,1,0:T(8,128)(2,1)S(1)} %bitcast.366, bf16[2,256,1024]{2,1,0:T(8,128)(2,1)S(1)} %bitcast.369, ...), custom_call_target="tpu_custom_call" | custom-call | flops 17179869184 | bytes 8388608 | tf_op jit(solution)/shard_map/pallas_call | solution.py:291
  1070.6 14.3 %fusion = f32[512,2048]{1,0:T(8,128)} fusion(bf16[2048,6144]{1,0:T(8,128)(2,1)} %all-gather.8.cloned.1.call-done.weights, bf16[512,512]{1,0:T(8,128)(2,1)} %slice.588, bf16[512,512]{1,0:T(8,128)(2,1)} %slice.587, bf16[512,1024]{1,0:T(8,128)(2,1)} %slice.586, bf16[512,1024]{1,0:T(8,128)(2,1)} %slice.585, f32[]{:T(128)} %bitcast.118), kind=kOutput, calls=%fused_computation | convolution fusion | flops 6458179584 | bytes 19923456 | tf_op jit(solution)/shard_map/dot_general | solution.py:45
  1160.5 27.8 %collective-permute-done.34 = bf16[256,1024]{1,0:T(8,128)(2,1)S(1)} collective-permute-done((bf16[256,1024]{1,0:T(8,128)(2,1)S(1)}, bf16[256,1024]{1,0:T(8,128)(2,1)S(1)}, u32[]{:S(2)}, u32[]{:S(2)}) %collective-permute-start.34) | collective-permute-done | bytes 524320 | tf_op jit(solution)/shard_map/ppermute | solution.py:557
  1203.7 12.3 %collective-permute-done.23 = bf16[608,256]{1,0:T(8,128)(2,1)S(1)} collective-permute-done((bf16[608,256]{1,0:T(8,128)(2,1)}, bf16[608,256]{1,0:T(8,128)(2,1)S(1)}, u32[]{:S(2)}, u32[]{:S(2)}) %collective-permute-start.23) | collective-permute-done | bytes 311328 | tf_op jit(solution)/shard_map/ppermute | solution.py:566
  (729 shorter events, 360.2 us)
Async XLA Ops:
  7.2 82.4 %all-gather.6.cloned.1.call-start = ((), (), s32[]{:S(2)}) async-start(), calls=%async_computation.5 | async-start | bytes 2801664 | tf_op jit(solution)/shard_map/all_gather | solution.py:581
  35.3 220.4 %all-gather.8.cloned.1.call-start = ((), (), s32[]{:S(2)}) async-start(), calls=%async_computation.6 | async-start | bytes 28311552 | tf_op jit(solution)/shard_map/all_gather | solution.py:581
  86.6 234.4 %all-gather.12.cloned.1.call-start = ((), (), s32[]{:S(2)}) async-start(), calls=%async_computation.8 | async-start | bytes 19464192 | tf_op jit(solution)/shard_map/all_gather | solution.py:581
  117.8 275.8 %all-gather.10.cloned.1.call-start = ((), (), s32[]{:S(2)}) async-start(), calls=%async_computation.7 | async-start | bytes 9732096 | tf_op jit(solution)/shard_map/all_gather | solution.py:581
  137.0 472.0 %all-gather.14.cloned.1.call-start = ((), (), s32[]{:S(2)}) async-start(), calls=%async_computation.9 | async-start | bytes 19464192 | tf_op jit(solution)/shard_map/all_gather | solution.py:581
  156.3 536.4 %reduce-scatter.6.cloned.1.call-start = ((), (), s32[]{:S(2)}) async-start(), calls=%async_computation.10 | async-start | bytes 9732096 | tf_op jit(solution)/shard_map/reduce_scatter | solution.py:585
  164.0 45.8 %collective-permute-start.7 = (bf16[512,2048]{1,0:T(8,128)(2,1)}, bf16[512,2048]{1,0:T(8,128)(2,1)}, u32[]{:S(2)}, u32[]{:S(2)}) collective-permute-start(bf16[512,2048]{1,0:T(8,128)(2,1)} %add_convert_fusion.20.refs_1_.refs_5_), channel_id=1, source_target_pairs={{0,1},{1,2},{2,3},{3,0},{4,5},{5,6},{6,7},{7,4},{8,9},{9,10},{10,1... | collective-permute-start | bytes 6291464 | tf_op jit(solution)/shard_map/ppermute | solution.py:518
  209.8 45.6 %collective-permute-start.10 = (bf16[512,2048]{1,0:T(8,128)(2,1)}, bf16[512,2048]{1,0:T(8,128)(2,1)}, u32[]{:S(2)}, u32[]{:S(2)}) collective-permute-start(bf16[512,2048]{1,0:T(8,128)(2,1)} %collective-permute-done.7.refs_1_.refs_6_), channel_id=1, source_target_pairs={{0,1},{1,2},{2,3},{3,0},{4,5},{5,6},{6,7},{7,4},{8,9},{9,10},{10,1... | collective-permute-start | bytes 6291464 | tf_op jit(solution)/shard_map/ppermute | solution.py:518
  255.4 211.3 %collective-permute-start.11 = (bf16[512,2048]{1,0:T(8,128)(2,1)}, bf16[512,2048]{1,0:T(8,128)(2,1)}, u32[]{:S(2)}, u32[]{:S(2)}) collective-permute-start(bf16[512,2048]{1,0:T(8,128)(2,1)} %collective-permute-done.10.refs_1_.refs_2_.refs_7_), channel_id=1, source_target_pairs={{0,1},{1,2},{2,3},{3,0},{4,5},{5,6},{6,7},{7,4},{8,9},{9,10},{10,1... | collective-permute-start | bytes 6291464 | tf_op jit(solution)/shard_map/ppermute | solution.py:518
  317.3 42.2 %collective-permute-start.6 = (bf16[512,2048]{1,0:T(8,128)(2,1)}, bf16[512,2048]{1,0:T(8,128)(2,1)}, u32[]{:S(2)}, u32[]{:S(2)}) collective-permute-start(bf16[512,2048]{1,0:T(8,128)(2,1)} %multiply_convert_fusion.1.refs_0_.refs_1_), channel_id=1, source_target_pairs={{0,1},{1,2},{2,3},{3,0},{4,5},{5,6},{6,7},{7,4},{8,9},{9,10},{10,1... | collective-permute-start | bytes 6291464 | tf_op jit(solution)/shard_map/ppermute | solution.py:518
  363.0 47.7 %collective-permute-start.8 = (bf16[512,2048]{1,0:T(8,128)(2,1)}, bf16[512,2048]{1,0:T(8,128)(2,1)}, u32[]{:S(2)}, u32[]{:S(2)}) collective-permute-start(bf16[512,2048]{1,0:T(8,128)(2,1)} %collective-permute-done.6.refs_0_.refs_2_), channel_id=1, source_target_pairs={{0,1},{1,2},{2,3},{3,0},{4,5},{5,6},{6,7},{7,4},{8,9},{9,10},{10,1... | collective-permute-start | bytes 6291464 | tf_op jit(solution)/shard_map/ppermute | solution.py:518
  414.2 49.0 %collective-permute-start.9 = (bf16[512,2048]{1,0:T(8,128)(2,1)}, bf16[512,2048]{1,0:T(8,128)(2,1)}, u32[]{:S(2)}, u32[]{:S(2)}) collective-permute-start(bf16[512,2048]{1,0:T(8,128)(2,1)} %collective-permute-done.8.refs_6_.refs_0_.refs_3_), channel_id=1, source_target_pairs={{0,1},{1,2},{2,3},{3,0},{4,5},{5,6},{6,7},{7,4},{8,9},{9,10},{10,1... | collective-permute-start | bytes 6291464 | tf_op jit(solution)/shard_map/ppermute | solution.py:518
  559.2 230.4 %reduce-scatter.8.cloned.1.call-start = ((), (), s32[]{:S(2)}) async-start(), calls=%async_computation.11 | async-start | bytes 19464192 | tf_op jit(solution)/shard_map/reduce_scatter | solution.py:585
  608.9 364.3 %reduce-scatter.10.cloned.1.call-start = ((), (), s32[]{:S(2)}) async-start(), calls=%async_computation.12 | async-start | bytes 19464192 | tf_op jit(solution)/shard_map/reduce_scatter | solution.py:585
  647.7 86.5 %collective-permute-start.13 = (bf16[512,2048]{1,0:T(8,128)(2,1)}, bf16[512,2048]{1,0:T(8,128)(2,1)}, u32[]{:S(2)}, u32[]{:S(2)}) collective-permute-start(bf16[512,2048]{1,0:T(8,128)(2,1)} %add_convert_fusion.18.refs_6_), channel_id=1, source_target_pairs={{0,1},{1,2},{2,3},{3,0},{4,5},{5,6},{6,7},{7,4},{8,9},{9,10},{10,1... | collective-permute-start | bytes 6291464 | tf_op jit(solution)/shard_map/ppermute | solution.py:518
  701.1 44.7 %collective-permute-start.12 = (bf16[512,2048]{1,0:T(8,128)(2,1)}, bf16[512,2048]{1,0:T(8,128)(2,1)}, u32[]{:S(2)}, u32[]{:S(2)}) collective-permute-start(bf16[512,2048]{1,0:T(8,128)(2,1)} %add_convert_fusion.17.refs_7_), channel_id=1, source_target_pairs={{0,1},{1,2},{2,3},{3,0},{4,5},{5,6},{6,7},{7,4},{8,9},{9,10},{10,1... | collective-permute-start | bytes 6291464 | tf_op jit(solution)/shard_map/ppermute | solution.py:518
  744.2 39.0 %collective-permute-start.14 = (bf16[512,2048]{1,0:T(8,128)(2,1)}, bf16[512,2048]{1,0:T(8,128)(2,1)}, u32[]{:S(2)}, u32[]{:S(2)}) collective-permute-start(bf16[512,2048]{1,0:T(8,128)(2,1)} %add_convert_fusion.15.refs_6_), channel_id=1, source_target_pairs={{0,1},{1,2},{2,3},{3,0},{4,5},{5,6},{6,7},{7,4},{8,9},{9,10},{10,1... | collective-permute-start | bytes 6291464 | tf_op jit(solution)/shard_map/ppermute | solution.py:518
  838.0 272.8 %reduce-scatter.12.cloned.1.call-start = ((), (), s32[]{:S(2)}) async-start(), calls=%async_computation.13 | async-start | bytes 3276800 | tf_op jit(solution)/shard_map/reduce_scatter | solution.py:551
  884.8 68.8 %collective-permute-start.17 = (bf16[4,256,2048]{2,1,0:T(8,128)(2,1)}, bf16[4,256,2048]{2,1,0:T(8,128)(2,1)}, u32[]{:S(2)}, u32[]{:S(2)}) collective-permute-start(bf16[4,256,2048]{2,1,0:T(8,128)(2,1)} %convolution_convert_fusion.2.refs_13_), channel_id=1, source_target_pairs={{0,4},{4,0},{8,12},{12,8},{16,20},{20,16},{24,28},{28,24},{1,5},{5... | collective-permute-start | bytes 12582920 | tf_op jit(solution)/shard_map/ppermute | solution.py:577
  886.5 79.6 %collective-permute-start.16 = (bf16[512,2048]{1,0:T(8,128)(2,1)}, bf16[512,2048]{1,0:T(8,128)(2,1)}, u32[]{:S(2)}, u32[]{:S(2)}) collective-permute-start(bf16[512,2048]{1,0:T(8,128)(2,1)} %add_convert_fusion.11.refs_14_), channel_id=1, source_target_pairs={{0,1},{1,2},{2,3},{3,0},{4,5},{5,6},{6,7},{7,4},{8,9},{9,10},{10,1... | collective-permute-start | bytes 6291464 | tf_op jit(solution)/shard_map/ppermute | solution.py:518
  953.6 71.7 %collective-permute-start.20 = (bf16[4,256,2048]{2,1,0:T(8,128)(2,1)}, bf16[4,256,2048]{2,1,0:T(8,128)(2,1)}, u32[]{:S(2)}, u32[]{:S(2)}) collective-permute-start(bf16[4,256,2048]{2,1,0:T(8,128)(2,1)} %maximum_maximum_fusion.1), channel_id=1, source_target_pairs={{0,4},{4,0},{8,12},{12,8},{16,20},{20,16},{24,28},{28,24},{1,5},{5... | collective-permute-start | bytes 12582920 | tf_op jit(solution)/shard_map/ppermute | solution.py:577
  963.7 68.4 %collective-permute-start.21 = (bf16[2,128,2048]{2,1,0:T(8,128)(2,1)}, bf16[2,128,2048]{2,1,0:T(8,128)(2,1)}, u32[]{:S(2)}, u32[]{:S(2)}) collective-permute-start(bf16[2,128,2048]{2,1,0:T(8,128)(2,1)} %get-tuple-element.245), channel_id=1, source_target_pairs={{0,8},{4,12},{8,0},{12,4},{16,24},{20,28},{24,16},{28,20},{1,9},{5... | collective-permute-start | bytes 3145736 | tf_op jit(solution)/shard_map/ppermute | solution.py:577
  963.9 68.2 %collective-permute-start.37 = (bf16[2,128,2048]{2,1,0:T(8,128)(2,1)}, bf16[2,128,2048]{2,1,0:T(8,128)(2,1)}, u32[]{:S(2)}, u32[]{:S(2)}) collective-permute-start(bf16[2,128,2048]{2,1,0:T(8,128)(2,1)} %get-tuple-element.244), channel_id=1, source_target_pairs={{0,16},{4,20},{8,24},{12,28},{16,0},{20,4},{24,8},{28,12},{1,17},{... | collective-permute-start | bytes 3145736 | tf_op jit(solution)/shard_map/ppermute | solution.py:577
  970.9 56.1 %collective-permute-start.18 = (bf16[512,2048]{1,0:T(8,128)(2,1)}, bf16[512,2048]{1,0:T(8,128)(2,1)}, u32[]{:S(2)}, u32[]{:S(2)}) collective-permute-start(bf16[512,2048]{1,0:T(8,128)(2,1)} %add_convert_fusion.8.refs_13_), channel_id=1, source_target_pairs={{0,1},{1,2},{2,3},{3,0},{4,5},{5,6},{6,7},{7,4},{8,9},{9,10},{10,1... | collective-permute-start | bytes 6291464 | tf_op jit(solution)/shard_map/ppermute | solution.py:518
  1019.0 45.9 %collective-permute-start.19 = (bf16[4,256,2048]{2,1,0:T(8,128)(2,1)}, bf16[4,256,2048]{2,1,0:T(8,128)(2,1)}, u32[]{:S(2)}, u32[]{:S(2)}) collective-permute-start(bf16[4,256,2048]{2,1,0:T(8,128)(2,1)} %maximum_maximum_fusion), channel_id=1, source_target_pairs={{0,4},{4,0},{8,12},{12,8},{16,20},{20,16},{24,28},{28,24},{1,5},{5... | collective-permute-start | bytes 12582920 | tf_op jit(solution)/shard_map/ppermute | solution.py:577
  1035.2 83.7 %collective-permute-start.36 = (bf16[128,2048]{1,0:T(8,128)(2,1)}, bf16[128,2048]{1,0:T(8,128)(2,1)}, u32[]{:S(2)}, u32[]{:S(2)}) collective-permute-start(bf16[128,2048]{1,0:T(8,128)(2,1)} %get-tuple-element.243), channel_id=1, source_target_pairs={{0,16},{4,20},{8,24},{12,28},{16,0},{20,4},{24,8},{28,12},{1,17},{... | collective-permute-start | bytes 1572872 | tf_op jit(solution)/shard_map/ppermute | solution.py:577
  1038.4 80.5 %collective-permute-start.38 = (bf16[128,2048]{1,0:T(8,128)(2,1)}, bf16[128,2048]{1,0:T(8,128)(2,1)}, u32[]{:S(2)}, u32[]{:S(2)}) collective-permute-start(bf16[128,2048]{1,0:T(8,128)(2,1)} %get-tuple-element.242), channel_id=1, source_target_pairs={{0,8},{4,12},{8,0},{12,4},{16,24},{20,28},{24,16},{28,20},{1,9},{5... | collective-permute-start | bytes 1572872 | tf_op jit(solution)/shard_map/ppermute | solution.py:577
  1047.5 143.8 %reduce-scatter.14.cloned.1.call-start = ((), (), s32[]{:S(2)}) async-start(), calls=%async_computation.14 | async-start | bytes 2801664 | tf_op jit(solution)/shard_map/reduce_scatter | solution.py:585
  1108.1 52.4 %collective-permute-start.29 = (bf16[256,1024]{1,0:T(8,128)(2,1)}, bf16[256,1024]{1,0:T(8,128)(2,1)}, u32[]{:S(2)}, u32[]{:S(2)}) collective-permute-start(bf16[256,1024]{1,0:T(8,128)(2,1)} %pad_maximum_fusion.9), channel_id=1, source_target_pairs={{0,3},{1,0},{2,1},{3,2},{4,7},{5,4},{6,5},{7,6},{8,11},{9,8},{10,9... | collective-permute-start | bytes 1572872 | tf_op jit(solution)/shard_map/ppermute | solution.py:557
  1123.9 33.6 %collective-permute-start.40 = (bf16[256,512]{1,0:T(8,128)(2,1)}, bf16[256,512]{1,0:T(8,128)(2,1)}, u32[]{:S(2)}, u32[]{:S(2)}) collective-permute-start(bf16[256,512]{1,0:T(8,128)(2,1)} %get-tuple-element.314), channel_id=1, source_target_pairs={{0,2},{1,3},{2,0},{3,1},{4,6},{5,7},{6,4},{7,5},{8,10},{9,11},{10,... | collective-permute-start | bytes 786440 | tf_op jit(solution)/shard_map/ppermute | solution.py:557
  1149.9 38.4 %collective-permute-start.34 = (bf16[256,1024]{1,0:T(8,128)(2,1)S(1)}, bf16[256,1024]{1,0:T(8,128)(2,1)S(1)}, u32[]{:S(2)}, u32[]{:S(2)}) collective-permute-start(bf16[256,1024]{1,0:T(8,128)(2,1)S(1)} %pad_maximum_fusion.10), channel_id=1, source_target_pairs={{0,2},{1,3},{2,0},{3,1},{4,6},{5,7},{6,4},{7,5},{8,10},{9,11},{10,... | collective-permute-start | bytes 1572872 | tf_op jit(solution)/shard_map/ppermute | solution.py:557
  1152.4 35.9 %collective-permute-start.35 = (bf16[256,1024]{1,0:T(8,128)(2,1)}, bf16[256,1024]{1,0:T(8,128)(2,1)S(1)}, u32[]{:S(2)}, u32[]{:S(2)}) collective-permute-start(bf16[256,1024]{1,0:T(8,128)(2,1)} %pad_maximum_fusion.11), channel_id=1, source_target_pairs={{0,1},{1,2},{2,3},{3,0},{4,5},{5,6},{6,7},{7,4},{8,9},{9,10},{10,1... | collective-permute-start | bytes 1572872 | tf_op jit(solution)/shard_map/ppermute | solution.py:557
  (207 other events, 3924.7 us)
Sparse Core Ops, SparseCore 0:
  35.4 31.2 all-gather.5
  86.7 123.0 all-gather.7
  212.3 92.0 all-gather.11
  306.7 57.1 all-gather.9
  365.6 92.0 all-gather.13
  559.3 72.7 reduce-scatter.5
  636.1 118.5 reduce-scatter.7
  838.1 119.8 reduce-scatter.9
  1047.6 50.6 reduce-scatter.11
  1138.7 41.5 reduce-scatter.13
